TPU v7x, 32 devices: a whole 2x2x4 slice. The times are simulated.
32 devices in a mesh: wide: 8 (over z, x), narrow: 4 (over y, core).
Axes of the slice: x: 2, y: 2, z: 4, core: 2. Of those that a mesh axis runs over, the one named last changes fastest.
Arguments:
- latents: float32 [128, 4096], P(('wide', 'narrow')), may hold values from -6 to 6
- noise: float32 [128, 4096], P(('wide', 'narrow')), may hold values from -6 to 6
- timesteps: int32 [128], P(('wide', 'narrow')), may hold values from 0 to 999
- labels: int32 [128], P(('wide', 'narrow')), may hold values from 0 to 999
- routes: int32 [32768, 2], P(('wide', 'narrow')), may hold values from 0 to 15, all different within a row; in each aligned block of 1024 rows (0 to 1023, 1024 to 2047, ...) at most 1024 rows name the same one
- mats: float32 [384, 6296], P(('wide', 'narrow')), may hold values from -4 to 4
- up_weights: float32 [18, 384, 1536], P(None, ('wide', 'narrow')), may hold values from -0.3125 to 0.3125
- down_weights: float32 [18, 1536, 384], P(None, ('wide', 'narrow')), may hold values from -0.15625 to 0.15625
- biases: float32 [5760], P(('wide', 'narrow')), may hold values from -1.8 to 1.8
- mats_row: float32 [10, 384], P(None, ('wide', 'narrow')), may hold values from 1.5258789e-06 to 1.2207031e-05
- mats_col: float32 [6296], replicated, may hold values from 1.5258789e-06 to 0.09
- up_row: float32 [18, 384], P(None, ('wide', 'narrow')), may hold values from 1.5258789e-06 to 1.2207031e-05
- up_col: float32 [18, 1536], replicated, may hold values from 1.5258789e-06 to 1.2207031e-05
- down_row: float32 [18, 1536], P(None, ('wide', 'narrow')), may hold values from 1.5258789e-06 to 1.2207031e-05
- down_col: float32 [18, 384], replicated, may hold values from 1.5258789e-06 to 1.2207031e-05
- bias_state: float32 [5760], P(('wide', 'narrow')), may hold values from 1.5258789e-06 to 1.2207031e-05
Outputs:
- loss: float32 [], replicated
- mats_grad: float32 [384, 6296], P(('wide', 'narrow'))
- mats_new: float32 [384, 6296], P(('wide', 'narrow'))
- mats_copy: bfloat16 [384, 6296], P(('wide', 'narrow'))
- mats_row_new: float32 [10, 384], P(None, ('wide', 'narrow'))
- mats_col_new: float32 [6296], replicated
- up_grad: float32 [18, 384, 1536], P(None, ('wide', 'narrow'))
- up_new: float32 [18, 384, 1536], P(None, ('wide', 'narrow'))
- up_copy: bfloat16 [18, 384, 1536], P(None, ('wide', 'narrow'))
- up_row_new: float32 [18, 384], P(None, ('wide', 'narrow'))
- up_col_new: float32 [18, 1536], replicated
- down_grad: float32 [18, 1536, 384], P(None, ('wide', 'narrow'))
- down_new: float32 [18, 1536, 384], P(None, ('wide', 'narrow'))
- down_copy: bfloat16 [18, 1536, 384], P(None, ('wide', 'narrow'))
- down_row_new: float32 [18, 1536], P(None, ('wide', 'narrow'))
- down_col_new: float32 [18, 384], replicated
- bias_grad: float32 [5760], P(('wide', 'narrow'))
- bias_new: float32 [5760], P(('wide', 'narrow'))
- bias_copy: bfloat16 [5760], P(('wide', 'narrow'))
- bias_state_new: float32 [5760], P(('wide', 'narrow'))
Inputs may be any that keep to these rules, and one draw needn't show every extreme that they name: `routes`: each patch names two different experts.
All inputs are finite; a program needn't handle non-finite values.
Results may differ from a plain program's by a relative error of at most 0.0055.
The roundings to bfloat16 on the way count: a program that leaves them out, or rounds other values in their place, can miss the bound.
Values may be sent and summed in bfloat16 or wider, within the bound.
A program may use at most 448 MiB of HBM per device.

v0:
```python
import math
from types import SimpleNamespace

import jax
import jax.numpy as jnp
from jax import lax
from jax.experimental import pallas as pl
from jax.experimental.pallas import tpu as pltpu
from jax.sharding import PartitionSpec as P

WIDE = "wide"
NARROW = "narrow"
AXES = (WIDE, NARROW)
MESH_ID = pl.DeviceIdType.MESH

D = 384
HEADS = 6
HD = 64
FF = 1536
EXPERTS = 16
SHARED = 2
PD = 16
GRID = 16
FREQ = 256
CLASSES = 1000
BLK = 256
WIDE_PIECES = 8
NARROW_PIECES = 4
PIECE = 48
ROWS = 12
LAT_ROWS = 16
LAT_COLS = 1536
PATCHES = 256


eps_norm = 1e-06
eps_fact = 1e-30
decay = 0.5
clip_level = 0.1
learn_rate = 0.5

SQRT_2_PI = math.sqrt(2.0 / math.pi)
VMEM_ROOM = 56 * 1024 * 1024
REDUCE_ROOM = 60 * 1024 * 1024


def column_widths():
    return [3 * D, D, 6 * D, D, 2 * D, EXPERTS, PD, PD, FREQ, CLASSES]


def bias_widths():
    return [3 * D, D, 6 * D, D, D, D, 2 * D]


def cut_pieces(source, widths, along):
    pieces = []
    start = 0
    for width in widths:
        pieces.append(lax.slice_in_dim(source, start, start + width, axis=along))
        start = start + width
    return pieces


def product(left, right):
    return jnp.dot(left, right, preferred_element_type=jnp.float32)


def contract(left, right, left_dim, right_dim):
    return lax.dot_general(
        left, right, (((left_dim,), (right_dim,)), ((), ())), preferred_element_type=jnp.float32
    )


def gelu_tanh(values):
    return jax.nn.gelu(values, approximate=True)


def slope_back(function, source, grad_out):
    return jax.vjp(function, source)[1](grad_out)[0]


def layer_norm(source):
    centred = source - jnp.mean(source, -1, keepdims=True)
    inv_std = lax.rsqrt(jnp.mean(centred * centred, -1, keepdims=True) + eps_norm)
    return (centred * inv_std, inv_std)


def norm_back(grad_norm, normed, inv_std):
    return inv_std * (
        grad_norm
        - jnp.mean(grad_norm, -1, keepdims=True)
        - normed * jnp.mean(grad_norm * normed, -1, keepdims=True)
    )


def linear_back(grad_out, inputs, weight):
    grad_low = grad_out.astype(jnp.bfloat16)
    return (
        contract(inputs, grad_low, 0, 0),
        contract(grad_low, weight, 1, 1),
        jnp.sum(grad_out, 0),
    )


def sincos(coords, width):
    omegas = 1.0 / 10000.0 ** (jnp.arange(width // 2, dtype=jnp.float32) / (width / 2.0))
    angles = coords[:, None] * omegas[None, :]
    return jnp.concatenate([jnp.sin(angles), jnp.cos(angles)], 1)


def positions():
    places = jnp.arange(PATCHES, dtype=jnp.int32)
    grid_row = (places // GRID).astype(jnp.float32)
    grid_col = (places % GRID).astype(jnp.float32)
    return jnp.concatenate([sincos(grid_row, D // 2), sincos(grid_col, D // 2)], 1)


def time_features(steps_f):
    half_width = FREQ // 2
    freq_rates = jnp.exp(
        -math.log(10000.0) * jnp.arange(half_width, dtype=jnp.float32) / half_width
    )
    angles = steps_f[:, None] * freq_rates[None, :]
    return jnp.concatenate([jnp.cos(angles), jnp.sin(angles)], 1)


def noise_level(steps_f):
    alpha_bar = jnp.cos((steps_f / 1000.0 + 0.008) / 1.008 * (math.pi / 2)) ** 2
    return (jnp.sqrt(alpha_bar), jnp.sqrt(1.0 - alpha_bar))


def pack_slots(routes):
    ids = jnp.arange(EXPERTS, dtype=jnp.int32)[:, None]
    named = [(routes[:, k][None, :] == ids) for k in range(2)]
    either = (named[0] | named[1]).astype(jnp.bfloat16)
    rows_here = routes.shape[0]
    place = jnp.arange(rows_here, dtype=jnp.int32)
    before = (place[:, None] < place[None, :]).astype(jnp.bfloat16)
    rank_in = product(either, before)
    counts = jnp.sum(either.astype(jnp.float32), 1).astype(jnp.int32)
    padded = (counts + 7) // 8 * 8
    starts = jnp.sum(jnp.where(ids > ids.T, padded[None, :], 0), 1)
    slots = rank_in.astype(jnp.int32) + starts[:, None]
    slot_of = jnp.stack([jnp.sum(jnp.where(member, slots, 0), 0) for member in named], 0)
    return (slot_of, jnp.stack([starts, counts], 0))


def gelu_slope(values):
    inner = SQRT_2_PI * (values + 0.044715 * values * values * values)
    bend = jnp.tanh(inner)
    return (
        0.5 * values * (1.0 + bend),
        0.5 * (1.0 + bend)
        + 0.5
        * values
        * (1.0 - bend * bend)
        * SQRT_2_PI
        * (1.0 + 3.0 * 0.044715 * values * values),
    )


def gelu_only(values):
    inner = SQRT_2_PI * (values + 0.044715 * values * values * values)
    return 0.5 * values * (1.0 + jnp.tanh(inner))


def slot_pick(slots_ref, base, rows):
    place = base + lax.broadcasted_iota(jnp.int32, (rows, slots_ref.shape[1]), 0)
    return ((slots_ref[0:1, :] == place) | (slots_ref[1:2, :] == place)).astype(jnp.bfloat16)


def forward_kernel(meta, slot_at, slots_ref, x_ref, up_ref, down_ref, routed_ref, shared_ref, y_ref):
    stack_id = pl.program_id(0)
    tokens = x_ref.shape[0]

    def expert(rows):
        total = None
        for cut in range(0, FF, D):
            pre_act = product(rows, up_ref[0, :, cut : cut + D])
            part = product(gelu_only(pre_act).astype(jnp.bfloat16), down_ref[0, cut : cut + D, :])
            total = part if total is None else total + part
        return total

    @pl.when(stack_id < EXPERTS)
    def _():
        owner = jnp.minimum(stack_id, EXPERTS - 1)
        start = meta[0, owner]

        def block(number, unused):
            base = pl.multiple_of(start + number * BLK, 8)
            rows = product(slot_pick(slots_ref, base, BLK), x_ref[...]).astype(jnp.bfloat16)
            y_ref[pl.ds(base, BLK), :] = expert(rows)
            return unused

        lax.fori_loop(0, (meta[1, owner] + BLK - 1) // BLK, block, 0)

    @pl.when(stack_id >= EXPERTS)
    def _():
        @pl.when(stack_id == EXPERTS)
        def _():
            shared_ref[...] = jnp.zeros_like(shared_ref)

        def block(number, unused):
            base = pl.multiple_of(number * BLK, BLK)
            shared_ref[pl.ds(base, BLK), :] += expert(x_ref[pl.ds(base, BLK), :])
            return unused

        lax.fori_loop(0, tokens // BLK, block, 0)

    @pl.when(stack_id == EXPERTS + SHARED - 1)
    def _():
        def group(number, unused):
            for step in range(8):
                token = number * 8 + step
                for k in range(2):
                    routed_ref[k, pl.ds(token, 1), :] = y_ref[pl.ds(slot_at[k, token], 1), :]
            return unused

        lax.fori_loop(0, tokens // 8, group, 0)


def slot_room(tokens):
    return tokens * 2 + EXPERTS * 8 + BLK


def whole_block(shape):
    return pl.BlockSpec(shape, lambda e, *unused: (0,) * len(shape))


def experts_forward(slot_of, meta, moe_in, up_full, down_full):
    tokens = moe_in.shape[0]
    return pl.pallas_call(
        forward_kernel,
        grid_spec=pltpu.PrefetchScalarGridSpec(
            num_scalar_prefetch=2,
            grid=(EXPERTS + SHARED,),
            in_specs=[
                whole_block((2, tokens)),
                whole_block((tokens, D)),
                pl.BlockSpec((1, D, FF), lambda e, *unused: (e, 0, 0)),
                pl.BlockSpec((1, FF, D), lambda e, *unused: (e, 0, 0)),
            ],
            out_specs=[whole_block((2, tokens, D)), whole_block((tokens, D))],
            scratch_shapes=[pltpu.VMEM((slot_room(tokens), D), jnp.float32)],
        ),
        out_shape=[
            jax.ShapeDtypeStruct((2, tokens, D), jnp.float32),
            jax.ShapeDtypeStruct((tokens, D), jnp.float32),
        ],
        compiler_params=pltpu.CompilerParams(vmem_limit_bytes=VMEM_ROOM),
        cost_estimate=pl.CostEstimate(
            flops=20_000_000_000, bytes_accessed=50_000_000, transcendentals=0
        ),
        name="experts_forward",
    )(meta, slot_of, slot_of, moe_in, up_full, down_full)


def backward_kernel(
    meta,
    slot_at,
    slots_ref,
    x_ref,
    pair_ref,
    both_ref,
    up_ref,
    down_ref,
    up_out,
    down_out,
    dx_ref,
    up_sum,
    down_sum,
    dx_slots,
):
    stack_id = pl.program_id(0)
    tokens = x_ref.shape[0]
    up_sum[...] = jnp.zeros_like(up_sum)
    down_sum[...] = jnp.zeros_like(down_sum)

    def expert(rows, grads):
        total = None
        for cut in range(0, FF, D):
            up_part = up_ref[0, :, cut : cut + D]
            activated, slope = gelu_slope(product(rows, up_part))
            grad_act = contract(grads, down_ref[0, cut : cut + D, :], 1, 1)
            grad_pre = (grad_act * slope).astype(jnp.bfloat16)
            down_sum[cut : cut + D, :] += contract(activated.astype(jnp.bfloat16), grads, 0, 0)
            up_sum[:, cut : cut + D] += contract(rows, grad_pre, 0, 0)
            part = contract(grad_pre, up_part, 1, 1)
            total = part if total is None else total + part
        return total

    @pl.when(stack_id < EXPERTS)
    def _():
        owner = jnp.minimum(stack_id, EXPERTS - 1)
        start = meta[0, owner]
        stop = start + meta[1, owner]

        def block(number, unused):
            base = pl.multiple_of(start + number * BLK, 8)
            rows = product(slot_pick(slots_ref, base, BLK), x_ref[...]).astype(jnp.bfloat16)
            place = base + lax.broadcasted_iota(jnp.int32, (BLK, tokens), 0)
            place = jnp.where(place < stop, place, -1)
            grads = None
            for k in range(2):
                part = product(
                    (slots_ref[k : k + 1, :] == place).astype(jnp.bfloat16), pair_ref[k]
                )
                grads = part if grads is None else grads + part
            dx_slots[pl.ds(base, BLK), :] = expert(rows, grads.astype(jnp.bfloat16))
            return unused

        lax.fori_loop(0, (meta[1, owner] + BLK - 1) // BLK, block, 0)

    @pl.when(stack_id >= EXPERTS)
    def _():
        @pl.when(stack_id == EXPERTS)
        def _():
            dx_ref[...] = jnp.zeros_like(dx_ref)

        def block(number, unused):
            base = pl.multiple_of(number * BLK, BLK)
            dx_ref[pl.ds(base, BLK), :] += expert(
                x_ref[pl.ds(base, BLK), :], both_ref[pl.ds(base, BLK), :]
            )
            return unused

        lax.fori_loop(0, tokens // BLK, block, 0)

    for n in range(NARROW_PIECES):
        up_out[0, :, n] = (
            up_sum[:, n * D : (n + 1) * D]
            .astype(jnp.bfloat16)
            .reshape(WIDE_PIECES, PIECE, D)
        )
    down_out[0] = down_sum[...].astype(jnp.bfloat16).reshape(WIDE_PIECES, NARROW_PIECES, PIECE, D)

    @pl.when(stack_id == EXPERTS + SHARED - 1)
    def _():
        def group(number, unused):
            for step in range(8):
                token = number * 8 + step
                dx_ref[pl.ds(token, 1), :] += (
                    dx_slots[pl.ds(slot_at[0, token], 1), :]
                    + dx_slots[pl.ds(slot_at[1, token], 1), :]
                )
            return unused

        lax.fori_loop(0, tokens // 8, group, 0)


def experts_backward(slot_of, meta, moe_in, grad_pair, grad_both, up_full, down_full):
    tokens = moe_in.shape[0]
    slabs = (EXPERTS + SHARED, WIDE_PIECES, NARROW_PIECES, PIECE, D)
    slab_spec = pl.BlockSpec((1,) + slabs[1:], lambda e, *unused: (e, 0, 0, 0, 0))
    return pl.pallas_call(
        backward_kernel,
        grid_spec=pltpu.PrefetchScalarGridSpec(
            num_scalar_prefetch=2,
            grid=(EXPERTS + SHARED,),
            in_specs=[
                whole_block((2, tokens)),
                whole_block((tokens, D)),
                whole_block((2, tokens, D)),
                whole_block((tokens, D)),
                pl.BlockSpec((1, D, FF), lambda e, *unused: (e, 0, 0)),
                pl.BlockSpec((1, FF, D), lambda e, *unused: (e, 0, 0)),
            ],
            out_specs=[slab_spec, slab_spec, whole_block((tokens, D))],
            scratch_shapes=[
                pltpu.VMEM((D, FF), jnp.float32),
                pltpu.VMEM((FF, D), jnp.float32),
                pltpu.VMEM((slot_room(tokens), D), jnp.float32),
            ],
        ),
        out_shape=[
            jax.ShapeDtypeStruct(slabs, jnp.bfloat16),
            jax.ShapeDtypeStruct(slabs, jnp.bfloat16),
            jax.ShapeDtypeStruct((tokens, D), jnp.float32),
        ],
        compiler_params=pltpu.CompilerParams(vmem_limit_bytes=VMEM_ROOM),
        cost_estimate=pl.CostEstimate(
            flops=45_000_000_000, bytes_accessed=90_000_000, transcendentals=0
        ),
        name="experts_backward",
    )(meta, slot_of, slot_of, moe_in, grad_pair, grad_both, up_full, down_full)


def reduce_kernel(
    down_ref,
    thin_ref,
    up_ref,
    mats_ref,
    lat_in,
    out_ref,
    rows_ref,
    lat_ref,
    own,
    got_core,
    out_one,
    keep_one,
    got_one,
    out_two,
    keep_two,
    got_two,
    keep_z,
    out_rise,
    out_fall,
    got_rise,
    got_fall,
    row_parts,
    own_sem,
    core_send,
    core_recv,
    one_send,
    one_recv,
    two_send,
    two_recv,
    rise_send,
    rise_recv,
    fall_send,
    fall_recv,
    row_send,
    row_recv,
    lat_own,
    lat_send,
    lat_recv,
):
    counts = [member.shape[0] for member in (down_ref, thin_ref, up_ref, mats_ref)]
    slabs = sum(counts)
    direct = counts[0] + counts[1]
    ahead = 2
    wide, narrow = lax.axis_index(WIDE), lax.axis_index(NARROW)
    z, x = wide // 2, wide % 2
    y, c = narrow // 2, narrow % 2
    x_one, y_one = x + (1 - c) * (1 - 2 * x), y + c * (1 - 2 * y)
    x_two, y_two = x + c * (1 - 2 * x), y + (1 - c) * (1 - 2 * y)
    to_core = (wide, y * 2 + 1 - c)
    to_one = (z * 2 + x_one, y_one * 2 + c)
    to_two = (z * 2 + x_two, y_two * 2 + c)
    to_rise = (jnp.minimum(z + 1, 3) * 2 + x, narrow)
    to_fall = (jnp.maximum(z - 1, 0) * 2 + x, narrow)
    first_mine = x * (1 - c) + y * c
    second_mine = y * (1 - c) + x * c
    first_step, second_step = 2 - c, 1 + c

    mates = [
        (wide, (y + (k // 2) * (1 - 2 * y)) * 2 + c + (k % 2) * (1 - 2 * c)) for k in range(1, 4)
    ]
    levels = [(((z + k) % 4) * 2 + x, narrow) for k in range(1, 4)]
    to_x = (z * 2 + 1 - x, narrow)
    barrier = pltpu.get_barrier_semaphore()
    for target in mates + levels + [to_x]:
        pl.semaphore_signal(barrier, inc=1, device_id=target, device_id_type=MESH_ID)
    pl.semaphore_wait(barrier, 7)

    def remote(source, target, send, recv, device):
        return pltpu.make_async_remote_copy(
            src_ref=source,
            dst_ref=target,
            send_sem=send,
            recv_sem=recv,
            device_id=device,
            device_id_type=MESH_ID,
        )

    def core_copy(source, s):
        return remote(
            source.at[:, 1 - c], got_core.at[s], core_send.at[s % 4], core_recv.at[s], to_core
        )

    def own_copy(source, s):
        return pltpu.make_async_copy(source.at[:, c], own.at[s % 3], own_sem.at[s % 3])

    def one_copy(s):
        return remote(
            out_one.at[s % 2], got_one.at[s], one_send.at[s % 2], one_recv.at[s], to_one
        )

    def two_copy(s):
        return remote(
            out_two.at[s % 2], got_two.at[s], two_send.at[s % 2], two_recv.at[s], to_two
        )

    def rise_copy(s):
        return remote(
            out_rise.at[s % 2], got_rise.at[s], rise_send.at[s % 2], rise_recv.at[s], to_rise
        )

    def fall_copy(s):
        return remote(
            out_fall.at[s % 2], got_fall.at[s], fall_send.at[s % 2], fall_recv.at[s], to_fall
        )

    def row_copy(s, k):
        mate = mates[k - 1]
        return remote(
            row_parts.at[s % 2, mate[1]],
            rows_ref.at[s - direct, narrow],
            row_send.at[s % 2, k - 1],
            row_recv.at[s - direct, k - 1],
            mate,
        )

    def lat_level(k):
        spot = lat_ref.at[z, x, y, c]
        return remote(spot, spot, lat_send.at[k - 1], lat_recv.at[k - 1], levels[k - 1])

    def lat_x():
        spot = lat_ref.at[:, x, y, c]
        return remote(spot, spot, lat_send.at[3], lat_recv.at[3], to_x)

    def lat_y():
        spot = lat_ref.at[:, :, y, c]
        return remote(spot, spot, lat_send.at[4], lat_recv.at[4], mates[1])

    def lat_core():
        spot = lat_ref.at[:, :, :, c]
        return remote(spot, spot, lat_send.at[5], lat_recv.at[5], mates[0])

    own_lat = pltpu.make_async_copy(lat_in, lat_ref.at[z, x, y, c], lat_own.at[0])
    own_lat.start()
    own_lat.wait()
    for k in range(1, 4):
        lat_level(k).start()

    def begin(source, s):
        @pl.when(s >= 4)
        def _():
            core_copy(source, s).wait_send()

        core_copy(source, s).start()
        own_copy(source, s).start()

    def stage_core(s):
        own_copy(down_ref.at[0], s).wait()
        core_copy(down_ref.at[0], s).wait_recv()

        @pl.when(s >= 2)
        def _():
            one_copy(s).wait_send()

        for level in range(4):
            for other in range(2):
                place = level * 2 + other
                base = level * 4 + other * second_step
                send_at = base + (1 - first_mine) * first_step
                keep_at = base + first_mine * first_step
                out_one[s % 2, place] = (
                    own[s % 3, send_at].astype(jnp.float32)
                    + got_core[s, send_at].astype(jnp.float32)
                ).astype(jnp.bfloat16)
                keep_one[s % 2, place] = own[s % 3, keep_at].astype(jnp.float32) + got_core[
                    s, keep_at
                ].astype(jnp.float32)
        one_copy(s).start()

    def stage_one(s):
        one_copy(s).wait_recv()

        @pl.when(s >= 2)
        def _():
            two_copy(s).wait_send()

        for level in range(4):
            send_at = level * 2 + 1 - second_mine
            keep_at = level * 2 + second_mine
            out_two[s % 2, level] = (
                keep_one[s % 2, send_at] + got_one[s, send_at].astype(jnp.float32)
            ).astype(jnp.bfloat16)
            keep_two[s % 2, level] = keep_one[s % 2, keep_at] + got_one[s, keep_at].astype(
                jnp.float32
            )
        two_copy(s).start()

    def stage_two(s):
        two_copy(s).wait_recv()
        for level in range(4):
            keep_z[s % 4, level] = keep_two[s % 2, level] + got_two[s, level].astype(jnp.float32)
        stage_z(s, 0)

    def stage_z(s, hop):
        def pass_on(copy, out, got, shift):
            @pl.when(s >= 2)
            def _():
                copy(s).wait_send()

            if hop > 0:
                copy(s).wait_recv()
            for level in range(3):
                value = keep_z[s % 4, level + shift]
                if hop > 0:
                    value = value + got[s, level].astype(jnp.float32)
                out[s % 2, level] = value.astype(jnp.bfloat16)
            copy(s).start()

        @pl.when(z == hop)
        def _():
            pass_on(rise_copy, out_rise, got_rise, 1)

        @pl.when(z == 3 - hop)
        def _():
            pass_on(fall_copy, out_fall, got_fall, 0)

    def finish(s):
        @pl.when(z == 3)
        def _():
            rise_copy(s).wait_recv()

        @pl.when(z == 0)
        def _():
            fall_copy(s).wait_recv()

        total = keep_z[s % 4, z]
        rise = got_rise[s, jnp.maximum(z - 1, 0)].astype(jnp.float32)
        fall = got_fall[s, jnp.minimum(z, 2)].astype(jnp.float32)
        total = total + jnp.where(z > 0, rise, 0.0) + jnp.where(z < 3, fall, 0.0)

        @pl.when(s < direct)
        def _():
            out_ref[jnp.minimum(s, direct - 1)] = total

        @pl.when(s >= direct)
        def _():
            @pl.when(s >= direct + 2)
            def _():
                for k in range(1, 4):
                    row_copy(s, k).wait_send()

            for n in range(NARROW_PIECES):
                row_parts[s % 2, n] = total[n * ROWS : (n + 1) * ROWS]
            rows_ref[s - direct, narrow] = row_parts[s % 2, narrow]
            for k in range(1, 4):
                row_copy(s, k).start()

    def rows_in(s):
        @pl.when(s >= direct)
        def _():
            for k in range(1, 4):
                row_copy(s, k).wait_recv()

    def inside(s):
        return (s >= 0) & (s < slabs)

    def tick(t, unused):
        first = 0
        for source, count in zip((down_ref, thin_ref, up_ref, mats_ref), counts):

            @pl.when((t >= first) & (t < first + count))
            def _():
                begin(source.at[jnp.clip(t - first, 0, count - 1)], t)

            first += count

        @pl.when(t == 4)
        def _():
            for k in range(1, 4):
                lat_level(k).wait_recv()
            lat_x().start()

        @pl.when(t == 6)
        def _():
            lat_x().wait_recv()
            lat_y().start()

        @pl.when(t == 8)
        def _():
            lat_y().wait_recv()
            lat_core().start()

        for lag, stage in enumerate(
            (
                stage_core,
                stage_one,
                stage_two,
                lambda s: stage_z(s, 1),
                lambda s: stage_z(s, 2),
                finish,
                rows_in,
            )
        ):
            s = t - ahead - lag

            @pl.when(inside(s))
            def _():
                stage(s)

        return unused

    lax.fori_loop(0, slabs + ahead + 6, tick, 0)

    for back in range(4):
        core_copy(down_ref.at[0], slabs - 1 - back).wait_send()
    for back in range(2):
        one_copy(slabs - 1 - back).wait_send()
        two_copy(slabs - 1 - back).wait_send()
        for k in range(1, 4):
            row_copy(slabs - 1 - back, k).wait_send()

        @pl.when(z < 3)
        def _():
            rise_copy(slabs - 1 - back).wait_send()

        @pl.when(z > 0)
        def _():
            fall_copy(slabs - 1 - back).wait_send()

    for k in range(1, 4):
        lat_level(k).wait_send()
    lat_x().wait_send()
    lat_y().wait_send()
    lat_core().wait()


def reduce_slabs(down_slabs, up_slabs, mats_slabs, thin, lat):
    members = (down_slabs, thin, up_slabs, mats_slabs)
    slabs = sum(member.shape[0] for member in members)
    direct = down_slabs.shape[0] + thin.shape[0]
    turned = slabs - direct
    low, full = jnp.bfloat16, jnp.float32
    sources = [
        member.reshape(member.shape[0], WIDE_PIECES * NARROW_PIECES // 2, 2, PIECE, D)
        for member in members
    ]
    dma = pltpu.SemaphoreType.DMA
    vmem = pl.BlockSpec(memory_space=pltpu.VMEM)
    sums, rows, lats = pl.pallas_call(
        reduce_kernel,
        out_shape=[
            jax.ShapeDtypeStruct((direct, PIECE, D), full),
            jax.ShapeDtypeStruct((turned, NARROW_PIECES, ROWS, D), full),
            jax.ShapeDtypeStruct((4, 2, 2, 2, LAT_ROWS, LAT_COLS), low),
        ],
        in_specs=[pl.BlockSpec(memory_space=pl.ANY)] * 5,
        out_specs=[vmem, vmem, pl.BlockSpec(memory_space=pl.ANY)],
        scratch_shapes=[
            pltpu.VMEM((3, 16, PIECE, D), low),
            pltpu.VMEM((slabs, 16, PIECE, D), low),
            pltpu.VMEM((2, 8, PIECE, D), low),
            pltpu.VMEM((2, 8, PIECE, D), full),
            pltpu.VMEM((slabs, 8, PIECE, D), low),
            pltpu.VMEM((2, 4, PIECE, D), low),
            pltpu.VMEM((2, 4, PIECE, D), full),
            pltpu.VMEM((slabs, 4, PIECE, D), low),
            pltpu.VMEM((4, 4, PIECE, D), full),
            pltpu.VMEM((2, 3, PIECE, D), low),
            pltpu.VMEM((2, 3, PIECE, D), low),
            pltpu.VMEM((slabs, 3, PIECE, D), low),
            pltpu.VMEM((slabs, 3, PIECE, D), low),
            pltpu.VMEM((2, NARROW_PIECES, ROWS, D), full),
            dma((3,)),
            dma((4,)),
            dma((slabs,)),
            dma((2,)),
            dma((slabs,)),
            dma((2,)),
            dma((slabs,)),
            dma((2,)),
            dma((slabs,)),
            dma((2,)),
            dma((slabs,)),
            dma((2, 3)),
            dma((turned, 3)),
            dma((1,)),
            dma((6,)),
            dma((6,)),
        ],
        compiler_params=pltpu.CompilerParams(
            collective_id=0, has_side_effects=True, vmem_limit_bytes=REDUCE_ROOM
        ),
        name="reduce_slabs",
    )(*sources, lat)
    return sums, rows, lats.reshape(-1, LAT_COLS)


def thin_slab(thin, grad_bias):
    owners = WIDE_PIECES * NARROW_PIECES
    top = thin.reshape(owners, ROWS, -1)
    top = jnp.pad(top, ((0, 0), (0, 0), (0, D - top.shape[2])))
    line = grad_bias.reshape(owners, 1, -1)
    line = jnp.pad(line, ((0, 0), (0, PIECE - ROWS - 1), (0, D - line.shape[2])))
    both = jnp.concatenate([top, line], 1).astype(jnp.bfloat16)
    return both.reshape(1, WIDE_PIECES, NARROW_PIECES, PIECE, D)


def lat_block(lows, grad_cond, labels):
    high = lax.reduce_precision(grad_cond, 8, 7)
    middle = lax.reduce_precision(grad_cond - high, 8, 7)
    label_parts = jnp.stack([labels // 32, labels % 32], 1).astype(jnp.bfloat16)
    whole = jnp.concatenate(
        [
            lows,
            middle.astype(jnp.bfloat16),
            (grad_cond - high - middle).astype(jnp.bfloat16),
            label_parts,
        ],
        1,
    )
    room = LAT_ROWS * LAT_COLS // labels.shape[0] - whole.shape[1]
    return jnp.pad(whole, ((0, 0), (0, room))).reshape(LAT_ROWS, LAT_COLS)


def plain_grads(
    down_slabs, up_slabs, mats_slabs, thin, grad_bias, lows, grad_cond, labels, row_count
):
    def scattered(member, up_form):
        order = (0, 1, 3, 2, 4) if up_form else (0, 1, 2, 3, 4)
        member = member.astype(jnp.float32).transpose(order)
        member = member.reshape(member.shape[0], -1, FF if up_form else D)
        return lax.psum_scatter(member, AXES, scatter_dimension=1, tiled=True)

    proj_grad = scattered(mats_slabs, True)
    row_start = lax.axis_index(AXES) * row_count
    thin_grad = lax.psum_scatter(thin, AXES, scatter_dimension=0, tiled=True)
    bias_grad = lax.psum_scatter(grad_bias, AXES, scatter_dimension=0, tiled=True)
    grad_mod, grad_time2, grad_fin, grad_time1, grad_table = latent_grads(
        lows, grad_cond, labels, row_start, row_count
    )
    mats_grad = jnp.concatenate(
        [proj_grad[0], grad_mod, grad_time2, grad_fin, thin_grad, grad_time1, grad_table], 1
    )
    return (mats_grad, scattered(up_slabs, True), scattered(down_slabs, False), bias_grad)


def update_kernel(
    sums_ref,
    rows_ref,
    lat_ref,
    loss_ref,
    mats_ref,
    up_ref,
    down_ref,
    bias_ref,
    mats_row,
    mats_col,
    up_row,
    up_col,
    down_row,
    down_col,
    bias_state,
    loss_out,
    mats_grad,
    mats_new,
    mats_copy,
    mats_row_new,
    mats_col_new,
    up_grad,
    up_new,
    up_copy,
    up_row_new,
    up_col_new,
    down_grad,
    down_new,
    down_copy,
    down_row_new,
    down_col_new,
    bias_grad,
    bias_new,
    bias_copy,
    bias_state_new,
    part,
    got_plane,
    mine,
    got_level,
    column,
    result,
    squares_plane,
    squares_level,
    sems,
):
    full, low = jnp.float32, jnp.bfloat16
    wide, narrow = lax.axis_index(WIDE), lax.axis_index(NARROW)
    z, spot = wide // 2, (wide % 2) * 4 + narrow

    def plane_device(k):
        there = (spot + k) % 8
        return (z * 2 + there // 4, there % 4)

    def level_device(k):
        return (((z + k) % 4) * 2 + wide % 2, narrow)

    barrier = pltpu.get_barrier_semaphore()
    for k in range(1, 8):
        pl.semaphore_signal(barrier, inc=1, device_id=plane_device(k), device_id_type=MESH_ID)
    for k in range(1, 4):
        pl.semaphore_signal(barrier, inc=1, device_id=level_device(k), device_id_type=MESH_ID)
    pl.semaphore_wait(barrier, 10)

    def remote(source, target, phase, k, device):
        return pltpu.make_async_remote_copy(
            src_ref=source,
            dst_ref=target,
            send_sem=sems.at[0, phase, k],
            recv_sem=sems.at[1, phase, k],
            device_id=device,
            device_id_type=MESH_ID,
        )

    def exchange(copies):
        for copy in copies:
            copy.start()
        for copy in copies:
            copy.wait()

    lane = lax.broadcasted_iota(jnp.int32, (1, 128), 1)

    def spread(value, place):
        return jnp.where(lane == place, value, 0.0)

    def pick(row, place):
        return jnp.sum(jnp.where(lane == place, row, 0.0), 1, keepdims=True)

    def total(values):
        return jnp.sum(jnp.sum(values, 1, keepdims=True), 0, keepdims=True)

    count = lat_ref.shape[0] // 4
    order = lax.broadcasted_iota(jnp.int32, (count, count * 4), 0) * 4
    place = lax.broadcasted_iota(jnp.int32, (count, count * 4), 1)
    quarters = [
        product((place == order + k).astype(low), lat_ref[...]).astype(low) for k in range(4)
    ]
    owner_row = (wide * NARROW_PIECES + narrow) * ROWS
    chosen = (
        lax.broadcasted_iota(jnp.int32, (16, D), 1)
        == lax.broadcasted_iota(jnp.int32, (16, D), 0) + owner_row
    ).astype(low)

    def rows_of(member):
        return contract(chosen, member, 1, 1).astype(low)

    act_rows = rows_of(quarters[0][:, :D])
    hid_rows = rows_of(quarters[0][:, D : 2 * D])
    high = quarters[2][:, 2 * D : 3 * D]
    for j in range(NARROW_PIECES):
        mats_grad[:, j * D : (j + 1) * D] = rows_ref[EXPERTS + SHARED, j]
    mats_grad[:, 4 * D : 6 * D] = product(act_rows, quarters[0][:, 2 * D :])[:ROWS]
    mats_grad[:, 6 * D : 10 * D] = product(act_rows, quarters[1])[:ROWS]
    mats_grad[:, 10 * D : 11 * D] = product(hid_rows, high)[:ROWS]
    mats_grad[:, 11 * D : 13 * D] = product(act_rows, quarters[2][:, : 2 * D])[:ROWS]
    time_rows = rows_of(quarters[2][:, 3 * D :])
    time_one = product(time_rows, quarters[3][:, :FREQ])
    label_at = FREQ + 2 * D
    labels = quarters[3][:, label_at : label_at + 128].astype(full)
    label = labels[:, 0:1] * 32.0 + labels[:, 1:2]
    label_hot = (
        lax.broadcasted_iota(jnp.int32, (count, 1024), 1).astype(full) == label
    ).astype(low)
    table = (
        product(rows_of(high), label_hot)
        + product(rows_of(quarters[3][:, FREQ : FREQ + D]), label_hot)
        + product(rows_of(quarters[3][:, FREQ + D : FREQ + 2 * D]), label_hot)
    )
    start_last = 13 * D
    width_last = mats_grad.shape[1] - start_last
    room = 11 * 128
    thin = sums_ref[EXPERTS + SHARED][:16, :128]
    thin = jnp.where(
        (lax.broadcasted_iota(jnp.int32, (16, 128), 1) < EXPERTS + 2 * PD)
        & (lax.broadcasted_iota(jnp.int32, (16, 128), 0) < ROWS),
        thin,
        0.0,
    )

    def padded(member):
        return jnp.concatenate(
            [member, jnp.zeros((16, room - member.shape[1]), full)], 1
        )

    last = (
        padded(thin)
        + pltpu.roll(padded(time_one), EXPERTS + 2 * PD, 1)
        + pltpu.roll(padded(table), EXPERTS + 2 * PD + FREQ, 1)
    )
    mats_grad[:, start_last:] = last[:ROWS, :width_last]
    bias_grad[...] = sums_ref[EXPERTS + SHARED][ROWS : ROWS + 1, : bias_grad.shape[1]]

    part[...] = jnp.zeros_like(part)
    widths = column_widths()
    mats_at, line_at = 360, 416
    total_cols = mats_grad.shape[1]
    cuts = [(at, min(at + 128, total_cols)) for at in range(0, total_cols, 128)]
    for number, (begin, end) in enumerate(cuts):
        values = mats_grad[:, begin:end]
        part[mats_at + number : mats_at + number + 1, : end - begin] = jnp.sum(
            values * values + eps_fact, 0, keepdims=True
        )
    bounds = [sum(widths[:k]) for k in range(len(widths) + 1)]
    last_lane = lax.broadcasted_iota(jnp.int32, (ROWS, width_last), 1) + start_last
    last_sq = mats_grad[:, start_last:] * mats_grad[:, start_last:] + eps_fact
    line = spread(loss_ref[...], 46)
    for k in range(len(widths)):
        if k < 5:
            values = mats_grad[:, bounds[k] : bounds[k + 1]]
            sq = values * values + eps_fact
        else:
            sq = jnp.where((last_lane >= bounds[k]) & (last_lane < bounds[k + 1]), last_sq, 0.0)
        new = decay * mats_row[:, k : k + 1] + (1.0 - decay) * (
            jnp.sum(sq, 1, keepdims=True) / widths[k]
        )
        mats_row_new[:, k : k + 1] = new
        line = line + spread(jnp.sum(new, 0, keepdims=True), k)

    def begin_up(e, line):
        for j in range(NARROW_PIECES):
            up_grad[e, :, j * D : (j + 1) * D] = rows_ref[e, j]
        values = up_grad[e]
        sq = values * values + eps_fact
        new = decay * up_row[e] + (1.0 - decay) * (jnp.sum(sq, 1, keepdims=True) / FF)
        up_row_new[e] = new
        cols = jnp.sum(sq, 0, keepdims=True)
        for k in range(FF // 128):
            part[pl.ds(24 * k + e, 1), :] = cols[:, 128 * k : 128 * (k + 1)]
        return line + spread(jnp.sum(new, 0, keepdims=True), 10 + e)

    def begin_down(e, line):
        values = sums_ref[e]
        down_grad[e] = values
        sq = values * values + eps_fact
        new = decay * down_row[e] + (1.0 - decay) * (jnp.sum(sq, 1, keepdims=True) / D)
        down_row_new[e] = new
        cols = jnp.sum(sq, 0, keepdims=True)
        for k in range(D // 128):
            part[pl.ds(24 * (12 + k) + e, 1), :] = cols[:, 128 * k : 128 * (k + 1)]
        return line + spread(jnp.sum(new, 0, keepdims=True), 28 + e)

    line = lax.fori_loop(0, EXPERTS + SHARED, begin_up, line)
    line = lax.fori_loop(0, EXPERTS + SHARED, begin_down, line)
    part[line_at : line_at + 1, :] = line

    exchange(
        [
            remote(
                part.at[pl.ds(((spot + k) % 8) * 64, 64)], got_plane.at[k], 0, k, plane_device(k)
            )
            for k in range(1, 8)
        ]
    )
    here = part[pl.ds(pl.multiple_of(spot * 64, 64), 64), :]
    for k in range(1, 8):
        here = here + got_plane[k]
    mine[...] = here.reshape(4, 16, 128)
    exchange(
        [
            remote(mine.at[(z + k) % 4], got_level.at[k], 1, k, level_device(k))
            for k in range(1, 4)
        ]
    )
    column[z] = mine[z] + got_level[1] + got_level[2] + got_level[3]
    exchange(
        [remote(column.at[z], column.at[z], 2, k, level_device(k)) for k in range(1, 4)]
    )
    result[spot] = column[...]
    exchange(
        [remote(result.at[spot], result.at[spot], 3, k, plane_device(k)) for k in range(1, 8)]
    )

    def sums_row(row, width=128):
        if isinstance(row, int):
            return result[row // 64, (row // 16) % 4, row % 16 : row % 16 + 1, :width]
        return result[row // 64, (row // 16) % 4, pl.ds(row % 16, 1), :width]

    line = sums_row(line_at)
    loss_out[...] = pick(line, 46)
    for number, (begin, end) in enumerate(cuts):
        mats_col_new[:, begin:end] = decay * mats_col[:, begin:end] + (1.0 - decay) * (
            sums_row(mats_at + number, end - begin) / D
        )

    squares = jnp.zeros((1, 128), full)
    for k in range(5):
        begin, end = bounds[k], bounds[k + 1]
        step = mats_grad[:, begin:end] * lax.rsqrt(
            mats_row_new[:, k : k + 1] * mats_col_new[:, begin:end] / (pick(line, k) / D)
        )
        mats_new[:, begin:end] = step
        squares = squares + spread(total(step * step), k)

    def by_piece(values):
        chosen_value = values[0]
        for k in range(6, len(widths)):
            chosen_value = jnp.where(last_lane >= bounds[k], values[k - 5], chosen_value)
        return chosen_value

    row_last = by_piece([mats_row_new[:, k : k + 1] for k in range(5, len(widths))])
    mean_last = by_piece([pick(line, k) / D for k in range(5, len(widths))])
    step_last = mats_grad[:, start_last:] * lax.rsqrt(
        row_last * mats_col_new[:, start_last:] / mean_last
    )
    mats_new[:, start_last:] = step_last
    for k in range(5, len(widths)):
        inside = (last_lane >= bounds[k]) & (last_lane < bounds[k + 1])
        squares = squares + spread(total(jnp.where(inside, step_last * step_last, 0.0)), k)

    def step_up(e, squares):
        cols = jnp.concatenate([sums_row(24 * k + e) for k in range(FF // 128)], 1)
        new = decay * up_col[pl.ds(e, 1), :] + (1.0 - decay) * (cols / D)
        up_col_new[pl.ds(e, 1), :] = new
        step = up_grad[e] * lax.rsqrt(up_row_new[e] * new / (pick(line, 10 + e) / D))
        up_new[e] = step
        return squares + spread(total(step * step), 10 + e)

    def step_down(e, squares):
        cols = jnp.concatenate([sums_row(24 * (12 + k) + e) for k in range(D // 128)], 1)
        new = decay * down_col[pl.ds(e, 1), :] + (1.0 - decay) * (cols / FF)
        down_col_new[pl.ds(e, 1), :] = new
        step = down_grad[e] * lax.rsqrt(down_row_new[e] * new / (pick(line, 28 + e) / FF))
        down_new[e] = step
        return squares + spread(total(step * step), 28 + e)

    squares = lax.fori_loop(0, EXPERTS + SHARED, step_up, squares)
    squares = lax.fori_loop(0, EXPERTS + SHARED, step_down, squares)
    state = decay * bias_state[...] + (1.0 - decay) * (
        bias_grad[...] * bias_grad[...] + eps_fact
    )
    bias_state_new[...] = state
    bias_step = bias_grad[...] * lax.rsqrt(state)
    squares = squares + spread(total(bias_step * bias_step), 46)
    squares_plane[spot] = jnp.broadcast_to(squares, (8, 128))
    exchange(
        [
            remote(squares_plane.at[spot], squares_plane.at[spot], 4, k, plane_device(k))
            for k in range(1, 8)
        ]
    )
    squares_level[z] = jnp.sum(squares_plane[...], 0)
    exchange(
        [
            remote(squares_level.at[z], squares_level.at[z], 5, k, level_device(k))
            for k in range(1, 4)
        ]
    )
    squares = jnp.sum(squares_level[...], 0)[0:1]

    def clipped(place, entries):
        rms = jnp.sqrt(pick(squares, place) / entries)
        return jnp.maximum(1.0, rms / clip_level)

    def settle(new_ref, copy_ref, index, master, step, limit):
        value = master - learn_rate * (step / limit)
        new_ref[index] = value
        copy_ref[index] = value.astype(low)

    for k in range(5):
        index = (slice(None), slice(bounds[k], bounds[k + 1]))
        settle(
            mats_new, mats_copy, index, mats_ref[index], mats_new[index], clipped(k, D * widths[k])
        )
    limit = by_piece([clipped(k, D * widths[k]) for k in range(5, len(widths))])
    index = (slice(None), slice(start_last, None))
    settle(mats_new, mats_copy, index, mats_ref[index], mats_new[index], limit)

    def settle_pair(e, unused):
        settle(up_new, up_copy, e, up_ref[e], up_new[e], clipped(10 + e, D * FF))
        settle(down_new, down_copy, e, down_ref[e], down_new[e], clipped(28 + e, D * FF))
        return unused

    lax.fori_loop(0, EXPERTS + SHARED, settle_pair, 0)
    index = (slice(None), slice(None))
    settle(bias_new, bias_copy, index, bias_ref[...], bias_step, clipped(46, 15 * D))


def update_kernel_call(sums, rows, lat, masters, factors, loss_part):
    mats, up_weights, down_weights, biases = masters
    mats_row, mats_col, up_row, up_col, down_row, down_col, bias_state = factors
    full, low = jnp.float32, jnp.bfloat16
    args = (
        sums,
        rows,
        lat,
        loss_part.reshape(1, 1),
        mats,
        up_weights,
        down_weights,
        biases.reshape(1, -1),
        mats_row.T,
        mats_col.reshape(1, -1),
        up_row[:, :, None],
        up_col,
        down_row[:, :, None],
        down_col,
        bias_state.reshape(1, -1),
    )

    def like(member, kind):
        return jax.ShapeDtypeStruct(member.shape, kind)

    stacks = []
    for at in (4, 5, 6):
        stacks.append([like(args[at], full), like(args[at], full), like(args[at], low)])
        stacks[-1] += [like(args[2 * at], full), like(args[2 * at + 1], full)]
    lines = [like(args[7], full), like(args[7], full), like(args[7], low), like(args[7], full)]
    vmem = pl.BlockSpec(memory_space=pltpu.VMEM)
    dma = pltpu.SemaphoreType.DMA
    outs = pl.pallas_call(
        update_kernel,
        out_shape=[jax.ShapeDtypeStruct((1, 1), full)] + stacks[0] + stacks[1] + stacks[2] + lines,
        in_specs=[vmem] * len(args),
        out_specs=[vmem] * 20,
        scratch_shapes=[
            pltpu.VMEM((512, 128), full),
            pltpu.VMEM((8, 64, 128), full),
            pltpu.VMEM((4, 16, 128), full),
            pltpu.VMEM((4, 16, 128), full),
            pltpu.VMEM((4, 16, 128), full),
            pltpu.VMEM((8, 4, 16, 128), full),
            pltpu.VMEM((8, 8, 128), full),
            pltpu.VMEM((4, 8, 128), full),
            dma((2, 6, 8)),
        ],
        compiler_params=pltpu.CompilerParams(
            collective_id=1, has_side_effects=True, vmem_limit_bytes=VMEM_ROOM
        ),
        name="update",
    )(*args)
    return (
        outs[0][0, 0],
        outs[1],
        outs[2],
        outs[3],
        outs[4].T,
        outs[5].reshape(-1),
        outs[6],
        outs[7],
        outs[8],
        outs[9][:, :, 0],
        outs[10],
        outs[11],
        outs[12],
        outs[13],
        outs[14][:, :, 0],
        outs[15],
        outs[16].reshape(-1),
        outs[17].reshape(-1),
        outs[18].reshape(-1),
        outs[19].reshape(-1),
    )


def split_weights(weights):
    mats_full, up_full, down_full, bias_full = weights
    matrices = cut_pieces(mats_full, column_widths(), 1)
    vectors = [member.astype(jnp.float32) for member in cut_pieces(bias_full, bias_widths(), 0)]
    return (matrices, vectors, up_full, down_full)


def forward(weights, latents, noise, timesteps, labels, routes):
    matrices, vectors, up_full, down_full = split_weights(weights)
    w_qkv, w_proj, w_mod, w_time2, w_final, w_router, w_head, w_patch, w_time1, w_table = matrices
    b_qkv, b_proj, b_mod, b_patch, b_time1, b_time2, b_final = vectors
    num_latents = latents.shape[0]
    rows_here = num_latents * PATCHES
    steps_f = timesteps.astype(jnp.float32)
    signal, spread = noise_level(steps_f)
    noisy = signal[:, None] * latents + spread[:, None] * noise
    patches = noisy.reshape(rows_here, PD).astype(jnp.bfloat16)
    embedded = (
        contract(patches, w_patch, 1, 1).reshape(num_latents, PATCHES, D)
        + b_patch
        + positions()[None]
    )
    freq_low = time_features(steps_f).astype(jnp.bfloat16)
    pre_time = contract(freq_low, w_time1, 1, 1) + b_time1
    hid_time = jax.nn.silu(pre_time).astype(jnp.bfloat16)
    label_hot = (labels[:, None] == jnp.arange(CLASSES, dtype=jnp.int32)[None, :]).astype(
        jnp.float32
    )
    label_emb = lax.dot_general(
        label_hot,
        w_table.astype(jnp.float32),
        (((1,), (1,)), ((), ())),
        precision=lax.Precision.HIGHEST,
        preferred_element_type=jnp.float32,
    )
    cond = product(hid_time, w_time2) + b_time2 + label_emb
    cond_act = jax.nn.silu(cond).astype(jnp.bfloat16)
    modulation = product(cond_act, w_mod) + b_mod
    final_mod = product(cond_act, w_final) + b_final
    shift_attn, scale_attn, gate_attn, shift_moe, scale_moe, gate_moe = [
        member[:, None, :] for member in jnp.split(modulation, 6, 1)
    ]
    shift_fin, scale_fin = [member[:, None, :] for member in jnp.split(final_mod, 2, 1)]
    normed_one, inv_one = layer_norm(embedded)
    attn_in = (
        (normed_one * (1.0 + scale_attn) + shift_attn).astype(jnp.bfloat16).reshape(rows_here, D)
    )
    qkv_out = (
        (product(attn_in, w_qkv) + b_qkv)
        .astype(jnp.bfloat16)
        .reshape(num_latents, PATCHES, 3, HEADS, HD)
    )
    scores = jnp.einsum(
        "lqhd,lkhd->lhqk", qkv_out[:, :, 0], qkv_out[:, :, 1], preferred_element_type=jnp.float32
    ) * HD ** (-0.5)
    log_totals = jax.nn.logsumexp(scores, -1)
    probs_low = jax.nn.softmax(scores, -1).astype(jnp.bfloat16)
    attended = (
        jnp.einsum(
            "lhqk,lkhd->lqhd", probs_low, qkv_out[:, :, 2], preferred_element_type=jnp.float32
        )
        .astype(jnp.bfloat16)
        .reshape(rows_here, D)
    )
    attn_out = (product(attended, w_proj) + b_proj).reshape(num_latents, PATCHES, D)
    middle = embedded + gate_attn * attn_out
    normed_two, inv_two = layer_norm(middle)
    moe_in = (normed_two * (1.0 + scale_moe) + shift_moe).astype(jnp.bfloat16).reshape(rows_here, D)
    logits = product(moe_in, w_router)
    route_hot = (routes[:, :, None] == jnp.arange(EXPERTS, dtype=jnp.int32)[None, None, :]).astype(
        jnp.float32
    )
    gate_vals = jax.nn.softmax(jnp.sum(route_hot * logits[:, None, :], 2), -1)
    slot_of, slot_meta = pack_slots(routes)
    routed, shared_out = experts_forward(slot_of, slot_meta, moe_in, up_full, down_full)
    moe_out = gate_vals[:, 0:1] * routed[0] + gate_vals[:, 1:2] * routed[1] + shared_out
    moe_out = moe_out.reshape(num_latents, PATCHES, D)
    final_state = middle + gate_moe * moe_out
    normed_fin, inv_fin = layer_norm(final_state)
    head_in = (
        (normed_fin * (1.0 + scale_fin) + shift_fin).astype(jnp.bfloat16).reshape(rows_here, D)
    )
    errors = product(head_in, w_head) - noise.reshape(rows_here, PD)
    return SimpleNamespace(
        patches=patches,
        freq_low=freq_low,
        pre_time=pre_time,
        hid_time=hid_time,
        label_hot=label_hot,
        cond=cond,
        cond_act=cond_act,
        scale_attn=scale_attn,
        gate_attn=gate_attn,
        scale_moe=scale_moe,
        gate_moe=gate_moe,
        scale_fin=scale_fin,
        normed_one=normed_one,
        inv_one=inv_one,
        attn_in=attn_in,
        qkv_out=qkv_out,
        log_totals=log_totals,
        attended=attended,
        attn_out=attn_out,
        normed_two=normed_two,
        inv_two=inv_two,
        moe_in=moe_in,
        route_hot=route_hot,
        gate_vals=gate_vals,
        slot_of=slot_of,
        slot_meta=slot_meta,
        routed=routed,
        moe_out=moe_out,
        normed_fin=normed_fin,
        inv_fin=inv_fin,
        head_in=head_in,
        errors=errors,
    )


def backward(weights, kept, total_tokens):
    matrices, vectors, up_full, down_full = split_weights(weights)
    w_qkv, w_proj, w_mod, w_time2, w_final, w_router, w_head, w_patch, w_time1, w_table = matrices
    num_latents = kept.normed_one.shape[0]
    rows_here = num_latents * PATCHES
    grad_head, grad_head_in, unused = linear_back(
        kept.errors * (2.0 / total_tokens), kept.head_in, w_head
    )
    grad_head_in = grad_head_in.reshape(num_latents, PATCHES, D)
    grad_final_mod = jnp.concatenate(
        [jnp.sum(grad_head_in, 1), jnp.sum(grad_head_in * kept.normed_fin, 1)], 1
    )
    grad_state = norm_back(
        grad_head_in * (1.0 + kept.scale_fin), kept.normed_fin, kept.inv_fin
    )
    grad_gate_moe = jnp.sum(kept.moe_out * grad_state, 1)
    grad_moe = (kept.gate_moe * grad_state).reshape(rows_here, D)
    grad_moe_low = grad_moe.astype(jnp.bfloat16)
    moe_in = kept.moe_in
    gate_vals = kept.gate_vals
    routed = kept.routed
    grad_gates = jnp.stack([jnp.sum(routed[k] * grad_moe, 1) for k in range(2)], 1)
    grad_pair = jnp.stack(
        [(gate_vals[:, k : k + 1] * grad_moe).astype(jnp.bfloat16) for k in range(2)], 0
    )
    up_slabs, down_slabs, grad_moe_in = experts_backward(
        kept.slot_of, kept.slot_meta, moe_in, grad_pair, grad_moe_low, up_full, down_full
    )
    grad_picked = gate_vals * (grad_gates - jnp.sum(gate_vals * grad_gates, 1, keepdims=True))
    grad_logits = jnp.sum(kept.route_hot * grad_picked[:, :, None], 1)
    grad_router, grad_from_router, unused = linear_back(grad_logits, moe_in, w_router)
    grad_moe_in = (grad_moe_in + grad_from_router).reshape(num_latents, PATCHES, D)
    grad_middle = grad_state + norm_back(
        grad_moe_in * (1.0 + kept.scale_moe), kept.normed_two, kept.inv_two
    )
    grad_gate_attn = jnp.sum(kept.attn_out * grad_middle, 1)
    grad_proj, grad_attended, grad_b_proj = linear_back(
        (kept.gate_attn * grad_middle).reshape(rows_here, D), kept.attended, w_proj
    )
    grad_att_low = grad_attended.astype(jnp.bfloat16).reshape(num_latents, PATCHES, HEADS, HD)
    qkv_out = kept.qkv_out
    queries = qkv_out[:, :, 0]
    key_rows = qkv_out[:, :, 1]
    values = qkv_out[:, :, 2]
    scores = jnp.einsum(
        "lqhd,lkhd->lhqk", queries, key_rows, preferred_element_type=jnp.float32
    ) * HD ** (-0.5)
    probs = jnp.exp(scores - kept.log_totals[..., None])
    probs_low = probs.astype(jnp.bfloat16)
    grad_values = jnp.einsum(
        "lhqk,lqhd->lkhd", probs_low, grad_att_low, preferred_element_type=jnp.float32
    )
    grad_probs = jnp.einsum(
        "lqhd,lkhd->lhqk", grad_att_low, values, preferred_element_type=jnp.float32
    )
    grad_scores = (
        probs * (grad_probs - jnp.sum(probs * grad_probs, -1, keepdims=True)) * HD ** (-0.5)
    ).astype(jnp.bfloat16)
    grad_queries = jnp.einsum(
        "lhqk,lkhd->lqhd", grad_scores, key_rows, preferred_element_type=jnp.float32
    )
    grad_keys = jnp.einsum(
        "lhqk,lqhd->lkhd", grad_scores, queries, preferred_element_type=jnp.float32
    )
    grad_qkv = jnp.stack([grad_queries, grad_keys, grad_values], 2).reshape(rows_here, 3 * D)
    grad_w_qkv, grad_attn_in, grad_b_qkv = linear_back(grad_qkv, kept.attn_in, w_qkv)
    grad_attn_in = grad_attn_in.reshape(num_latents, PATCHES, D)
    grad_embedded = grad_middle + norm_back(
        grad_attn_in * (1.0 + kept.scale_attn), kept.normed_one, kept.inv_one
    )
    grad_emb_flat = grad_embedded.reshape(rows_here, D)
    grad_patch = contract(grad_emb_flat.astype(jnp.bfloat16), kept.patches, 0, 0)
    grad_b_patch = jnp.sum(grad_emb_flat, 0)
    grad_modulation = jnp.concatenate(
        [
            jnp.sum(grad_attn_in, 1),
            jnp.sum(grad_attn_in * kept.normed_one, 1),
            grad_gate_attn,
            jnp.sum(grad_moe_in, 1),
            jnp.sum(grad_moe_in * kept.normed_two, 1),
            grad_gate_moe,
        ],
        1,
    )
    grad_mod_low = grad_modulation.astype(jnp.bfloat16)
    grad_fin_low = grad_final_mod.astype(jnp.bfloat16)
    grad_act = contract(grad_mod_low, w_mod, 1, 1) + contract(grad_fin_low, w_final, 1, 1)
    grad_cond = slope_back(jax.nn.silu, kept.cond, grad_act)
    grad_cond_low = grad_cond.astype(jnp.bfloat16)
    grad_hid_time = contract(grad_cond_low, w_time2, 1, 1)
    grad_pre_time = slope_back(jax.nn.silu, kept.pre_time, grad_hid_time)
    grad_time_low = grad_pre_time.astype(jnp.bfloat16)
    mats_slabs = (
        jnp.concatenate([grad_w_qkv, grad_proj], 1)
        .astype(jnp.bfloat16)
        .reshape(1, WIDE_PIECES, PIECE, NARROW_PIECES, D)
        .transpose(0, 1, 3, 2, 4)
    )
    thin = jnp.concatenate([grad_router, grad_head, grad_patch], 1)
    grad_bias = jnp.concatenate(
        [
            grad_b_qkv,
            grad_b_proj,
            jnp.sum(grad_modulation, 0),
            grad_b_patch,
            jnp.sum(grad_pre_time, 0),
            jnp.sum(grad_cond, 0),
            jnp.sum(grad_final_mod, 0),
        ]
    )
    lows = jnp.concatenate(
        [
            kept.cond_act,
            kept.hid_time,
            grad_mod_low,
            grad_fin_low,
            grad_cond_low,
            grad_time_low,
            kept.freq_low,
        ],
        1,
    )
    return (up_slabs, down_slabs, mats_slabs, thin, grad_bias, lows, grad_cond)


def latent_grads(lows, grad_cond, labels, row_start, row_count):
    lows = lax.all_gather(lows, AXES, axis=0, tiled=True)
    grad_cond = lax.all_gather(grad_cond, AXES, axis=0, tiled=True)
    labels = lax.all_gather(labels, AXES, axis=0, tiled=True)
    cond_act, hid_time, grad_mod, grad_fin, grad_low, grad_time, freq_low = cut_pieces(
        lows, [D, D, 6 * D, 2 * D, D, D, FREQ], 1
    )

    def rows_of(member):
        return lax.dynamic_slice_in_dim(member, row_start, row_count, 1)

    label_hot = (labels[:, None] == jnp.arange(CLASSES, dtype=jnp.int32)[None, :]).astype(
        jnp.float32
    )
    grad_table = lax.dot_general(
        rows_of(grad_cond),
        label_hot,
        (((0,), (0,)), ((), ())),
        precision=lax.Precision.HIGHEST,
        preferred_element_type=jnp.float32,
    )
    return (
        contract(rows_of(cond_act), grad_mod, 0, 0),
        contract(rows_of(hid_time), grad_low, 0, 0),
        contract(rows_of(cond_act), grad_fin, 0, 0),
        contract(rows_of(grad_time), freq_low, 0, 0),
        grad_table,
    )


def factor_start(grad, row_old):
    squares = grad * grad + eps_fact
    row_new = decay * row_old + (1.0 - decay) * jnp.mean(squares, 2)
    return (row_new, jnp.sum(squares, 1), jnp.sum(row_new, 1))


def factor_update(grad, row_new, col_total, row_total, col_old, row_count):
    col_new = decay * col_old + (1.0 - decay) * (col_total / row_count)
    row_mean = row_total / row_count
    update = grad * lax.rsqrt(row_new[:, :, None] * col_new[:, None, :] / row_mean[:, None, None])
    return (col_new, update, jnp.sum(update * update, (1, 2)))


def clip_apply(master, update, square_total, entry_count):
    update_rms = jnp.sqrt(square_total / entry_count)
    return master - learn_rate * (update / jnp.maximum(1.0, update_rms / clip_level)[:, None, None])


def update_plain(grads, masters, factors, loss_part):
    mats_grad, up_grad, down_grad, bias_grad = grads
    mats, up_weights, down_weights, biases = masters
    mats_row, mats_col, up_row, up_col, down_row, down_col, bias_state = factors
    widths = column_widths()
    grad_pieces = cut_pieces(mats_grad, widths, 1)
    starts = [
        factor_start(grad_pieces[k][None], mats_row[k][None]) for k in range(len(widths))
    ]
    up_row_new, up_col_part, up_row_part = factor_start(up_grad, up_row)
    down_row_new, down_col_part, down_row_part = factor_start(down_grad, down_row)
    col_totals, row_totals, up_cols, up_rows, down_cols, down_rows, loss_total = lax.psum(
        (
            jnp.concatenate([member[1] for member in starts], 1)[0],
            jnp.concatenate([member[2] for member in starts], 0),
            up_col_part,
            up_row_part,
            down_col_part,
            down_row_part,
            loss_part,
        ),
        AXES,
    )
    col_total_pieces = cut_pieces(col_totals, widths, 0)
    col_old_pieces = cut_pieces(mats_col, widths, 0)
    steps = [
        factor_update(
            grad_pieces[k][None],
            starts[k][0],
            col_total_pieces[k][None],
            row_totals[k][None],
            col_old_pieces[k][None],
            D,
        )
        for k in range(len(widths))
    ]
    up_col_new, up_update, up_square = factor_update(
        up_grad, up_row_new, up_cols, up_rows, up_col, D
    )
    down_col_new, down_update, down_square = factor_update(
        down_grad, down_row_new, down_cols, down_rows, down_col, FF
    )
    bias_state_new = decay * bias_state + (1.0 - decay) * (bias_grad * bias_grad + eps_fact)
    bias_update = bias_grad * lax.rsqrt(bias_state_new)
    square_mats, square_up, square_down, square_bias = lax.psum(
        (
            jnp.concatenate([member[2] for member in steps], 0),
            up_square,
            down_square,
            jnp.sum(bias_update * bias_update),
        ),
        AXES,
    )
    master_pieces = cut_pieces(mats, widths, 1)
    mats_new = jnp.concatenate(
        [
            clip_apply(
                master_pieces[k][None], steps[k][1], square_mats[k][None], D * widths[k]
            )[0]
            for k in range(len(widths))
        ],
        1,
    )
    up_new = clip_apply(up_weights, up_update, square_up, D * FF)
    down_new = clip_apply(down_weights, down_update, square_down, D * FF)
    bias_rms = jnp.sqrt(square_bias / (15 * D))
    bias_new = biases - learn_rate * (bias_update / jnp.maximum(1.0, bias_rms / clip_level))
    return (
        loss_total,
        mats_grad,
        mats_new,
        mats_new.astype(jnp.bfloat16),
        jnp.concatenate([member[0] for member in starts], 0),
        jnp.concatenate([member[0][0] for member in steps], 0),
        up_grad,
        up_new,
        up_new.astype(jnp.bfloat16),
        up_row_new,
        up_col_new,
        down_grad,
        down_new,
        down_new.astype(jnp.bfloat16),
        down_row_new,
        down_col_new,
        bias_grad,
        bias_new,
        bias_new.astype(jnp.bfloat16),
        bias_state_new,
    )


def body(
    latents,
    noise,
    timesteps,
    labels,
    routes,
    mats,
    up_weights,
    down_weights,
    biases,
    *factors,
):
    rows_here = mats.shape[0]
    flat = jnp.concatenate([mats.reshape(-1), biases], 0).astype(jnp.bfloat16)
    flat = lax.all_gather(flat, AXES, axis=0, tiled=False)
    gathered = (
        flat[:, : rows_here * mats.shape[1]].reshape(-1, mats.shape[1]),
        lax.all_gather(up_weights.astype(jnp.bfloat16), AXES, axis=1, tiled=True),
        lax.all_gather(down_weights.astype(jnp.bfloat16), AXES, axis=1, tiled=True),
        flat[:, rows_here * mats.shape[1] :].reshape(-1),
    )
    kept = forward(gathered, latents, noise, timesteps, labels, routes)
    total_tokens = latents.shape[0] * PATCHES * lax.axis_size(AXES)
    up_slabs, down_slabs, mats_slabs, thin, grad_bias, lows, grad_cond = backward(
        gathered, kept, total_tokens
    )
    loss_part = jnp.sum(kept.errors * kept.errors)
    masters = (mats, up_weights, down_weights, biases)
    kernel_fits = lax.axis_size(WIDE) == WIDE_PIECES and lax.axis_size(NARROW) == NARROW_PIECES
    if kernel_fits:
        sums, rows, lat = reduce_slabs(
            down_slabs,
            up_slabs,
            mats_slabs,
            thin_slab(thin, grad_bias),
            lat_block(lows, grad_cond, labels),
        )
        outs = update_kernel_call(sums, rows, lat, masters, factors, loss_part)
    else:
        grads = plain_grads(
            down_slabs, up_slabs, mats_slabs, thin, grad_bias, lows, grad_cond, labels, rows_here
        )
        outs = update_plain(grads, masters, factors, loss_part)
    return (outs[0] / total_tokens,) + tuple(outs[1:])


def solution(mesh):
    rows = P(AXES, None)
    middle_rows = P(None, AXES, None)
    row_factor = P(None, AXES)
    line = P(AXES)
    in_specs = (
        (rows, rows, line, line, rows)
        + (rows, middle_rows, middle_rows, line)
        + (row_factor, P(), row_factor, P(), row_factor, P(), line)
    )
    out_specs = (
        (P(), rows, rows, rows, row_factor, P())
        + (middle_rows, middle_rows, middle_rows, row_factor, P()) * 2
        + (line, line, line, line)
    )
    return jax.shard_map(body, mesh=mesh, in_specs=in_specs, out_specs=out_specs, check_vma=False)
```

profile of v0, /device:TPU:0, one launch (start us, length us, event | category | flops | bytes accessed | tf_op | source)
XLA Modules:
  0.0 1006.7 jit_solution(12027878039115000944)
XLA Ops:
  10.7 1.6 copy.187
  23.0 74.4 %all-gather.9.cloned.1.call-done = bf16[32,1,75732]{2,1,0:T(2,128)(2,1)} async-done(((bf16[1,1,75732]{2,1,0:T(2,128)(2,1)}), bf16[32,1,75732]{2,1,0:T(2,128)(2,1)}) %all-gather.9.cloned.1.call-update) | async-done | bytes 4846864 | tf_op jit(solution)/shard_map/all_gather | solution.py:1635
  97.3 6.6 copy.192
  103.9 2.5 slice.126
  106.5 9.8 reshape.560
  116.4 1.6 fusion.132
  118.5 1.8 multiply_convert_fusion.6
  121.4 2.2 multiply_convert_fusion.5
  125.3 2.9 fusion.13
  128.2 4.3 copy.127
  132.4 5.6 reshape.563
  138.1 2.4 fusion.126
  141.6 2.1 exponential_reduce_fusion
  144.3 1.4 fusion.52
  146.5 1.9 convolution_add_fusion.3
  154.0 115.2 %all-gather.5.cloned.1.call-done = bf16[18,384,1536]{2,0,1:T(8,128)(2,1)} async-done(((bf16[18,12,1536]{2,0,1:T(8,128)(2,1)}), bf16[18,384,1536]{2,0,1:T(8,128)(2,1)}) %all-gather.5.cloned.1.call-update) | async-done | bytes 21233680 | tf_op jit(solution)/shard_map/all_gather | solution.py:1638
  269.2 24.2 %copy.134.up_ref = bf16[18,384,1536]{2,1,0:T(8,128)(2,1)} copy(bf16[18,384,1536]{2,0,1:T(8,128)(2,1)} %all-gather.5.cloned.1.call-done) | data formatting | bytes 42467328 | tf_op jit(solution)/shard_map/all_gather | solution.py:1638
  293.3 113.3 %all-gather.7.cloned.1.call-done.down_ref = bf16[18,1536,384]{2,1,0:T(8,128)(2,1)} async-done(((bf16[18,48,384]{2,1,0:T(8,128)(2,1)}), bf16[18,1536,384]{2,1,0:T(8,128)(2,1)}) %all-gather.7.cloned.1.call-update) | async-done | bytes 21233680 | tf_op jit(solution)/shard_map/all_gather | solution.py:1639
  406.6 60.8 %experts_forward.1 = (f32[2,1024,384]{2,1,0:T(8,128)}, f32[1024,384]{1,0:T(8,128)}) custom-call(s32[2,16]{1,0:T(2,128)} %pad_add_fusion.1.meta, s32[2,1024]{1,0:T(2,128)} %pad_add_fusion.slot_at.slots_ref, s32[2,1024]{1,0:T(2,128)} %pad_add_fusion.slot_at.slots_ref, bf16[1024,384]{1,0:T(8,128)(2,1)} %bitcast.193, bf16[18,384,1536]{2,1,0:T(8,128)(2,1)} %copy.134.up_ref, ...), custom_call_target="tpu_custom_call" | custom-call | flops 20000000000 | bytes 50000000 | tf_op jit(solution)/shard_map/experts_forward/pallas_call | solution.py:232
  467.4 2.7 fusion.37
  472.1 2.0 multiply_reduce_fusion.13
  474.1 1.5 fusion.35
  476.8 3.5 multiply_reduce_fusion.2
  481.6 1.8 copy-done.10
  485.2 1.3 pad_maximum_fusion.1.pair_ref
  486.5 125.8 %experts_backward.1 = (bf16[18,8,4,48,384]{4,3,2,1,0:T(8,128)(2,1)}, bf16[18,8,4,48,384]{4,3,2,1,0:T(8,128)(2,1)}, f32[1024,384]{1,0:T(8,128)}) custom-call(s32[2,16]{1,0:T(2,128)} %pad_add_fusion.1.meta, s32[2,1024]{1,0:T(2,128)} %pad_add_fusion.slot_at.slots_ref, s32[2,1024]{1,0:T(2,128)} %pad_add_fusion.slot_at.slots_ref, bf16[1024,384]{1,0:T(8,128)(2,1)} %bitcast.194, ...), custom_call_target="tpu_custom_call" | custom-call | flops 44999999488 | bytes 90000000 | tf_op jit(solution)/shard_map/experts_backward/pallas_call | solution.py:355
  612.3 2.0 fusion.29
  615.6 3.4 multiply_reduce_fusion.3
  620.3 1.6 convolution_convert_fusion.1
  623.1 2.4 reshape.575
  625.5 4.9 fusion.60
  630.4 13.0 %fusion.45 = f32[4,256,1,6,64]{1,4,3,0,2:T(8,128)} fusion(f32[4,6,256,256]{2,3,1,0:T(8,128)} %fusion.60, f32[4,6,256,256]{2,3,1,0:T(8,128)} %copy-done, f32[4,6,256]{2,1,0:T(8,128)S(1)} %log_add_fusion, bf16[4,256,1,6,64]{1,0,4,3,2:T(4,128)(2,1)} %copy-done.22), kind=kOutput, calls=%fused_computation.78 | convolution fusion | flops 215488768 | bytes 14966784 | tf_op jit(solution)/shard_map/lhqk,lkhd->lqhd/dot_general | solution.py:1415
  643.4 13.1 %fusion.48 = f32[4,256,1,6,64]{1,4,3,0,2:T(8,128)} fusion(f32[4,6,256,256]{2,3,1,0:T(8,128)} %fusion.60, f32[4,6,256,256]{2,3,1,0:T(8,128)} %copy-done, f32[4,6,256]{2,1,0:T(8,128)S(1)} %log_add_fusion, bf16[4,256,1,6,64]{1,0,4,3,2:T(4,128)(2,1)} %copy-done.21), kind=kOutput, calls=%fused_computation.79 | convolution fusion | flops 215488768 | bytes 14966784 | tf_op jit(solution)/shard_map/lhqk,lqhd->lkhd/dot_general | solution.py:1418
  656.5 4.2 fusion.42
  661.5 3.5 copy.147
  667.4 3.3 multiply_reduce_fusion.5
  673.5 2.3 copy.171
  678.3 2.6 copy.149
  680.8 1.9 fusion.123
  685.5 1.5 pad_maximum_fusion.2.thin_ref
  687.0 234.0 %reduce_slabs.1 = (f32[19,48,384]{2,1,0:T(8,128)}, f32[19,4,12,384]{3,2,1,0:T(8,128)}, bf16[4,2,2,2,16,1536]{5,4,3,2,1,0:T(8,128)(2,1)}) custom-call(bf16[18,16,2,48,384]{4,3,2,1,0:T(8,128)(2,1)} %bitcast.184, bf16[1,16,2,48,384]{4,3,2,1,0:T(8,128)(2,1)} %pad_maximum_fusion.2.thin_ref, bf16[18,16,2,48,384]{4,3,2,1,0:T(8,128)(2,1)} %bitcast.183, ...), custom_call_target="tpu_custom_call" | custom-call | tf_op jit(solution)/shard_map/reduce_slabs/pallas_call | solution.py:726
  921.0 54.0 %update.1 = (f32[1,1]{1,0:T(1,128)}, f32[12,6296]{1,0:T(8,128)}, f32[12,6296]{1,0:T(8,128)}, bf16[12,6296]{1,0:T(8,128)(2,1)}, f32[12,10]{1,0:T(8,128)}, /*index...) custom-call(f32[19,48,384]{2,1,0:T(8,128)} %get-tuple-element.53.sum, ...), custom_call_target="tpu_custom_call" | custom-call | tf_op jit(solution)/shard_map/update/pallas_call | solution.py:1193
  975.0 1.6 reduce.5
  976.5 1.8 reduce.6
  978.4 1.7 copy.155
  980.0 1.4 copy.156
  983.3 1.8 copy.219
  985.0 1.8 copy.220
  (292 shorter events, 59.3 us)
Async XLA Ops:
  7.2 3.5 copy-start.15
  7.2 90.1 %all-gather.9.cloned.1.call-start = ((), (), s32[]{:S(2)}) async-start(), calls=%async_computation.2 | async-start | bytes 10002432 | tf_op jit(solution)/shard_map/all_gather | solution.py:1635
  10.7 258.5 %all-gather.5.cloned.1.call-start = ((), (), s32[]{:S(2)}) async-start(), calls=%async_computation | async-start | bytes 29196288 | tf_op jit(solution)/shard_map/all_gather | solution.py:1638
  12.4 394.2 %all-gather.7.cloned.1.call-start = ((), (), s32[]{:S(2)}) async-start(), calls=%async_computation.1 | async-start | bytes 21897216 | tf_op jit(solution)/shard_map/all_gather | solution.py:1639
  13.4 3.2 copy-start.52
  13.4 4.2 copy-start.53
  13.4 5.0 copy-start.42
  13.4 5.7 copy-start.54
  13.4 6.4 copy-start.36
  22.9 95.6 %copy-start.55 = (bf16[4,128]{1,0:T(4,128)(2,1)}, bf16[4,128]{1,0:T(4,128)(2,1)S(1)}, u32[]{:S(2)}) copy-start(bf16[4,128]{1,0:T(4,128)(2,1)S(1)} %get-tuple-element.216) | copy-start | bytes 3076
  22.9 95.6 %copy-start.57 = (bf16[4,128]{1,0:T(4,128)(2,1)}, bf16[4,128]{1,0:T(4,128)(2,1)S(1)}, u32[]{:S(2)}) copy-start(bf16[4,128]{1,0:T(4,128)(2,1)S(1)} %get-tuple-element.217) | copy-start | bytes 3076
  116.4 7.2 copy-start.4
  120.3 3.3 copy-start.49
  123.6 29.0 %copy-start.43 = (bf16[4,384]{1,0:T(4,128)(2,1)}, bf16[4,384]{1,0:T(4,128)(2,1)S(1)}, u32[]{:S(2)}) copy-start(bf16[4,384]{1,0:T(4,128)(2,1)S(1)} %get-tuple-element.226) | copy-start | bytes 9220
  140.5 3.3 copy-start.23
  141.6 2.7 copy-start
  146.5 1.9 copy-start.19
  471.3 4.3 copy-start.1
  472.0 2.0 copy-start.11
  656.5 4.2 copy-start.16
  656.5 4.2 copy-start.17
  661.5 3.5 copy-start.20
  661.5 4.1 copy-start.14
  661.5 4.9 copy-start.12
  661.5 5.9 slice-start
  665.0 2.4 slice-start.1
  667.4 3.4 copy-start.47
  667.4 3.4 copy-start.46
  667.4 3.4 copy-start.45
  667.4 3.4 copy-start.48
  670.7 1.9 copy-start.44
  670.7 1.9 copy-start.50
  670.7 1.9 copy-start.56
  670.7 1.9 copy-start.58
  670.7 1.9 copy-start.60
  670.7 1.9 copy-start.61
  673.4 2.3 copy-start.31
  678.2 2.6 copy-start.6
  680.8 2.0 copy-start.28
  680.8 2.2 copy-start.40
  682.8 2.0 copy-start.65
  975.0 11.8 %copy-start.34 = (bf16[12,6296]{1,0:T(8,128)(2,1)S(1)}, bf16[12,6296]{1,0:T(8,128)(2,1)}, u32[]{:S(2)}) copy-start(bf16[12,6296]{1,0:T(8,128)(2,1)} %get-tuple-element.266) | copy-start | bytes 453316
  975.0 12.5 %copy-start.25 = (f32[18,12,1536]{2,1,0:T(8,128)S(1)}, f32[18,12,1536]{2,1,0:T(8,128)}, u32[]{:S(2)}) copy-start(f32[18,12,1536]{2,1,0:T(8,128)} %get-tuple-element.269) | copy-start | bytes 3981316
  987.5 2.1 copy-start.24
  994.2 2.3 copy-start.41
  994.2 2.9 copy-start.64
  994.2 3.5 copy-start.63
  994.2 4.0 copy-start.62
  (27 other events, 33.8 us)
Sparse Core Ops, SparseCore 0:
  11.5 85.7 all-gather.8
  100.8 168.2 all-gather.4
  272.6 134.0 all-gather.6
where the time goes:
time: 1010 us
  Pallas kernels  475 us (47%)
  waiting for transfers between devices  303 us (30%)
  local copies, waits for them, and re-layouts  108 us (11%)
  matrix products  67.2 us (7%)
  other arithmetic  36.5 us (4%)
  between operations  16.9 us (2%)
    pallas_call x1, Pallas kernels, reduce_slabs(): pl.pallas_call(reduce_kernel, out_shape=[jax.ShapeDtypeStruct((direct, PI...  234 us
    pallas_call x1, Pallas kernels, experts_backward(): pl.pallas_call(backward_kernel, grid_spec=pltpu.PrefetchScalarGridSpec(nu...  126 us
    all_gather x1, waiting for transfers between devices, body(): lax.all_gather(up_weights.astype(jnp.bfloat16), AXES, axis=1, tiled=True)  115 us
    all_gather x1, waiting for transfers between devices, body(): lax.all_gather(down_weights.astype(jnp.bfloat16), AXES, axis=1, tiled=True)  113 us
    all_gather x1, waiting for transfers between devices, body(): flat = lax.all_gather(flat, AXES, axis=0, tiled=False)  74.4 us
    pallas_call x1, Pallas kernels, experts_forward(): pl.pallas_call(forward_kernel, grid_spec=pltpu.PrefetchScalarGridSpec(num...  60.8 us
    pallas_call x1, Pallas kernels, update_kernel_call(): pl.pallas_call(update_kernel, out_shape=[jax.ShapeDtypeStruct((1, 1), ful...  54 us
    unnamed x175, local copies, waits for them, and re-layouts  38.6 us
  transfers between devices with their start and end apart: 3, of which 3 were waited for; matrix products, arithmetic and copies ran while one was open for 9% of the time, Pallas kernels for 0%

commit v1 on v0

--- a/solution.py
+++ b/solution.py
@@ -29,6 +29,8 @@
 PIECE = 48
 ROWS = 12
 LAT_ROWS = 16
+LQK = "lqhd,lkhd->lhqk"
+CUT = 768
 LAT_COLS = 1536
 PATCHES = 256
 
@@ -164,50 +166,38 @@
     return 0.5 * values * (1.0 + jnp.tanh(inner))
 
 
+def up_columns(chunks, cut):
+    return jnp.concatenate([chunks[cut // D + k] for k in range(CUT // D)], 1)
+
+
 def slot_pick(slots_ref, base, rows):
     place = base + lax.broadcasted_iota(jnp.int32, (rows, slots_ref.shape[1]), 0)
     return ((slots_ref[0:1, :] == place) | (slots_ref[1:2, :] == place)).astype(jnp.bfloat16)
 
 
-def forward_kernel(meta, slot_at, slots_ref, x_ref, up_ref, down_ref, routed_ref, shared_ref, y_ref):
+def forward_kernel(meta, slot_at, slots_ref, x_ref, up_ref, down_ref, routed_ref, y_ref):
     stack_id = pl.program_id(0)
     tokens = x_ref.shape[0]
 
     def expert(rows):
         total = None
-        for cut in range(0, FF, D):
-            pre_act = product(rows, up_ref[0, :, cut : cut + D])
-            part = product(gelu_only(pre_act).astype(jnp.bfloat16), down_ref[0, cut : cut + D, :])
+        for cut in range(0, FF, CUT):
+            pre_act = product(rows, up_columns(up_ref[0], cut))
+            part = product(gelu_only(pre_act).astype(jnp.bfloat16), down_ref[0, cut : cut + CUT])
             total = part if total is None else total + part
         return total
 
-    @pl.when(stack_id < EXPERTS)
-    def _():
-        owner = jnp.minimum(stack_id, EXPERTS - 1)
-        start = meta[0, owner]
-
-        def block(number, unused):
-            base = pl.multiple_of(start + number * BLK, 8)
-            rows = product(slot_pick(slots_ref, base, BLK), x_ref[...]).astype(jnp.bfloat16)
-            y_ref[pl.ds(base, BLK), :] = expert(rows)
-            return unused
-
-        lax.fori_loop(0, (meta[1, owner] + BLK - 1) // BLK, block, 0)
-
-    @pl.when(stack_id >= EXPERTS)
-    def _():
-        @pl.when(stack_id == EXPERTS)
-        def _():
-            shared_ref[...] = jnp.zeros_like(shared_ref)
-
-        def block(number, unused):
-            base = pl.multiple_of(number * BLK, BLK)
-            shared_ref[pl.ds(base, BLK), :] += expert(x_ref[pl.ds(base, BLK), :])
-            return unused
-
-        lax.fori_loop(0, tokens // BLK, block, 0)
-
-    @pl.when(stack_id == EXPERTS + SHARED - 1)
+    start = meta[0, stack_id]
+
+    def block(number, unused):
+        base = pl.multiple_of(start + number * BLK, 8)
+        rows = product(slot_pick(slots_ref, base, BLK), x_ref[...]).astype(jnp.bfloat16)
+        y_ref[pl.ds(base, BLK), :] = expert(rows)
+        return unused
+
+    lax.fori_loop(0, (meta[1, stack_id] + BLK - 1) // BLK, block, 0)
+
+    @pl.when(stack_id == EXPERTS - 1)
     def _():
         def group(number, unused):
             for step in range(8):
@@ -233,20 +223,17 @@
         forward_kernel,
         grid_spec=pltpu.PrefetchScalarGridSpec(
             num_scalar_prefetch=2,
-            grid=(EXPERTS + SHARED,),
+            grid=(EXPERTS,),
             in_specs=[
                 whole_block((2, tokens)),
                 whole_block((tokens, D)),
-                pl.BlockSpec((1, D, FF), lambda e, *unused: (e, 0, 0)),
+                pl.BlockSpec((1, NARROW_PIECES, D, D), lambda e, *unused: (e, 0, 0, 0)),
                 pl.BlockSpec((1, FF, D), lambda e, *unused: (e, 0, 0)),
             ],
-            out_specs=[whole_block((2, tokens, D)), whole_block((tokens, D))],
+            out_specs=whole_block((2, tokens, D)),
             scratch_shapes=[pltpu.VMEM((slot_room(tokens), D), jnp.float32)],
         ),
-        out_shape=[
-            jax.ShapeDtypeStruct((2, tokens, D), jnp.float32),
-            jax.ShapeDtypeStruct((tokens, D), jnp.float32),
-        ],
+        out_shape=jax.ShapeDtypeStruct((2, tokens, D), jnp.float32),
         compiler_params=pltpu.CompilerParams(vmem_limit_bytes=VMEM_ROOM),
         cost_estimate=pl.CostEstimate(
             flops=20_000_000_000, bytes_accessed=50_000_000, transcendentals=0
@@ -278,13 +265,13 @@
 
     def expert(rows, grads):
         total = None
-        for cut in range(0, FF, D):
-            up_part = up_ref[0, :, cut : cut + D]
+        for cut in range(0, FF, CUT):
+            up_part = up_columns(up_ref[0], cut)
             activated, slope = gelu_slope(product(rows, up_part))
-            grad_act = contract(grads, down_ref[0, cut : cut + D, :], 1, 1)
+            grad_act = contract(grads, down_ref[0, cut : cut + CUT], 1, 1)
             grad_pre = (grad_act * slope).astype(jnp.bfloat16)
-            down_sum[cut : cut + D, :] += contract(activated.astype(jnp.bfloat16), grads, 0, 0)
-            up_sum[:, cut : cut + D] += contract(rows, grad_pre, 0, 0)
+            down_sum[cut : cut + CUT, :] += contract(activated.astype(jnp.bfloat16), grads, 0, 0)
+            up_sum[:, cut : cut + CUT] += contract(rows, grad_pre, 0, 0)
             part = contract(grad_pre, up_part, 1, 1)
             total = part if total is None else total + part
         return total
@@ -362,7 +349,7 @@
                 whole_block((tokens, D)),
                 whole_block((2, tokens, D)),
                 whole_block((tokens, D)),
-                pl.BlockSpec((1, D, FF), lambda e, *unused: (e, 0, 0)),
+                pl.BlockSpec((1, NARROW_PIECES, D, D), lambda e, *unused: (e, 0, 0, 0)),
                 pl.BlockSpec((1, FF, D), lambda e, *unused: (e, 0, 0)),
             ],
             out_specs=[slab_spec, slab_spec, whole_block((tokens, D))],
@@ -1235,15 +1222,531 @@
     )
 
 
+def gather_kernel(
+    mats_in,
+    bias_in,
+    down_in,
+    up_in,
+    patches,
+    places,
+    freq_low,
+    label_hot,
+    mats_out,
+    bias_out,
+    down_out,
+    up_out,
+    mods_out,
+    fin_out,
+    time_out,
+    cond_out,
+    qkv_out,
+    att_out,
+    middle_out,
+    moe_out,
+    logits_out,
+    shared_out,
+    mats_got,
+    mats_own,
+    up_got,
+    up_wide,
+    up_own,
+    embedded,
+    down_here,
+    up_here,
+    near_send,
+    near_recv,
+    own_sem,
+    level_send,
+    level_recv,
+    one_send,
+    one_recv,
+    two_send,
+    two_recv,
+    core_send,
+    core_recv,
+    bias_send,
+    bias_recv,
+    here_sem,
+):
+    n_down, n_up = down_in.shape[0], up_own.shape[0]
+    slabs = 1 + n_down + n_up
+    wide, narrow = lax.axis_index(WIDE), lax.axis_index(NARROW)
+    z, x = wide // 2, wide % 2
+    y, c = narrow // 2, narrow % 2
+    mates = [
+        (wide, (y + (k // 2) * (1 - 2 * y)) * 2 + c + (k % 2) * (1 - 2 * c)) for k in range(1, 4)
+    ]
+    levels = [(((z + k) % 4) * 2 + x, narrow) for k in range(1, 4)]
+    to_x = (z * 2 + 1 - x, narrow)
+    to_core, to_y = mates[0], mates[1]
+    to_one = (z * 2 + x + (1 - c) * (1 - 2 * x), (y + c * (1 - 2 * y)) * 2 + c)
+    to_two = (z * 2 + x + c * (1 - 2 * x), (y + (1 - c) * (1 - 2 * y)) * 2 + c)
+    barrier = pltpu.get_barrier_semaphore()
+    for target in mates + levels + [to_x]:
+        pl.semaphore_signal(barrier, inc=1, device_id=target, device_id_type=MESH_ID)
+    pl.semaphore_wait(barrier, 7)
+
+    def remote(source, target, send, recv, device):
+        return pltpu.make_async_remote_copy(
+            src_ref=source,
+            dst_ref=target,
+            send_sem=send,
+            recv_sem=recv,
+            device_id=device,
+            device_id_type=MESH_ID,
+        )
+
+    def near_mats(k):
+        return remote(
+            mats_in.at[mates[k - 1][1]],
+            mats_got.at[narrow],
+            near_send.at[0, k],
+            near_recv.at[0, k],
+            mates[k - 1],
+        )
+
+    def near_up(k):
+        return remote(
+            up_in.at[mates[k - 1][1]],
+            up_got.at[narrow],
+            near_send.at[1, k],
+            near_recv.at[1, k],
+            mates[k - 1],
+        )
+
+    own_mats = pltpu.make_async_copy(mats_in.at[narrow], mats_got.at[narrow], own_sem.at[0])
+    own_up = pltpu.make_async_copy(up_in.at[narrow], up_got.at[narrow], own_sem.at[1])
+    own_bias = pltpu.make_async_copy(bias_in, bias_out.at[z, x, y, c], own_sem.at[2])
+    own_mats.start()
+    own_up.start()
+    own_bias.start()
+    for k in range(1, 4):
+        near_mats(k).start()
+
+    def bias_level(k):
+        return remote(
+            bias_in, bias_out.at[z, x, y, c], bias_send.at[k - 1], bias_recv.at[k - 1], levels[k - 1]
+        )
+
+    def bias_x():
+        part = bias_out.at[:, x, y, c]
+        return remote(part, part, bias_send.at[3], bias_recv.at[3], to_x)
+
+    def bias_y():
+        part = bias_out.at[:, :, y, c]
+        return remote(part, part, bias_send.at[4], bias_recv.at[4], to_y)
+
+    def bias_core():
+        part = bias_out.at[:, :, :, c]
+        return remote(part, part, bias_send.at[5], bias_recv.at[5], to_core)
+
+    for k in range(1, 4):
+        bias_level(k).start()
+    own_mats.wait()
+    for k in range(1, 4):
+        near_mats(k).wait_recv()
+        near_up(k).start()
+    for n in range(NARROW_PIECES):
+        mats_own[n * ROWS : (n + 1) * ROWS] = mats_got[n].astype(jnp.float32)[:ROWS]
+    mats_got[0, :, :] = mats_own[:16].astype(jnp.bfloat16)
+    mats_got[1, :, :] = mats_own[16:32].astype(jnp.bfloat16)
+    mats_got[2, :, :] = mats_own[32:].astype(jnp.bfloat16)
+    own_bias.wait()
+
+    def turn(number):
+        return (number + EXPERTS) % n_up
+
+    def whole(kind, s):
+        if kind == 0:
+            return mats_out
+        if kind == 1:
+            return down_out.at[turn(s - 1)]
+        return up_out.at[turn(s - 1 - n_down)]
+
+    def source(kind, s):
+        if kind == 0:
+            return mats_got.at[pl.ds(0, 3)]
+        if kind == 1:
+            return down_in.at[turn(s - 1)]
+        return up_own.at[turn(s - 1 - n_down)]
+
+    def piece(ref, kind, at):
+        z_at, x_at, y_at, c_at = at
+        if kind == 1:
+            return ref.at[z_at, x_at, y_at, c_at]
+        return ref.at[y_at, c_at, z_at, x_at]
+
+    every = slice(None)
+
+    def own_copy(kind, s):
+        return pltpu.make_async_copy(
+            source(kind, s), piece(whole(kind, s), kind, (z, x, y, c)), own_sem.at[3 + s % 2]
+        )
+
+    def level_copy(kind, s, k):
+        return remote(
+            source(kind, s),
+            piece(whole(kind, s), kind, (z, x, y, c)),
+            level_send.at[s % 4, k - 1],
+            level_recv.at[s, k - 1],
+            levels[k - 1],
+        )
+
+    def one_copy(kind, s):
+        part = piece(whole(kind, s), kind, (every, x, y, c))
+        return remote(part, part, one_send.at[s % 4], one_recv.at[s], to_one)
+
+    def two_copy(kind, s, first):
+        at = (every, every, y, c) if first == 0 else (every, x, every, c)
+        part = piece(whole(kind, s), kind, at)
+        return remote(part, part, two_send.at[s % 4], two_recv.at[s], to_two)
+
+    def core_copy(kind, s):
+        part = piece(whole(kind, s), kind, (every, every, every, c))
+        return remote(part, part, core_send.at[s % 4], core_recv.at[s], to_core)
+
+    def stage_level(kind, s):
+        own_copy(kind, s).start()
+        for k in range(1, 4):
+            level_copy(kind, s, k).start()
+
+    def stage_one(kind, s):
+        own_copy(kind, s).wait()
+        for k in range(1, 4):
+            level_copy(kind, s, k).wait_recv()
+        one_copy(kind, s).start()
+
+    def stage_two(kind, s):
+        one_copy(kind, s).wait_recv()
+        for first in range(2):
+
+            @pl.when(c == first)
+            def _():
+                two_copy(kind, s, first).start()
+
+    def stage_core(kind, s):
+        two_copy(kind, s, 0).wait_recv()
+        core_copy(kind, s).start()
+
+    def stage_last(kind, s):
+        core_copy(kind, s).wait_recv()
+
+    def stage_sent(kind, s):
+        for k in range(1, 4):
+            level_copy(kind, s, k).wait_send()
+        one_copy(kind, s).wait_send()
+        two_copy(kind, s, 0).wait_send()
+        core_copy(kind, s).wait_send()
+
+    stages = (
+        (stage_sent, 4),
+        (stage_level, 0),
+        (stage_one, 1),
+        (stage_two, 2),
+        (stage_core, 3),
+        (stage_last, 4),
+    )
+
+    lats = patches.shape[0] // PATCHES
+    shared_at = 1 + n_down + SHARED + 4
+    low, full = jnp.bfloat16, jnp.float32
+
+    def matrix(number, begin, end):
+        chunk = mats_out[number // 2, number % 2]
+        return chunk.reshape(D, chunk.shape[-1])[:, begin:end]
+
+    def bias_rows():
+        return jnp.sum(bias_out[...].astype(full).reshape(-1, 16, D), 0)
+
+    def wide_row(rows, begin, end):
+        return jnp.concatenate([rows[k : k + 1] for k in range(begin, end)], 1)
+
+    def conditions():
+        rows = bias_rows()
+        pre_time = contract(freq_low[...], matrix(3, 1408, 1664), 1, 1) + rows[11:12]
+        hid_time = jax.nn.silu(pre_time).astype(low)
+        cond = (
+            product(hid_time, matrix(3, 1024, 1408))
+            + rows[12:13]
+            + contract(label_hot[...], matrix(3, 0, 1024), 1, 1)
+        )
+        act = jax.nn.silu(cond).astype(low)
+        time_out[...] = pre_time
+        cond_out[...] = cond
+        mods_out[:, : 4 * D] = product(act, matrix(1, 0, 4 * D)) + wide_row(rows, 4, 8)
+        mods_out[:, 4 * D :] = product(act, matrix(2, 0, 2 * D)) + wide_row(rows, 8, 10)
+        fin_out[...] = product(act, matrix(2, 2 * D, 4 * D)) + wide_row(rows, 13, 15)
+
+    def mod_row(start, number):
+        return mods_out[pl.ds(start // PATCHES, 1), number * D : (number + 1) * D]
+
+    def attention_in(start):
+        rows = bias_rows()
+        span = pl.ds(start, PATCHES)
+        emb = contract(patches[span, :], matrix(2, 4 * D, 4 * D + 128), 1, 1)
+        emb = emb + rows[10:11] + places[...]
+        embedded[...] = emb
+        normed, unused_std = layer_norm(emb)
+        attn_in = (normed * (1.0 + mod_row(start, 1)) + mod_row(start, 0)).astype(low)
+        qkv_out[span, :] = (
+            product(attn_in, matrix(0, 0, 3 * D)) + wide_row(rows, 0, 3)
+        ).astype(low)
+
+    def attention_heads(start):
+        span = pl.ds(start, PATCHES)
+        lane = lax.broadcasted_iota(jnp.int32, (PATCHES, 2 * HD), 1)
+        for pair in range(HEADS // 2):
+            at = pair * 2 * HD
+            queries = qkv_out[span, at : at + 2 * HD]
+            keys = qkv_out[span, D + at : D + at + 2 * HD]
+            values = qkv_out[span, 2 * D + at : 2 * D + at + 2 * HD]
+            halves = []
+            for half in range(2):
+                mine = (lane < HD) if half == 0 else (lane >= HD)
+                scores = contract(jnp.where(mine, queries, 0), keys, 1, 1) * HD ** (-0.5)
+                powers = jnp.exp(scores - jnp.max(scores, 1, keepdims=True))
+                probs = (powers / jnp.sum(powers, 1, keepdims=True)).astype(low)
+                halves.append(product(probs, values))
+            att_out[span, at : at + 2 * HD] = jnp.where(lane < HD, halves[0], halves[1]).astype(low)
+
+    def attention_out(start):
+        rows = bias_rows()
+        span = pl.ds(start, PATCHES)
+        attn = product(att_out[span, :], matrix(0, 3 * D, 4 * D)) + rows[3:4]
+        middle = embedded[...] + mod_row(start, 2) * attn
+        middle_out[span, :] = middle
+        normed, unused_std = layer_norm(middle)
+        moe_in = (normed * (1.0 + mod_row(start, 4)) + mod_row(start, 3)).astype(low)
+        moe_out[span, :] = moe_in
+        logits_out[span, :] = product(moe_in, matrix(0, 4 * D, 4 * D + 128))
+
+    def fetch(shared_id):
+        e = EXPERTS + shared_id
+        first = pltpu.make_async_copy(down_out.at[e], down_here, here_sem.at[0])
+        second = pltpu.make_async_copy(up_out.at[e], up_here, here_sem.at[1])
+        first.start()
+        second.start()
+        first.wait()
+        second.wait()
+
+    def shared_block(shared_id, start):
+        span = pl.ds(start, PATCHES)
+        rows = moe_out[span, :]
+        chunks = [up_here[n // 2, n % 2].reshape(D, D) for n in range(NARROW_PIECES)]
+        down = down_here[...].reshape(FF, D)
+        total = None
+        for cut in range(0, FF, CUT):
+            pre_act = product(rows, up_columns(chunks, cut))
+            part = product(gelu_only(pre_act).astype(low), down[cut : cut + CUT])
+            total = part if total is None else total + part
+        if shared_id == 0:
+            shared_out[span, :] = total
+        else:
+            shared_out[span, :] += total
+
+    def tick(t, unused):
+        @pl.when(t == 1)
+        def _():
+            for k in range(1, 4):
+                bias_level(k).wait_recv()
+            bias_x().start()
+
+        @pl.when(t == 2)
+        def _():
+            bias_x().wait_recv()
+            bias_y().start()
+
+        @pl.when(t == 3)
+        def _():
+            bias_y().wait_recv()
+            bias_core().start()
+
+        @pl.when(t == 6)
+        def _():
+            own_up.wait()
+            for k in range(1, 4):
+                near_up(k).wait_recv()
+            for n in range(NARROW_PIECES):
+                up_wide[n] = up_got[n].astype(jnp.float32)
+
+            for e in range(n_up):
+                up_own[e] = jnp.concatenate(
+                    [up_wide[n, e * ROWS : (e + 1) * ROWS] for n in range(NARROW_PIECES)], 0
+                ).astype(jnp.bfloat16)
+
+        for stage, lag in stages:
+            s = t - lag
+
+            @pl.when(s == 0)
+            def _():
+                stage(0, 0)
+
+            @pl.when((s >= 1) & (s < 1 + n_down))
+            def _():
+                stage(1, jnp.clip(s, 1, n_down))
+
+            @pl.when((s >= 1 + n_down) & (s < slabs))
+            def _():
+                stage(2, jnp.clip(s, 1 + n_down, slabs - 1))
+
+        @pl.when(t == 5)
+        def _():
+            bias_core().wait_recv()
+            conditions()
+
+        for number, unit in enumerate((attention_in, attention_heads, attention_out)):
+
+            @pl.when((t >= 6) & (t < 6 + 3 * lats) & ((t - 6) % 3 == number))
+            def _():
+                unit(pl.multiple_of(jnp.clip((t - 6) // 3, 0, lats - 1) * PATCHES, PATCHES))
+
+        for shared_id in range(SHARED):
+            begin = shared_at + shared_id * lats
+
+            @pl.when(t == begin)
+            def _():
+                fetch(shared_id)
+
+            @pl.when((t >= begin) & (t < begin + lats))
+            def _():
+                shared_block(
+                    shared_id, pl.multiple_of(jnp.clip(t - begin, 0, lats - 1) * PATCHES, PATCHES)
+                )
+
+        return unused
+
+    lax.fori_loop(0, slabs + 4, tick, 0)
+    for k in range(1, 4):
+        near_mats(k).wait_send()
+        near_up(k).wait_send()
+        bias_level(k).wait_send()
+    bias_x().wait_send()
+    bias_y().wait_send()
+    bias_core().wait_send()
+
+
+def gather_weights(
+    mats, up_weights, down_weights, biases, patches, places, freq_low, label_hot
+):
+    low = jnp.bfloat16
+    owner = lax.axis_index(AXES)
+    m = mats.astype(low)
+    rows = m.shape[0]
+
+    thin = 13 * D
+
+    def thin_part(at):
+        return jnp.pad(m[:, at : at + 16], ((0, 0), (0, 112)))
+
+    mats_in = jnp.stack(
+        [
+            jnp.concatenate([m[:, : 4 * D], thin_part(thin)], 1),
+            jnp.concatenate([m[:, 4 * D : 8 * D], thin_part(thin + 16)], 1),
+            jnp.concatenate(
+                [m[:, 8 * D : 10 * D], m[:, 11 * D : 13 * D], thin_part(thin + 32)], 1
+            ),
+            jnp.concatenate(
+                [
+                    m[:, thin + 48 + FREQ :],
+                    jnp.zeros((rows, 24), low),
+                    m[:, 10 * D : 11 * D],
+                    m[:, thin + 48 : thin + 48 + FREQ],
+                ],
+                1,
+            ),
+        ],
+        0,
+    )
+    mats_in = jnp.pad(mats_in, ((0, 0), (0, 16 - rows), (0, 0)))
+    line = lax.dynamic_update_slice(
+        jnp.zeros((16 * D,), low), biases.astype(low), (owner * biases.shape[0],)
+    )
+    n_up = up_weights.shape[0]
+    up_in = (
+        up_weights.astype(low)
+        .reshape(n_up, rows, NARROW_PIECES, D)
+        .transpose(2, 0, 1, 3)
+        .reshape(NARROW_PIECES, n_up * rows, D)
+    )
+    room = (n_up * rows + 15) // 16 * 16
+    up_in = jnp.pad(up_in, ((0, 0), (0, room - n_up * rows), (0, 0)))
+    slabs = 1 + 2 * n_up
+    spread = mats_in.shape[2]
+    dma = pltpu.SemaphoreType.DMA
+    anywhere = pl.BlockSpec(memory_space=pl.ANY)
+    tokens = patches.shape[0]
+    full, vmem = jnp.float32, pl.BlockSpec(memory_space=pltpu.VMEM)
+    outs = pl.pallas_call(
+        gather_kernel,
+        out_shape=[
+            jax.ShapeDtypeStruct((2, 2, 4, 2, 3, 16, spread), low),
+            jax.ShapeDtypeStruct((4, 2, 2, 2, 16, D), low),
+            jax.ShapeDtypeStruct((n_up, 4, 2, 2, 2, PIECE, D), low),
+            jax.ShapeDtypeStruct((n_up, 2, 2, 4, 2, PIECE, D), low),
+            jax.ShapeDtypeStruct((8, 6 * D), full),
+            jax.ShapeDtypeStruct((8, 2 * D), full),
+            jax.ShapeDtypeStruct((8, D), full),
+            jax.ShapeDtypeStruct((8, D), full),
+            jax.ShapeDtypeStruct((tokens, 3 * D), low),
+            jax.ShapeDtypeStruct((tokens, D), low),
+            jax.ShapeDtypeStruct((tokens, D), full),
+            jax.ShapeDtypeStruct((tokens, D), low),
+            jax.ShapeDtypeStruct((tokens, 128), full),
+            jax.ShapeDtypeStruct((tokens, D), full),
+        ],
+        in_specs=[anywhere] * 4 + [vmem] * 4,
+        out_specs=[vmem] * 2 + [anywhere] * 2 + [vmem] * 10,
+        scratch_shapes=[
+            pltpu.VMEM((NARROW_PIECES, 16, spread), low),
+            pltpu.VMEM((PIECE, spread), jnp.float32),
+            pltpu.VMEM((NARROW_PIECES, room, D), low),
+            pltpu.VMEM((NARROW_PIECES, room, D), jnp.float32),
+            pltpu.VMEM((n_up, PIECE, D), low),
+            pltpu.VMEM((PATCHES, D), full),
+            pltpu.VMEM((4, 2, 2, 2, PIECE, D), low),
+            pltpu.VMEM((2, 2, 4, 2, PIECE, D), low),
+            dma((2, 4)),
+            dma((2, 4)),
+            dma((5,)),
+            dma((4, 3)),
+            dma((slabs, 3)),
+            dma((4,)),
+            dma((slabs,)),
+            dma((4,)),
+            dma((slabs,)),
+            dma((4,)),
+            dma((slabs,)),
+            dma((6,)),
+            dma((6,)),
+            dma((2,)),
+        ],
+        compiler_params=pltpu.CompilerParams(
+            collective_id=2, has_side_effects=True, vmem_limit_bytes=VMEM_ROOM
+        ),
+        name="gather_weights",
+    )(
+        mats_in,
+        line.reshape(16, D),
+        down_weights.astype(low),
+        up_in,
+        patches,
+        places,
+        freq_low,
+        label_hot,
+    )
+    return outs
+
+
 def split_weights(weights):
     mats_full, up_full, down_full, bias_full = weights
     matrices = cut_pieces(mats_full, column_widths(), 1)
     vectors = [member.astype(jnp.float32) for member in cut_pieces(bias_full, bias_widths(), 0)]
+    up_full = up_full.reshape(-1, D, NARROW_PIECES, D).transpose(0, 2, 1, 3)
     return (matrices, vectors, up_full, down_full)
 
 
 def forward(weights, latents, noise, timesteps, labels, routes):
-    matrices, vectors, up_full, down_full = split_weights(weights)
+    matrices, vectors, up_full, down_full = weights
     w_qkv, w_proj, w_mod, w_time2, w_final, w_router, w_head, w_patch, w_time1, w_table = matrices
     b_qkv, b_proj, b_mod, b_patch, b_time1, b_time2, b_final = vectors
     num_latents = latents.shape[0]
@@ -1288,7 +1791,7 @@
         .reshape(num_latents, PATCHES, 3, HEADS, HD)
     )
     scores = jnp.einsum(
-        "lqhd,lkhd->lhqk", qkv_out[:, :, 0], qkv_out[:, :, 1], preferred_element_type=jnp.float32
+        LQK, qkv_out[:, :, 0], qkv_out[:, :, 1], preferred_element_type=jnp.float32
     ) * HD ** (-0.5)
     log_totals = jax.nn.logsumexp(scores, -1)
     probs_low = jax.nn.softmax(scores, -1).astype(jnp.bfloat16)
@@ -1309,8 +1812,13 @@
     )
     gate_vals = jax.nn.softmax(jnp.sum(route_hot * logits[:, None, :], 2), -1)
     slot_of, slot_meta = pack_slots(routes)
-    routed, shared_out = experts_forward(slot_of, slot_meta, moe_in, up_full, down_full)
-    moe_out = gate_vals[:, 0:1] * routed[0] + gate_vals[:, 1:2] * routed[1] + shared_out
+    routed = experts_forward(slot_of, slot_meta, moe_in, up_full, down_full)
+    moe_out = gate_vals[:, 0:1] * routed[0] + gate_vals[:, 1:2] * routed[1]
+    for shared_id in range(EXPERTS, EXPERTS + SHARED):
+        for cut in range(0, FF, CUT):
+            pre_act = product(moe_in, up_columns(up_full[shared_id], cut))
+            activated = gelu_only(pre_act).astype(jnp.bfloat16)
+            moe_out = moe_out + product(activated, down_full[shared_id, cut : cut + CUT])
     moe_out = moe_out.reshape(num_latents, PATCHES, D)
     final_state = middle + gate_moe * moe_out
     normed_fin, inv_fin = layer_norm(final_state)
@@ -1354,8 +1862,123 @@
     )
 
 
+def forward_fused(mats, up_weights, down_weights, biases, latents, noise, timesteps, labels, routes):
+    num_latents = latents.shape[0]
+    rows_here = num_latents * PATCHES
+    steps_f = timesteps.astype(jnp.float32)
+    signal, spread = noise_level(steps_f)
+    noisy = signal[:, None] * latents + spread[:, None] * noise
+    patches = noisy.reshape(rows_here, PD).astype(jnp.bfloat16)
+    freq_low = time_features(steps_f).astype(jnp.bfloat16)
+    label_low = (labels[:, None] == jnp.arange(1024, dtype=jnp.int32)[None, :]).astype(jnp.bfloat16)
+    less = ((0, 8 - num_latents), (0, 0))
+    outs = gather_weights(
+        mats,
+        up_weights,
+        down_weights,
+        biases,
+        jnp.pad(patches, ((0, 0), (0, 128 - PD))),
+        positions(),
+        jnp.pad(freq_low, less),
+        jnp.pad(label_low, less),
+    )
+    mats_full, bias_full, down_full, up_full = outs[:4]
+    modulation, final_mod, pre_time, cond = [member[:num_latents] for member in outs[4:8]]
+    qkv_out, attended, middle, moe_in, logits, shared_out = outs[8:]
+    logits = logits[:, :EXPERTS]
+    n_up = up_full.shape[0]
+    full = mats_full.reshape(NARROW_PIECES, D, -1)
+    matrices = [
+        full[0][:, : 3 * D],
+        full[0][:, 3 * D : 4 * D],
+        jnp.concatenate([full[1][:, : 4 * D], full[2][:, : 2 * D]], 1),
+        full[3][:, 1024 : 1024 + D],
+        full[2][:, 2 * D : 4 * D],
+        full[0][:, 4 * D : 4 * D + 16],
+        full[1][:, 4 * D : 4 * D + 16],
+        full[2][:, 4 * D : 4 * D + 16],
+        full[3][:, 1024 + D :],
+        full[3][:, :CLASSES],
+    ]
+    line = jnp.sum(bias_full.reshape(-1, 16, D).astype(jnp.float32), 0).reshape(-1)[: 15 * D]
+    vectors = cut_pieces(line, bias_widths(), 0)
+    up_full = up_full.reshape(n_up, NARROW_PIECES, D, D)
+    down_full = down_full.reshape(n_up, FF, D)
+    weights = (matrices, vectors, up_full, down_full)
+    w_qkv, w_proj, w_mod, w_time2, w_final, w_router, w_head, w_patch, w_time1, w_table = matrices
+    b_qkv, b_proj, b_mod, b_patch, b_time1, b_time2, b_final = vectors
+    shift_attn, scale_attn, gate_attn, shift_moe, scale_moe, gate_moe = [
+        member[:, None, :] for member in jnp.split(modulation, 6, 1)
+    ]
+    shift_fin, scale_fin = [member[:, None, :] for member in jnp.split(final_mod, 2, 1)]
+    embedded = (
+        contract(patches, w_patch, 1, 1).reshape(num_latents, PATCHES, D)
+        + b_patch
+        + positions()[None]
+    )
+    normed_one, inv_one = layer_norm(embedded)
+    attn_in = (
+        (normed_one * (1.0 + scale_attn) + shift_attn).astype(jnp.bfloat16).reshape(rows_here, D)
+    )
+    qkv_out = qkv_out.reshape(num_latents, PATCHES, 3, HEADS, HD)
+    scores = jnp.einsum(
+        LQK, qkv_out[:, :, 0], qkv_out[:, :, 1], preferred_element_type=jnp.float32
+    ) * HD ** (-0.5)
+    attn_out = (product(attended, w_proj) + b_proj).reshape(num_latents, PATCHES, D)
+    middle = middle.reshape(num_latents, PATCHES, D)
+    normed_two, inv_two = layer_norm(middle)
+    route_hot = (routes[:, :, None] == jnp.arange(EXPERTS, dtype=jnp.int32)[None, None, :]).astype(
+        jnp.float32
+    )
+    gate_vals = jax.nn.softmax(jnp.sum(route_hot * logits[:, None, :], 2), -1)
+    slot_of, slot_meta = pack_slots(routes)
+    routed = experts_forward(slot_of, slot_meta, moe_in, up_full, down_full)
+    moe_out = gate_vals[:, 0:1] * routed[0] + gate_vals[:, 1:2] * routed[1] + shared_out
+    moe_out = moe_out.reshape(num_latents, PATCHES, D)
+    final_state = middle + gate_moe * moe_out
+    normed_fin, inv_fin = layer_norm(final_state)
+    head_in = (
+        (normed_fin * (1.0 + scale_fin) + shift_fin).astype(jnp.bfloat16).reshape(rows_here, D)
+    )
+    errors = product(head_in, w_head) - noise.reshape(rows_here, PD)
+    kept = SimpleNamespace(
+        patches=patches,
+        freq_low=freq_low,
+        pre_time=pre_time,
+        hid_time=jax.nn.silu(pre_time).astype(jnp.bfloat16),
+        cond=cond,
+        cond_act=jax.nn.silu(cond).astype(jnp.bfloat16),
+        scale_attn=scale_attn,
+        gate_attn=gate_attn,
+        scale_moe=scale_moe,
+        gate_moe=gate_moe,
+        scale_fin=scale_fin,
+        normed_one=normed_one,
+        inv_one=inv_one,
+        attn_in=attn_in,
+        qkv_out=qkv_out,
+        log_totals=jax.nn.logsumexp(scores, -1),
+        attended=attended,
+        attn_out=attn_out,
+        normed_two=normed_two,
+        inv_two=inv_two,
+        moe_in=moe_in,
+        route_hot=route_hot,
+        gate_vals=gate_vals,
+        slot_of=slot_of,
+        slot_meta=slot_meta,
+        routed=routed,
+        moe_out=moe_out,
+        normed_fin=normed_fin,
+        inv_fin=inv_fin,
+        head_in=head_in,
+        errors=errors,
+    )
+    return weights, kept
+
+
 def backward(weights, kept, total_tokens):
-    matrices, vectors, up_full, down_full = split_weights(weights)
+    matrices, vectors, up_full, down_full = weights
     w_qkv, w_proj, w_mod, w_time2, w_final, w_router, w_head, w_patch, w_time1, w_table = matrices
     num_latents = kept.normed_one.shape[0]
     rows_here = num_latents * PATCHES
@@ -1399,7 +2022,7 @@
     key_rows = qkv_out[:, :, 1]
     values = qkv_out[:, :, 2]
     scores = jnp.einsum(
-        "lqhd,lkhd->lhqk", queries, key_rows, preferred_element_type=jnp.float32
+        LQK, queries, key_rows, preferred_element_type=jnp.float32
     ) * HD ** (-0.5)
     probs = jnp.exp(scores - kept.log_totals[..., None])
     probs_low = probs.astype(jnp.bfloat16)
@@ -1407,7 +2030,7 @@
         "lhqk,lqhd->lkhd", probs_low, grad_att_low, preferred_element_type=jnp.float32
     )
     grad_probs = jnp.einsum(
-        "lqhd,lkhd->lhqk", grad_att_low, values, preferred_element_type=jnp.float32
+        LQK, grad_att_low, values, preferred_element_type=jnp.float32
     )
     grad_scores = (
         probs * (grad_probs - jnp.sum(probs * grad_probs, -1, keepdims=True)) * HD ** (-0.5)
@@ -1631,22 +2254,29 @@
     *factors,
 ):
     rows_here = mats.shape[0]
-    flat = jnp.concatenate([mats.reshape(-1), biases], 0).astype(jnp.bfloat16)
-    flat = lax.all_gather(flat, AXES, axis=0, tiled=False)
-    gathered = (
-        flat[:, : rows_here * mats.shape[1]].reshape(-1, mats.shape[1]),
-        lax.all_gather(up_weights.astype(jnp.bfloat16), AXES, axis=1, tiled=True),
-        lax.all_gather(down_weights.astype(jnp.bfloat16), AXES, axis=1, tiled=True),
-        flat[:, rows_here * mats.shape[1] :].reshape(-1),
-    )
-    kept = forward(gathered, latents, noise, timesteps, labels, routes)
+    kernel_fits = lax.axis_size(WIDE) == WIDE_PIECES and lax.axis_size(NARROW) == NARROW_PIECES
+    if kernel_fits:
+        gathered, kept = forward_fused(
+            mats, up_weights, down_weights, biases, latents, noise, timesteps, labels, routes
+        )
+    else:
+        flat = jnp.concatenate([mats.reshape(-1), biases], 0).astype(jnp.bfloat16)
+        flat = lax.all_gather(flat, AXES, axis=0, tiled=False)
+        gathered = split_weights(
+            (
+                flat[:, : rows_here * mats.shape[1]].reshape(-1, mats.shape[1]),
+                lax.all_gather(up_weights.astype(jnp.bfloat16), AXES, axis=1, tiled=True),
+                lax.all_gather(down_weights.astype(jnp.bfloat16), AXES, axis=1, tiled=True),
+                flat[:, rows_here * mats.shape[1] :].reshape(-1),
+            )
+        )
+        kept = forward(gathered, latents, noise, timesteps, labels, routes)
     total_tokens = latents.shape[0] * PATCHES * lax.axis_size(AXES)
     up_slabs, down_slabs, mats_slabs, thin, grad_bias, lows, grad_cond = backward(
         gathered, kept, total_tokens
     )
     loss_part = jnp.sum(kept.errors * kept.errors)
     masters = (mats, up_weights, down_weights, biases)
-    kernel_fits = lax.axis_size(WIDE) == WIDE_PIECES and lax.axis_size(NARROW) == NARROW_PIECES
     if kernel_fits:
         sums, rows, lat = reduce_slabs(
             down_slabs,

time: 1010 us -> 880 us (0.87)
  waiting for transfers between devices: 303 us -> 0 us
  Pallas kernels: 475 us -> 693 us
  local copies, waits for them, and re-layouts: 108 us -> 78.3 us
  between operations: 16.9 us -> 4.6 us
  matrix products: 67.2 us -> 55.8 us
    all_gather x3 -> x0, waiting for transfers between devices: 303 us -> none  [the longest x1 115 us: body(): lax.all_gather(up_weights.astype(jnp.bfloat16), AXES, axis=1, tiled=True)]
    pallas_call x0 -> x1, Pallas kernels: none -> 254 us  [gather_weights(): pl.pallas_call(gather_kernel, out_shape=[jax.ShapeDtypeStruct((2, 2, 4, 2...]
    all_gather x1 -> x0, local copies, waits for them, and re-layouts: 24.2 us -> none  [body(): lax.all_gather(up_weights.astype(jnp.bfloat16), AXES, axis=1, tiled=True)]
    pallas_call x1, Pallas kernels: 60.8 us -> 41.6 us  [experts_forward(): pl.pallas_call(forward_kernel, grid_spec=pltpu.PrefetchScalarGridSpec(num...]
    pallas_call x1, Pallas kernels: 126 us -> 110 us  [experts_backward(): pl.pallas_call(backward_kernel, grid_spec=pltpu.PrefetchScalarGridSpec(nu...]
    unnamed x175 -> x223, local copies, waits for them, and re-layouts: 38.6 us -> 29.6 us
  transfers between devices with their start and end apart: 3 -> 0, of which waited for: 3 -> 0; matrix products, arithmetic and copies ran while one was open for 9% -> 0% of each run, Pallas kernels for 0% -> 0%
where the time goes in v1:
time: 880 us; the launch traced here: 870 us
  Pallas kernels  693 us (79%)
  local copies, waits for them, and re-layouts  78.3 us (9%)
  matrix products  55.8 us (6%)
  other arithmetic  38.4 us (4%)
    pallas_call x1, Pallas kernels, gather_weights(): pl.pallas_call(gather_kernel, out_shape=[jax.ShapeDtypeStruct((2, 2, 4, 2...  254 us
    pallas_call x1, Pallas kernels, reduce_slabs(): pl.pallas_call(reduce_kernel, out_shape=[jax.ShapeDtypeStruct((direct, PI...  234 us
    pallas_call x1, Pallas kernels, experts_backward(): pl.pallas_call(backward_kernel, grid_spec=pltpu.PrefetchScalarGridSpec(nu...  110 us
    pallas_call x1, Pallas kernels, update_kernel_call(): pl.pallas_call(update_kernel, out_shape=[jax.ShapeDtypeStruct((1, 1), ful...  54 us
    pallas_call x1, Pallas kernels, experts_forward(): pl.pallas_call(forward_kernel, grid_spec=pltpu.PrefetchScalarGridSpec(num...  41.6 us
    unnamed x223, local copies, waits for them, and re-layouts  29.6 us

profile of v1, /device:TPU:0, one launch (start us, length us, event | category | flops | bytes accessed | tf_op | source)
XLA Modules:
  0.0 870.2 jit_solution(12375643136445444656)
XLA Ops:
  12.9 253.7 %gather_weights.1 = (bf16[2,2,4,2,3,16,1664]{6,5,4,3,2,1,0:T(8,128)(2,1)}, bf16[4,2,2,2,16,384]{5,4,3,2,1,0:T(8,128)(2,1)}, bf16[18,4,2,2,2,48,384]{6,5,4,3,2,1,...) custom-call(bf16[4,16,1664]{2,1,0:T(8,128)(2,1)} %fusion.67.mats_in,, ...), custom_call_target="tpu_custom_call" | custom-call | tf_op jit(solution)/shard_map/gather_weights/pallas_call | solution.py:1679
  266.7 41.6 %experts_forward.1 = f32[2,1024,384]{2,1,0:T(8,128)} custom-call(s32[2,16]{1,0:T(2,128)} %pad_add_fusion.1.meta, s32[2,1024]{1,0:T(2,128)} %pad_add_fusion.slot_at.slots_ref, s32[2,1024]{1,0:T(2,128)} %pad_add_fusion.slot_at.slots_ref, bf16[1024,384]{1,0:T(8,128)(2,1)} %get-tuple-element.60.x_ref, bf16[18,4,384,384]{3,2,1,0:T(8,128)(2,1)} %bitcast.257, ...), custom_call_target="tpu_custom_call" | custom-call | flops 20000000000 | bytes 50000000 | tf_op jit(solution)/shard_map/experts_forward/pallas_call | solution.py:222
  308.2 1.4 fusion.132
  310.2 4.0 fusion.126
  314.6 2.5 slice_bitcast_fusion.2
  319.7 2.0 multiply_reduce_fusion.14
  321.7 2.0 fusion.45
  323.8 1.4 multiply_reduce_fusion.10
  325.2 1.4 fusion.46
  326.6 1.3 pad_maximum_fusion.1.pair_ref
  327.9 109.6 %experts_backward.1 = (bf16[18,8,4,48,384]{4,3,2,1,0:T(8,128)(2,1)}, bf16[18,8,4,48,384]{4,3,2,1,0:T(8,128)(2,1)}, f32[1024,384]{1,0:T(8,128)}) custom-call(s32[2,16]{1,0:T(2,128)} %pad_add_fusion.1.meta, s32[2,1024]{1,0:T(2,128)} %pad_add_fusion.slot_at.slots_ref, s32[2,1024]{1,0:T(2,128)} %pad_add_fusion.slot_at.slots_ref, ...), custom_call_target="tpu_custom_call" | custom-call | flops 44999999488 | bytes 90000000 | tf_op jit(solution)/shard_map/experts_backward/pallas_call | solution.py:342
  437.5 4.3 copy.94
  441.8 16.4 %reshape.563 = bf16[4,256,3,6,64]{1,0,4,3,2:T(4,128)(2,1)} reshape(bf16[1024,1152]{0,1:T(8,128)(2,1)} %copy.94) | data formatting | bytes 4718592 | tf_op jit(solution)/shard_map/reshape | solution.py:1923
  458.2 3.3 fusion.128
  463.7 1.6 copy-done
  465.5 2.1 fusion.44
  469.6 1.6 convolution_convert_fusion.1
  471.6 1.4 reshape.564
  473.0 4.4 fusion.35
  477.4 3.7 fusion.50
  481.1 12.7 %fusion.41 = f32[4,256,1,6,64]{1,4,3,0,2:T(8,128)} fusion(f32[4,6,256,256]{2,3,1,0:T(8,128)} %fusion.50, f32[4,6,256,256]{2,3,1,0:T(8,128)} %copy-done, f32[4,6,256]{2,1,0:T(8,128)S(1)} %log_add_fusion, bf16[4,256,1,6,64]{1,0,4,3,2:T(4,128)(2,1)} %copy-done.26), kind=kOutput, calls=%fused_computation.69 | convolution fusion | flops 215488768 | bytes 14966784 | tf_op jit(solution)/shard_map/lhqk,lqhd->lkhd/dot_general | solution.py:2041
  493.8 12.6 %fusion.38 = f32[4,256,1,6,64]{1,4,3,0,2:T(8,128)} fusion(f32[4,6,256,256]{2,3,1,0:T(8,128)} %fusion.50, f32[4,6,256,256]{2,3,1,0:T(8,128)} %copy-done, f32[4,6,256]{2,1,0:T(8,128)S(1)} %log_add_fusion, bf16[4,256,1,6,64]{1,0,4,3,2:T(4,128)(2,1)} %copy-done.25), kind=kOutput, calls=%fused_computation.68 | convolution fusion | flops 215488768 | bytes 14966784 | tf_op jit(solution)/shard_map/lhqk,lkhd->lqhd/dot_general | solution.py:2038
  506.4 2.2 fusion.12
  511.4 1.7 convert_element_type.219
  513.1 2.7 copy.125
  515.9 1.6 fusion.137
  518.6 1.2 copy-done.6
  520.6 3.3 multiply_reduce_fusion.5
  524.2 5.7 fusion.124
  529.8 1.7 multiply_reduce_fusion.3
  531.6 1.4 fusion.33
  533.5 1.6 reduce_sum.406
  535.3 1.3 slice.202
  537.6 1.4 fusion.92
  541.9 1.3 convolution_convert_fusion.4
  543.6 1.5 pad_maximum_fusion.2.thin_ref
  546.1 2.0 copy.109
  549.3 1.2 convolution_convert_fusion
  553.2 234.3 %reduce_slabs.1 = (f32[19,48,384]{2,1,0:T(8,128)}, f32[19,4,12,384]{3,2,1,0:T(8,128)}, bf16[4,2,2,2,16,1536]{5,4,3,2,1,0:T(8,128)(2,1)}) custom-call(bf16[18,16,2,48,384]{4,3,2,1,0:T(8,128)(2,1)} %bitcast.209, bf16[1,16,2,48,384]{4,3,2,1,0:T(8,128)(2,1)} %pad_maximum_fusion.2.thin_ref, bf16[18,16,2,48,384]{4,3,2,1,0:T(8,128)(2,1)} %bitcast.208, ...), custom_call_target="tpu_custom_call" | custom-call | tf_op jit(solution)/shard_map/reduce_slabs/pallas_call | solution.py:713
  790.7 54.0 %update.1 = (f32[1,1]{1,0:T(1,128)}, f32[12,6296]{1,0:T(8,128)}, f32[12,6296]{1,0:T(8,128)}, bf16[12,6296]{1,0:T(8,128)(2,1)}, f32[12,10]{1,0:T(8,128)}, /*index...) custom-call(f32[19,48,384]{2,1,0:T(8,128)} %get-tuple-element.77.sum, ...), custom_call_target="tpu_custom_call" | custom-call | tf_op jit(solution)/shard_map/update/pallas_call | solution.py:1180
  845.5 1.4 copy.118
  846.9 1.4 reduce.13
  848.3 1.7 copy.117
  850.0 1.8 reduce.14
  853.0 1.8 copy.174
  854.8 1.8 copy.175
  857.3 1.2 copy.177
  859.4 1.2 copy.178
  (340 shorter events, 48.5 us)
Async XLA Ops:
  2.3 3.0 copy-start.20
  3.6 2.7 copy-start.15
  6.8 5.4 copy-start.89
  7.9 258.7 %copy-start.44 = (bf16[4,4096]{1,0:T(4,128)(2,1)}, bf16[4,4096]{1,0:T(4,128)(2,1)S(1)}, u32[]{:S(2)}) copy-start(bf16[4,4096]{1,0:T(4,128)(2,1)S(1)} %add_convert_fusion.1) | copy-start | bytes 98308
  8.1 258.4 %copy-start.28 = (bf16[1024,16]{1,0:T(8,128)(2,1)}, bf16[1024,16]{1,0:T(8,128)(2,1)S(1)}, u32[]{:S(2)}) copy-start(bf16[1024,16]{1,0:T(8,128)(2,1)S(1)} %convert_element_type.210) | copy-start | bytes 98308
  11.1 255.5 %copy-start.76 = (bf16[4,128]{1,0:T(4,128)(2,1)}, bf16[4,128]{1,0:T(4,128)(2,1)S(1)}, u32[]{:S(2)}) copy-start(bf16[4,128]{1,0:T(4,128)(2,1)S(1)} %get-tuple-element.231) | copy-start | bytes 3076
  266.6 43.0 %copy-start.80 = (f32[8,768]{1,0:T(8,128)S(1)}, f32[8,768]{1,0:T(8,128)}, u32[]{:S(2)}) copy-start(f32[8,768]{1,0:T(8,128)} %get-tuple-element.67) | copy-start | bytes 73732
  266.6 43.0 %copy-start.41 = (f32[1024,128]{1,0:T(8,128)S(1)}, f32[1024,128]{1,0:T(8,128)}, u32[]{:S(2)}) copy-start(f32[1024,128]{1,0:T(8,128)} %get-tuple-element.61) | copy-start | bytes 1572868
  266.6 43.1 %copy-start.56 = (s32[1024,2]{0,1:T(2,128)S(1)}, s32[1024,2]{0,1:T(2,128)}, u32[]{:S(2)}) copy-start(s32[1024,2]{0,1:T(2,128)} %param.20) | copy-start | bytes 24580
  266.6 43.3 %copy-start.1 = (f32[1024,384]{1,0:T(8,128)S(1)}, f32[1024,384]{1,0:T(8,128)}, u32[]{:S(2)}) copy-start(f32[1024,384]{1,0:T(8,128)} %get-tuple-element.63) | copy-start | bytes 4718596
  309.6 158.1 %copy-start.54 = (f32[4,384]{1,0:T(4,128)}, f32[4,384]{1,0:T(4,128)S(1)}, u32[]{:S(2)}) copy-start(f32[4,384]{1,0:T(4,128)S(1)} %get-tuple-element.210) | copy-start | bytes 18436
  310.1 4.5 slice-start
  310.2 157.5 %copy-start.52 = (f32[1024]{0:T(1024)}, f32[1024]{0:T(1024)S(1)}, u32[]{:S(2)}) copy-start(f32[1024]{0:T(1024)S(1)} %broadcast_multiply_fusion.5) | copy-start | bytes 12292
  310.2 4.4 slice-start.1
  314.2 9.6 %copy-start.47 = (f32[1024]{0:T(1024)}, f32[1024]{0:T(1024)S(1)}, u32[]{:S(2)}) copy-start(f32[1024]{0:T(1024)S(1)} %broadcast_multiply_fusion.8) | copy-start | bytes 12292
  314.6 9.2 %copy-start.50 = (f32[1024]{0:T(1024)}, f32[1024]{0:T(1024)S(1)}, u32[]{:S(2)}) copy-start(f32[1024]{0:T(1024)S(1)} %add_rsqrt_fusion.2) | copy-start | bytes 12292
  319.7 4.0 copy-start.13
  462.6 2.7 copy-start
  462.6 2.8 copy-start.34
  473.0 4.4 copy-start.16
  473.0 4.4 copy-start.27
  509.7 6.1 copy-start.21
  520.5 3.4 copy-start.68
  520.5 3.4 copy-start.53
  520.5 3.5 copy-start.66
  520.6 3.5 copy-start.59
  520.6 3.5 copy-start.63
  520.6 3.5 copy-start.48
  520.6 3.5 copy-start.61
  520.6 3.5 copy-start.51
  520.6 3.5 copy-start.3
  520.6 3.5 copy-start.55
  524.1 5.7 copy-start.84
  524.2 5.7 copy-start.91
  524.2 7.5 copy-start.11
  537.5 4.0 copy-start.22
  537.5 4.0 copy-start.29
  537.6 4.1 copy-start.14
  537.6 4.1 copy-start.40
  553.2 234.3 %copy-start.79 = (f32[10,12]{1,0:T(8,128)S(1)}, f32[10,12]{1,0:T(8,128)}, u32[]{:S(2)}) copy-start(f32[10,12]{1,0:T(8,128)} %param.25) | copy-start | bytes 1444
  553.2 235.0 %copy-start.69 = (f32[6296]{0:T(1024)S(1)}, f32[6296]{0:T(1024)}, u32[]{:S(2)}) copy-start(f32[6296]{0:T(1024)} %param.26) | copy-start | bytes 75556
  553.2 235.7 %copy-start.78 = (f32[18,12]{0,1:T(8,128)S(1)}, f32[18,12]{0,1:T(8,128)}, u32[]{:S(2)}) copy-start(f32[18,12]{0,1:T(8,128)} %param.27) | copy-start | bytes 2596
  553.2 236.5 %copy-start.73 = (f32[18,48]{1,0:T(8,128)S(1)}, f32[18,48]{1,0:T(8,128)}, u32[]{:S(2)}) copy-start(f32[18,48]{1,0:T(8,128)} %param.29) | copy-start | bytes 10372
  844.8 11.8 %copy-start.46 = (bf16[12,6296]{1,0:T(8,128)(2,1)S(1)}, bf16[12,6296]{1,0:T(8,128)(2,1)}, u32[]{:S(2)}) copy-start(bf16[12,6296]{1,0:T(8,128)(2,1)} %get-tuple-element.278) | copy-start | bytes 453316
  844.8 12.5 %copy-start.32 = (f32[18,12,1536]{2,1,0:T(8,128)S(1)}, f32[18,12,1536]{2,1,0:T(8,128)}, u32[]{:S(2)}) copy-start(f32[18,12,1536]{2,1,0:T(8,128)} %get-tuple-element.281) | copy-start | bytes 3981316
  864.0 2.9 copy-start.88
  864.0 3.5 copy-start.87
  864.0 4.0 copy-start.86
  (49 other events, 79.4 us)

commit v2 on v1

--- a/solution.py
+++ b/solution.py
@@ -248,7 +248,6 @@
     slots_ref,
     x_ref,
     pair_ref,
-    both_ref,
     up_ref,
     down_ref,
     up_out,
@@ -276,43 +275,22 @@
             total = part if total is None else total + part
         return total
 
-    @pl.when(stack_id < EXPERTS)
-    def _():
-        owner = jnp.minimum(stack_id, EXPERTS - 1)
-        start = meta[0, owner]
-        stop = start + meta[1, owner]
-
-        def block(number, unused):
-            base = pl.multiple_of(start + number * BLK, 8)
-            rows = product(slot_pick(slots_ref, base, BLK), x_ref[...]).astype(jnp.bfloat16)
-            place = base + lax.broadcasted_iota(jnp.int32, (BLK, tokens), 0)
-            place = jnp.where(place < stop, place, -1)
-            grads = None
-            for k in range(2):
-                part = product(
-                    (slots_ref[k : k + 1, :] == place).astype(jnp.bfloat16), pair_ref[k]
-                )
-                grads = part if grads is None else grads + part
-            dx_slots[pl.ds(base, BLK), :] = expert(rows, grads.astype(jnp.bfloat16))
-            return unused
-
-        lax.fori_loop(0, (meta[1, owner] + BLK - 1) // BLK, block, 0)
-
-    @pl.when(stack_id >= EXPERTS)
-    def _():
-        @pl.when(stack_id == EXPERTS)
-        def _():
-            dx_ref[...] = jnp.zeros_like(dx_ref)
-
-        def block(number, unused):
-            base = pl.multiple_of(number * BLK, BLK)
-            dx_ref[pl.ds(base, BLK), :] += expert(
-                x_ref[pl.ds(base, BLK), :], both_ref[pl.ds(base, BLK), :]
-            )
-            return unused
-
-        lax.fori_loop(0, tokens // BLK, block, 0)
-
+    start = meta[0, stack_id]
+    stop = start + meta[1, stack_id]
+
+    def block(number, unused):
+        base = pl.multiple_of(start + number * BLK, 8)
+        rows = product(slot_pick(slots_ref, base, BLK), x_ref[...]).astype(jnp.bfloat16)
+        place = base + lax.broadcasted_iota(jnp.int32, (BLK, tokens), 0)
+        place = jnp.where(place < stop, place, -1)
+        grads = None
+        for k in range(2):
+            part = product((slots_ref[k : k + 1, :] == place).astype(jnp.bfloat16), pair_ref[k])
+            grads = part if grads is None else grads + part
+        dx_slots[pl.ds(base, BLK), :] = expert(rows, grads.astype(jnp.bfloat16))
+        return unused
+
+    lax.fori_loop(0, (meta[1, stack_id] + BLK - 1) // BLK, block, 0)
     for n in range(NARROW_PIECES):
         up_out[0, :, n] = (
             up_sum[:, n * D : (n + 1) * D]
@@ -321,12 +299,12 @@
         )
     down_out[0] = down_sum[...].astype(jnp.bfloat16).reshape(WIDE_PIECES, NARROW_PIECES, PIECE, D)
 
-    @pl.when(stack_id == EXPERTS + SHARED - 1)
+    @pl.when(stack_id == EXPERTS - 1)
     def _():
         def group(number, unused):
             for step in range(8):
                 token = number * 8 + step
-                dx_ref[pl.ds(token, 1), :] += (
+                dx_ref[pl.ds(token, 1), :] = (
                     dx_slots[pl.ds(slot_at[0, token], 1), :]
                     + dx_slots[pl.ds(slot_at[1, token], 1), :]
                 )
@@ -335,20 +313,19 @@
         lax.fori_loop(0, tokens // 8, group, 0)
 
 
-def experts_backward(slot_of, meta, moe_in, grad_pair, grad_both, up_full, down_full):
+def experts_backward(slot_of, meta, moe_in, grad_pair, up_full, down_full):
     tokens = moe_in.shape[0]
-    slabs = (EXPERTS + SHARED, WIDE_PIECES, NARROW_PIECES, PIECE, D)
+    slabs = (EXPERTS, WIDE_PIECES, NARROW_PIECES, PIECE, D)
     slab_spec = pl.BlockSpec((1,) + slabs[1:], lambda e, *unused: (e, 0, 0, 0, 0))
     return pl.pallas_call(
         backward_kernel,
         grid_spec=pltpu.PrefetchScalarGridSpec(
             num_scalar_prefetch=2,
-            grid=(EXPERTS + SHARED,),
+            grid=(EXPERTS,),
             in_specs=[
                 whole_block((2, tokens)),
                 whole_block((tokens, D)),
                 whole_block((2, tokens, D)),
-                whole_block((tokens, D)),
                 pl.BlockSpec((1, NARROW_PIECES, D, D), lambda e, *unused: (e, 0, 0, 0)),
                 pl.BlockSpec((1, FF, D), lambda e, *unused: (e, 0, 0)),
             ],
@@ -369,18 +346,38 @@
             flops=45_000_000_000, bytes_accessed=90_000_000, transcendentals=0
         ),
         name="experts_backward",
-    )(meta, slot_of, slot_of, moe_in, grad_pair, grad_both, up_full, down_full)
+    )(meta, slot_of, slot_of, moe_in, grad_pair, up_full, down_full)
 
 
 def reduce_kernel(
     down_ref,
-    thin_ref,
     up_ref,
-    mats_ref,
-    lat_in,
+    up_all,
+    down_all,
+    moe_in,
+    grad_both,
+    dx_routed,
+    grad_logits,
+    middle,
+    qkv,
+    attended,
+    grad_state,
+    patches,
+    places,
+    mods,
+    mats_all,
+    bias_rows,
+    pre_time,
+    cond,
+    freq_low,
+    grad_gate,
+    grad_fin,
+    thin_in,
+    label_parts,
     out_ref,
     rows_ref,
     lat_ref,
+    bias_ref,
     own,
     got_core,
     out_one,
@@ -390,11 +387,24 @@
     keep_two,
     got_two,
     keep_z,
-    out_rise,
-    out_fall,
-    got_rise,
-    got_fall,
+    out_z,
+    got_z,
     row_parts,
+    late,
+    up_here,
+    down_here,
+    up_sum,
+    down_sum,
+    dx_sum,
+    grad_mid,
+    grad_att,
+    grad_qkv,
+    qkv_sum,
+    proj_sum,
+    patch_sum,
+    grad_mods,
+    lat_full,
+    lat_low,
     own_sem,
     core_send,
     core_recv,
@@ -402,39 +412,36 @@
     one_recv,
     two_send,
     two_recv,
-    rise_send,
-    rise_recv,
-    fall_send,
-    fall_recv,
+    z_send,
+    z_recv,
     row_send,
     row_recv,
     lat_own,
     lat_send,
     lat_recv,
+    here_sem,
+    core_free,
+    one_free,
 ):
-    counts = [member.shape[0] for member in (down_ref, thin_ref, up_ref, mats_ref)]
-    slabs = sum(counts)
-    direct = counts[0] + counts[1]
-    ahead = 2
+    full, low = jnp.float32, jnp.bfloat16
+    n_down, n_up, n_late = down_ref.shape[0], up_ref.shape[0], late.shape[0]
+    slabs = n_down + n_up + n_late
+    ahead, ring = 2, got_core.shape[0]
     wide, narrow = lax.axis_index(WIDE), lax.axis_index(NARROW)
     z, x = wide // 2, wide % 2
     y, c = narrow // 2, narrow % 2
     x_one, y_one = x + (1 - c) * (1 - 2 * x), y + c * (1 - 2 * y)
     x_two, y_two = x + c * (1 - 2 * x), y + (1 - c) * (1 - 2 * y)
-    to_core = (wide, y * 2 + 1 - c)
     to_one = (z * 2 + x_one, y_one * 2 + c)
     to_two = (z * 2 + x_two, y_two * 2 + c)
-    to_rise = (jnp.minimum(z + 1, 3) * 2 + x, narrow)
-    to_fall = (jnp.maximum(z - 1, 0) * 2 + x, narrow)
     first_mine = x * (1 - c) + y * c
     second_mine = y * (1 - c) + x * c
     first_step, second_step = 2 - c, 1 + c
-
     mates = [
         (wide, (y + (k // 2) * (1 - 2 * y)) * 2 + c + (k % 2) * (1 - 2 * c)) for k in range(1, 4)
     ]
     levels = [(((z + k) % 4) * 2 + x, narrow) for k in range(1, 4)]
-    to_x = (z * 2 + 1 - x, narrow)
+    to_x, to_core = (z * 2 + 1 - x, narrow), mates[0]
     barrier = pltpu.get_barrier_semaphore()
     for target in mates + levels + [to_x]:
         pl.semaphore_signal(barrier, inc=1, device_id=target, device_id_type=MESH_ID)
@@ -452,7 +459,11 @@
 
     def core_copy(source, s):
         return remote(
-            source.at[:, 1 - c], got_core.at[s], core_send.at[s % 4], core_recv.at[s], to_core
+            source.at[:, 1 - c],
+            got_core.at[s % ring],
+            core_send.at[s % 4],
+            core_recv.at[s % ring],
+            to_core,
         )
 
     def own_copy(source, s):
@@ -460,37 +471,35 @@
 
     def one_copy(s):
         return remote(
-            out_one.at[s % 2], got_one.at[s], one_send.at[s % 2], one_recv.at[s], to_one
+            out_one.at[s % 2], got_one.at[s % ring], one_send.at[s % 2], one_recv.at[s % ring], to_one
         )
 
     def two_copy(s):
+        return remote(out_two.at[s % 2], got_two.at[s], two_send.at[s % 2], two_recv.at[s], to_two)
+
+    def z_copy(s, k):
         return remote(
-            out_two.at[s % 2], got_two.at[s], two_send.at[s % 2], two_recv.at[s], to_two
-        )
-
-    def rise_copy(s):
-        return remote(
-            out_rise.at[s % 2], got_rise.at[s], rise_send.at[s % 2], rise_recv.at[s], to_rise
-        )
-
-    def fall_copy(s):
-        return remote(
-            out_fall.at[s % 2], got_fall.at[s], fall_send.at[s % 2], fall_recv.at[s], to_fall
-        )
-
-    def row_copy(s, k):
+            out_z.at[s % 2, (z + k) % 4],
+            got_z.at[s, k - 1],
+            z_send.at[s % 2, k - 1],
+            z_recv.at[s, k - 1],
+            levels[k - 1],
+        )
+
+    def row_copy(r, k):
         mate = mates[k - 1]
         return remote(
-            row_parts.at[s % 2, mate[1]],
-            rows_ref.at[s - direct, narrow],
-            row_send.at[s % 2, k - 1],
-            row_recv.at[s - direct, k - 1],
+            row_parts.at[r % 2, mate[1]],
+            rows_ref.at[r, narrow],
+            row_send.at[r % 2, k - 1],
+            row_recv.at[r, k - 1],
             mate,
         )
 
     def lat_level(k):
-        spot = lat_ref.at[z, x, y, c]
-        return remote(spot, spot, lat_send.at[k - 1], lat_recv.at[k - 1], levels[k - 1])
+        return remote(
+            lat_low, lat_ref.at[z, x, y, c], lat_send.at[k - 1], lat_recv.at[k - 1], levels[k - 1]
+        )
 
     def lat_x():
         spot = lat_ref.at[:, x, y, c]
@@ -502,19 +511,20 @@
 
     def lat_core():
         spot = lat_ref.at[:, :, :, c]
-        return remote(spot, spot, lat_send.at[5], lat_recv.at[5], mates[0])
-
-    own_lat = pltpu.make_async_copy(lat_in, lat_ref.at[z, x, y, c], lat_own.at[0])
-    own_lat.start()
-    own_lat.wait()
-    for k in range(1, 4):
-        lat_level(k).start()
+        return remote(spot, spot, lat_send.at[5], lat_recv.at[5], to_core)
+
+    def lat_own_copy():
+        return pltpu.make_async_copy(lat_low, lat_ref.at[z, x, y, c], lat_own.at[0])
 
     def begin(source, s):
         @pl.when(s >= 4)
         def _():
             core_copy(source, s).wait_send()
 
+        @pl.when(s >= ring)
+        def _():
+            pl.semaphore_wait(core_free, 1)
+
         core_copy(source, s).start()
         own_copy(source, s).start()
 
@@ -525,21 +535,32 @@
         @pl.when(s >= 2)
         def _():
             one_copy(s).wait_send()
+
+        @pl.when(s >= ring)
+        def _():
+            pl.semaphore_wait(one_free, 1)
 
         for level in range(4):
             for other in range(2):
                 place = level * 2 + other
                 base = level * 4 + other * second_step
                 send_at = base + (1 - first_mine) * first_step
+                out_one[s % 2, place] = (
+                    own[s % 3, send_at].astype(full) + got_core[s % ring, send_at].astype(full)
+                ).astype(low)
+        one_copy(s).start()
+        for level in range(4):
+            for other in range(2):
+                place = level * 2 + other
+                base = level * 4 + other * second_step
                 keep_at = base + first_mine * first_step
-                out_one[s % 2, place] = (
-                    own[s % 3, send_at].astype(jnp.float32)
-                    + got_core[s, send_at].astype(jnp.float32)
-                ).astype(jnp.bfloat16)
-                keep_one[s % 2, place] = own[s % 3, keep_at].astype(jnp.float32) + got_core[
-                    s, keep_at
-                ].astype(jnp.float32)
-        one_copy(s).start()
+                keep_one[s % 2, place] = own[s % 3, keep_at].astype(full) + got_core[
+                    s % ring, keep_at
+                ].astype(full)
+
+        @pl.when(s < slabs - ring)
+        def _():
+            pl.semaphore_signal(core_free, inc=1, device_id=to_core, device_id_type=MESH_ID)
 
     def stage_one(s):
         one_copy(s).wait_recv()
@@ -550,87 +571,276 @@
 
         for level in range(4):
             send_at = level * 2 + 1 - second_mine
+            out_two[s % 2, level] = (
+                keep_one[s % 2, send_at] + got_one[s % ring, send_at].astype(full)
+            ).astype(low)
+        two_copy(s).start()
+        for level in range(4):
             keep_at = level * 2 + second_mine
-            out_two[s % 2, level] = (
-                keep_one[s % 2, send_at] + got_one[s, send_at].astype(jnp.float32)
-            ).astype(jnp.bfloat16)
-            keep_two[s % 2, level] = keep_one[s % 2, keep_at] + got_one[s, keep_at].astype(
-                jnp.float32
+            keep_two[s % 2, level] = keep_one[s % 2, keep_at] + got_one[s % ring, keep_at].astype(
+                full
             )
-        two_copy(s).start()
+
+        @pl.when(s < slabs - ring)
+        def _():
+            pl.semaphore_signal(one_free, inc=1, device_id=to_one, device_id_type=MESH_ID)
 
     def stage_two(s):
         two_copy(s).wait_recv()
+
+        @pl.when(s >= 2)
+        def _():
+            for k in range(1, 4):
+                z_copy(s, k).wait_send()
+
         for level in range(4):
-            keep_z[s % 4, level] = keep_two[s % 2, level] + got_two[s, level].astype(jnp.float32)
-        stage_z(s, 0)
-
-    def stage_z(s, hop):
-        def pass_on(copy, out, got, shift):
-            @pl.when(s >= 2)
-            def _():
-                copy(s).wait_send()
-
-            if hop > 0:
-                copy(s).wait_recv()
-            for level in range(3):
-                value = keep_z[s % 4, level + shift]
-                if hop > 0:
-                    value = value + got[s, level].astype(jnp.float32)
-                out[s % 2, level] = value.astype(jnp.bfloat16)
-            copy(s).start()
-
-        @pl.when(z == hop)
+            out_z[s % 2, level] = (
+                keep_two[s % 2, level] + got_two[s, level].astype(full)
+            ).astype(low)
+        for k in range(1, 4):
+            z_copy(s, k).start()
+        keep_z[s % 2] = keep_two[s % 2, z] + got_two[s, z].astype(full)
+
+    def direct_place(s):
+        late_at = s - n_down - n_up
+        return (s < n_down) | ((late_at >= 0) & (late_at < SHARED))
+
+    def row_place(s):
+        return jnp.where(s < n_down + n_up, s - n_down, s - n_down - SHARED)
+
+    def finish(s):
+        total = keep_z[s % 2]
+        for k in range(1, 4):
+            z_copy(s, k).wait_recv()
+        for k in range(3):
+            total = total + got_z[s, k].astype(full)
+
+        @pl.when(direct_place(s))
         def _():
-            pass_on(rise_copy, out_rise, got_rise, 1)
-
-        @pl.when(z == 3 - hop)
+            out_ref[jnp.clip(jnp.where(s < n_down, s, s - n_up), 0, n_down + SHARED - 1)] = total
+
+        @pl.when(jnp.logical_not(direct_place(s)))
         def _():
-            pass_on(fall_copy, out_fall, got_fall, 0)
-
-    def finish(s):
-        @pl.when(z == 3)
-        def _():
-            rise_copy(s).wait_recv()
-
-        @pl.when(z == 0)
-        def _():
-            fall_copy(s).wait_recv()
-
-        total = keep_z[s % 4, z]
-        rise = got_rise[s, jnp.maximum(z - 1, 0)].astype(jnp.float32)
-        fall = got_fall[s, jnp.minimum(z, 2)].astype(jnp.float32)
-        total = total + jnp.where(z > 0, rise, 0.0) + jnp.where(z < 3, fall, 0.0)
-
-        @pl.when(s < direct)
-        def _():
-            out_ref[jnp.minimum(s, direct - 1)] = total
-
-        @pl.when(s >= direct)
-        def _():
-            @pl.when(s >= direct + 2)
+            r = row_place(s)
+
+            @pl.when(r >= 2)
             def _():
                 for k in range(1, 4):
-                    row_copy(s, k).wait_send()
+                    row_copy(r, k).wait_send()
 
             for n in range(NARROW_PIECES):
-                row_parts[s % 2, n] = total[n * ROWS : (n + 1) * ROWS]
-            rows_ref[s - direct, narrow] = row_parts[s % 2, narrow]
+                row_parts[r % 2, n] = total[n * ROWS : (n + 1) * ROWS]
+            rows_ref[r, narrow] = row_parts[r % 2, narrow]
             for k in range(1, 4):
-                row_copy(s, k).start()
+                row_copy(r, k).start()
 
     def rows_in(s):
-        @pl.when(s >= direct)
+        @pl.when(jnp.logical_not(direct_place(s)))
         def _():
             for k in range(1, 4):
-                row_copy(s, k).wait_recv()
-
-    def inside(s):
-        return (s >= 0) & (s < slabs)
+                row_copy(row_place(s), k).wait_recv()
+
+    tokens = moe_in.shape[0]
+    lats = tokens // PATCHES
+
+    def matrix(number, start, stop):
+        chunk = mats_all[number // 2, number % 2]
+        return chunk.reshape(D, chunk.shape[-1])[:, start:stop]
+
+    def mod_row(start, number):
+        return mods[pl.ds(start // PATCHES, 1), number * D : (number + 1) * D]
+
+    def keep_mod(start, number, values):
+        grad_mods[pl.ds(start // PATCHES, 1), number * D : (number + 1) * D] = jnp.sum(
+            values, 0, keepdims=True
+        )
+
+    def add_bias(number, values):
+        for k in range(values.shape[1] // D):
+            bias_ref[number + k : number + k + 1, :] += jnp.sum(
+                values[:, k * D : (k + 1) * D], 0, keepdims=True
+            )
+
+    def prepare():
+        bias_ref[...] = jnp.zeros_like(bias_ref)
+        qkv_sum[...] = jnp.zeros_like(qkv_sum)
+        proj_sum[...] = jnp.zeros_like(proj_sum)
+        patch_sum[...] = jnp.zeros_like(patch_sum)
+        grad_mods[...] = jnp.zeros_like(grad_mods)
+
+    def fetch(shared_id):
+        e = EXPERTS + shared_id
+        first = pltpu.make_async_copy(down_all.at[e], down_here, here_sem.at[0])
+        second = pltpu.make_async_copy(up_all.at[e], up_here, here_sem.at[1])
+        first.start()
+        second.start()
+        first.wait()
+        second.wait()
+        up_sum[...] = jnp.zeros_like(up_sum)
+        down_sum[...] = jnp.zeros_like(down_sum)
+
+    def shared_block(shared_id, start):
+        span = pl.ds(start, PATCHES)
+        rows, grads = moe_in[span, :], grad_both[span, :]
+        total = dx_routed[span, :] if shared_id == 0 else dx_sum[span, :]
+        for cut in range(0, FF, CUT):
+            up_part = up_columns(up_here, cut)
+            activated, slope = gelu_slope(product(rows, up_part))
+            grad_act = contract(grads, down_here[cut : cut + CUT], 1, 1)
+            grad_pre = (grad_act * slope).astype(low)
+            down_sum[cut : cut + CUT, :] += contract(activated.astype(low), grads, 0, 0)
+            up_sum[:, cut : cut + CUT] += contract(rows, grad_pre, 0, 0)
+            total = total + contract(grad_pre, up_part, 1, 1)
+        dx_sum[span, :] = total
+
+    def shared_slabs(shared_id):
+        for w in range(WIDE_PIECES):
+            for n in range(NARROW_PIECES):
+                at = (w * NARROW_PIECES + n) * PIECE
+                late[shared_id, w * 2 + n // 2, n % 2] = down_sum[at : at + PIECE, :].astype(low)
+                late[SHARED + shared_id, w * 2 + n // 2, n % 2] = up_sum[
+                    w * PIECE : (w + 1) * PIECE, n * D : (n + 1) * D
+                ].astype(low)
+
+    def back_out(start):
+        span = pl.ds(start, PATCHES)
+        grads = dx_sum[span, :] + contract(
+            grad_logits[span, :].astype(low), matrix(0, 4 * D, 4 * D + 128), 1, 1
+        )
+        normed, inv_std = layer_norm(middle[span, :])
+        keep_mod(start, 3, grads)
+        keep_mod(start, 4, grads * normed)
+        grads = grad_state[span, :] + norm_back(
+            grads * (1.0 + mod_row(start, 4)), normed, inv_std
+        )
+        grad_mid[...] = grads
+        proj = matrix(0, 3 * D, 4 * D)
+        rows = attended[span, :]
+        keep_mod(start, 2, (product(rows, proj) + bias_rows[3:4, :]) * grads)
+        grads = grads * mod_row(start, 2)
+        add_bias(3, grads)
+        grads = grads.astype(low)
+        proj_sum[...] += contract(rows, grads, 0, 0)
+        grad_att[...] = contract(grads, proj, 1, 1).astype(low)
+
+    def back_pair(pair, start):
+        span = pl.ds(start, PATCHES)
+        lane = lax.broadcasted_iota(jnp.int32, (PATCHES, 2 * HD), 1)
+        at = pair * 2 * HD
+        queries = qkv[span, at : at + 2 * HD]
+        keys = qkv[span, D + at : D + at + 2 * HD]
+        values = qkv[span, 2 * D + at : 2 * D + at + 2 * HD]
+        grads = grad_att[:, at : at + 2 * HD]
+        sums = None
+        for half in range(2):
+            mine = (lane < HD) if half == 0 else (lane >= HD)
+            scores = contract(jnp.where(mine, queries, 0), keys, 1, 1) * HD ** (-0.5)
+            powers = jnp.exp(scores - jnp.max(scores, 1, keepdims=True))
+            probs = powers / jnp.sum(powers, 1, keepdims=True)
+            grad_mine = jnp.where(mine, grads, 0)
+            grad_probs = contract(grad_mine, values, 1, 1)
+            grad_scores = (
+                probs
+                * (grad_probs - jnp.sum(probs * grad_probs, 1, keepdims=True))
+                * HD ** (-0.5)
+            ).astype(low)
+            parts = (
+                product(grad_scores, jnp.where(mine, keys, 0)),
+                contract(grad_scores, jnp.where(mine, queries, 0), 0, 0),
+                contract(probs.astype(low), grad_mine, 0, 0),
+            )
+            sums = parts if sums is None else [a + b for a, b in zip(sums, parts)]
+        for k in range(3):
+            where = k * D + at
+            grad_qkv[:, where : where + 2 * HD] = sums[k].astype(low)
+            bias_ref[k : k + 1, at : at + 2 * HD] += jnp.sum(sums[k], 0, keepdims=True)
+
+    def back_in(start):
+        span = pl.ds(start, PATCHES)
+        emb = contract(patches[span, :], matrix(2, 4 * D, 4 * D + 128), 1, 1)
+        emb = emb + bias_rows[10:11, :] + places[...]
+        normed, inv_std = layer_norm(emb)
+        rows = (normed * (1.0 + mod_row(start, 1)) + mod_row(start, 0)).astype(low)
+        qkv_sum[...] += contract(rows, grad_qkv[...], 0, 0)
+        grads = contract(grad_qkv[...], matrix(0, 0, 3 * D), 1, 1)
+        keep_mod(start, 0, grads)
+        keep_mod(start, 1, grads * normed)
+        grads = grad_mid[...] + norm_back(grads * (1.0 + mod_row(start, 1)), normed, inv_std)
+        add_bias(10, grads)
+        patch_sum[...] += contract(grads.astype(low), patches[span, :], 0, 0)
+
+    def silu_slope(values):
+        gate = jax.nn.sigmoid(values)
+        return gate + values * gate * (1.0 - gate)
+
+    def back_conditions():
+        grad_mods[:, 5 * D :] = grad_gate[...]
+        grads = grad_mods[...]
+        mod_low, fin_low = grads.astype(low), grad_fin[...].astype(low)
+        grad_act = (
+            contract(mod_low[:, : 4 * D], matrix(1, 0, 4 * D), 1, 1)
+            + contract(mod_low[:, 4 * D :], matrix(2, 0, 2 * D), 1, 1)
+            + contract(fin_low, matrix(2, 2 * D, 4 * D), 1, 1)
+        )
+        grad_cond = silu_slope(cond[...]) * grad_act
+        high = grad_cond.astype(low)
+        grad_time = silu_slope(pre_time[...]) * contract(high, matrix(3, 1024, 1408), 1, 1)
+        add_bias(4, grads)
+        add_bias(11, grad_time)
+        add_bias(12, grad_cond)
+        add_bias(13, grad_fin[...])
+        high = high.astype(full)
+        rest = grad_cond - high
+        middle_part = rest.astype(low).astype(full)
+        act = jax.nn.silu(cond[...]).astype(low).astype(full)
+        hid = jax.nn.silu(pre_time[...]).astype(low).astype(full)
+        mod_low, fin_low = mod_low.astype(full), fin_low.astype(full)
+        quarters = (
+            jnp.concatenate([act, hid, mod_low[:, : 2 * D]], 1),
+            mod_low[:, 2 * D :],
+            jnp.concatenate([fin_low, high, grad_time.astype(low).astype(full)], 1),
+            jnp.concatenate(
+                [
+                    freq_low[...].astype(full),
+                    middle_part,
+                    rest - middle_part,
+                    label_parts[...].astype(full),
+                    jnp.zeros((8, D), full),
+                ],
+                1,
+            ),
+        )
+        for lat in range(lats):
+            for k in range(4):
+                lat_full[lat * 4 + k : lat * 4 + k + 1, :] = quarters[k][lat : lat + 1, :]
+        lat_low[...] = lat_full[...].astype(low)
+
+    def last_slabs():
+        for w in range(WIDE_PIECES):
+            span = slice(w * PIECE, (w + 1) * PIECE)
+            for n in range(3):
+                late[2 * SHARED, w * 2 + n // 2, n % 2] = qkv_sum[
+                    span, n * D : (n + 1) * D
+                ].astype(low)
+            late[2 * SHARED, w * 2 + 1, 1] = proj_sum[span, :].astype(low)
+            thin = thin_in[span, :] + pltpu.roll(patch_sum[span, :], EXPERTS + PD, 1)
+            for n in range(NARROW_PIECES):
+                late[2 * SHARED + 1, w * 2 + n // 2, n % 2] = jnp.zeros((PIECE, D), low)
+            late[2 * SHARED + 1, w * 2, 0, :, :128] = thin.astype(low)
+
+    first_lat = SHARED * lats
+    units = (
+        back_out,
+        lambda start: back_pair(0, start),
+        lambda start: back_pair(1, start),
+        lambda start: back_pair(2, start),
+        back_in,
+    )
+    after = first_lat + len(units) * lats
 
     def tick(t, unused):
         first = 0
-        for source, count in zip((down_ref, thin_ref, up_ref, mats_ref), counts):
+        for source, count in ((down_ref, n_down), (up_ref, n_up), (late, n_late)):
 
             @pl.when((t >= first) & (t < first + count))
             def _():
@@ -638,59 +848,82 @@
 
             first += count
 
-        @pl.when(t == 4)
+        for lag, stage in enumerate((stage_core, stage_one, stage_two, finish, rows_in)):
+            s = t - ahead - lag
+
+            @pl.when((s >= 0) & (s < slabs))
+            def _():
+                stage(s)
+
+        @pl.when(t == 0)
+        def _():
+            prepare()
+
+        for shared_id in range(SHARED):
+            start_at = shared_id * lats
+
+            @pl.when(t == start_at)
+            def _():
+                fetch(shared_id)
+
+            @pl.when((t >= start_at) & (t < start_at + lats))
+            def _():
+                shared_block(
+                    shared_id,
+                    pl.multiple_of(jnp.clip(t - start_at, 0, lats - 1) * PATCHES, PATCHES),
+                )
+
+            @pl.when(t == start_at + lats - 1)
+            def _():
+                shared_slabs(shared_id)
+
+        for number, unit in enumerate(units):
+
+            @pl.when((t >= first_lat) & (t < after) & ((t - first_lat) % len(units) == number))
+            def _():
+                lat = jnp.clip((t - first_lat) // len(units), 0, lats - 1)
+                unit(pl.multiple_of(lat * PATCHES, PATCHES))
+
+        @pl.when(t == after)
+        def _():
+            back_conditions()
+            lat_own_copy().start()
+            for k in range(1, 4):
+                lat_level(k).start()
+            lat_own_copy().wait()
+
+        @pl.when(t == after + 1)
+        def _():
+            last_slabs()
+
+        @pl.when(t == after + 3)
         def _():
             for k in range(1, 4):
                 lat_level(k).wait_recv()
             lat_x().start()
 
-        @pl.when(t == 6)
+        @pl.when(t == after + 5)
         def _():
             lat_x().wait_recv()
             lat_y().start()
 
-        @pl.when(t == 8)
+        @pl.when(t == after + 7)
         def _():
             lat_y().wait_recv()
             lat_core().start()
 
-        for lag, stage in enumerate(
-            (
-                stage_core,
-                stage_one,
-                stage_two,
-                lambda s: stage_z(s, 1),
-                lambda s: stage_z(s, 2),
-                finish,
-                rows_in,
-            )
-        ):
-            s = t - ahead - lag
-
-            @pl.when(inside(s))
-            def _():
-                stage(s)
-
         return unused
 
-    lax.fori_loop(0, slabs + ahead + 6, tick, 0)
-
+    lax.fori_loop(0, slabs + ahead + 4, tick, 0)
     for back in range(4):
         core_copy(down_ref.at[0], slabs - 1 - back).wait_send()
+    turned = rows_ref.shape[0]
     for back in range(2):
         one_copy(slabs - 1 - back).wait_send()
         two_copy(slabs - 1 - back).wait_send()
         for k in range(1, 4):
-            row_copy(slabs - 1 - back, k).wait_send()
-
-        @pl.when(z < 3)
-        def _():
-            rise_copy(slabs - 1 - back).wait_send()
-
-        @pl.when(z > 0)
-        def _():
-            fall_copy(slabs - 1 - back).wait_send()
-
+            z_copy(slabs - 1 - back, k).wait_send()
+            row_copy(turned - 1 - back, k).wait_send()
     for k in range(1, 4):
         lat_level(k).wait_send()
     lat_x().wait_send()
@@ -698,104 +931,91 @@
     lat_core().wait()
 
 
-def reduce_slabs(down_slabs, up_slabs, mats_slabs, thin, lat):
-    members = (down_slabs, thin, up_slabs, mats_slabs)
-    slabs = sum(member.shape[0] for member in members)
-    direct = down_slabs.shape[0] + thin.shape[0]
-    turned = slabs - direct
+def reduce_slabs(down_slabs, up_slabs, up_all, down_all, members):
+    n_late = 2 * SHARED + 2
+    routed = down_slabs.shape[0]
+    slabs = 2 * routed + n_late
+    direct, turned = routed + SHARED, routed + SHARED + 2
+    ring = 6
     low, full = jnp.bfloat16, jnp.float32
     sources = [
-        member.reshape(member.shape[0], WIDE_PIECES * NARROW_PIECES // 2, 2, PIECE, D)
-        for member in members
+        member.reshape(routed, WIDE_PIECES * NARROW_PIECES // 2, 2, PIECE, D)
+        for member in (down_slabs, up_slabs)
     ]
-    dma = pltpu.SemaphoreType.DMA
-    vmem = pl.BlockSpec(memory_space=pltpu.VMEM)
-    sums, rows, lats = pl.pallas_call(
+    tokens = members[0].shape[0]
+    dma, regular = pltpu.SemaphoreType.DMA, pltpu.SemaphoreType.REGULAR
+    vmem, anywhere = pl.BlockSpec(memory_space=pltpu.VMEM), pl.BlockSpec(memory_space=pl.ANY)
+    sums, rows, lats, bias_sum = pl.pallas_call(
         reduce_kernel,
         out_shape=[
             jax.ShapeDtypeStruct((direct, PIECE, D), full),
             jax.ShapeDtypeStruct((turned, NARROW_PIECES, ROWS, D), full),
             jax.ShapeDtypeStruct((4, 2, 2, 2, LAT_ROWS, LAT_COLS), low),
+            jax.ShapeDtypeStruct((16, D), full),
         ],
-        in_specs=[pl.BlockSpec(memory_space=pl.ANY)] * 5,
-        out_specs=[vmem, vmem, pl.BlockSpec(memory_space=pl.ANY)],
+        in_specs=[anywhere] * 4 + [vmem] * len(members),
+        out_specs=[vmem, vmem, anywhere, vmem],
         scratch_shapes=[
             pltpu.VMEM((3, 16, PIECE, D), low),
-            pltpu.VMEM((slabs, 16, PIECE, D), low),
+            pltpu.VMEM((ring, 16, PIECE, D), low),
             pltpu.VMEM((2, 8, PIECE, D), low),
             pltpu.VMEM((2, 8, PIECE, D), full),
-            pltpu.VMEM((slabs, 8, PIECE, D), low),
+            pltpu.VMEM((ring, 8, PIECE, D), low),
             pltpu.VMEM((2, 4, PIECE, D), low),
             pltpu.VMEM((2, 4, PIECE, D), full),
             pltpu.VMEM((slabs, 4, PIECE, D), low),
-            pltpu.VMEM((4, 4, PIECE, D), full),
-            pltpu.VMEM((2, 3, PIECE, D), low),
-            pltpu.VMEM((2, 3, PIECE, D), low),
-            pltpu.VMEM((slabs, 3, PIECE, D), low),
+            pltpu.VMEM((2, PIECE, D), full),
+            pltpu.VMEM((2, 4, PIECE, D), low),
             pltpu.VMEM((slabs, 3, PIECE, D), low),
             pltpu.VMEM((2, NARROW_PIECES, ROWS, D), full),
+            pltpu.VMEM((n_late, 16, 2, PIECE, D), low),
+            pltpu.VMEM((NARROW_PIECES, D, D), low),
+            pltpu.VMEM((FF, D), low),
+            pltpu.VMEM((D, FF), full),
+            pltpu.VMEM((FF, D), full),
+            pltpu.VMEM((tokens, D), full),
+            pltpu.VMEM((PATCHES, D), full),
+            pltpu.VMEM((PATCHES, D), low),
+            pltpu.VMEM((PATCHES, 3 * D), low),
+            pltpu.VMEM((D, 3 * D), full),
+            pltpu.VMEM((D, D), full),
+            pltpu.VMEM((D, 128), full),
+            pltpu.VMEM((8, 6 * D), full),
+            pltpu.VMEM((LAT_ROWS, LAT_COLS), full),
+            pltpu.VMEM((LAT_ROWS, LAT_COLS), low),
             dma((3,)),
             dma((4,)),
-            dma((slabs,)),
+            dma((ring,)),
+            dma((2,)),
+            dma((ring,)),
             dma((2,)),
             dma((slabs,)),
-            dma((2,)),
-            dma((slabs,)),
-            dma((2,)),
-            dma((slabs,)),
-            dma((2,)),
-            dma((slabs,)),
+            dma((2, 3)),
+            dma((slabs, 3)),
             dma((2, 3)),
             dma((turned, 3)),
             dma((1,)),
             dma((6,)),
             dma((6,)),
+            dma((2,)),
+            regular,
+            regular,
         ],
         compiler_params=pltpu.CompilerParams(
             collective_id=0, has_side_effects=True, vmem_limit_bytes=REDUCE_ROOM
         ),
         name="reduce_slabs",
-    )(*sources, lat)
-    return sums, rows, lats.reshape(-1, LAT_COLS)
-
-
-def thin_slab(thin, grad_bias):
-    owners = WIDE_PIECES * NARROW_PIECES
-    top = thin.reshape(owners, ROWS, -1)
-    top = jnp.pad(top, ((0, 0), (0, 0), (0, D - top.shape[2])))
-    line = grad_bias.reshape(owners, 1, -1)
-    line = jnp.pad(line, ((0, 0), (0, PIECE - ROWS - 1), (0, D - line.shape[2])))
-    both = jnp.concatenate([top, line], 1).astype(jnp.bfloat16)
-    return both.reshape(1, WIDE_PIECES, NARROW_PIECES, PIECE, D)
-
-
-def lat_block(lows, grad_cond, labels):
-    high = lax.reduce_precision(grad_cond, 8, 7)
-    middle = lax.reduce_precision(grad_cond - high, 8, 7)
-    label_parts = jnp.stack([labels // 32, labels % 32], 1).astype(jnp.bfloat16)
-    whole = jnp.concatenate(
-        [
-            lows,
-            middle.astype(jnp.bfloat16),
-            (grad_cond - high - middle).astype(jnp.bfloat16),
-            label_parts,
-        ],
-        1,
-    )
-    room = LAT_ROWS * LAT_COLS // labels.shape[0] - whole.shape[1]
-    return jnp.pad(whole, ((0, 0), (0, room))).reshape(LAT_ROWS, LAT_COLS)
+    )(*sources, up_all, down_all, *members)
+    return sums, rows, lats.reshape(-1, LAT_COLS), bias_sum
 
 
 def plain_grads(
     down_slabs, up_slabs, mats_slabs, thin, grad_bias, lows, grad_cond, labels, row_count
 ):
-    def scattered(member, up_form):
-        order = (0, 1, 3, 2, 4) if up_form else (0, 1, 2, 3, 4)
-        member = member.astype(jnp.float32).transpose(order)
-        member = member.reshape(member.shape[0], -1, FF if up_form else D)
+    def scattered(member):
         return lax.psum_scatter(member, AXES, scatter_dimension=1, tiled=True)
 
-    proj_grad = scattered(mats_slabs, True)
+    proj_grad = scattered(mats_slabs)
     row_start = lax.axis_index(AXES) * row_count
     thin_grad = lax.psum_scatter(thin, AXES, scatter_dimension=0, tiled=True)
     bias_grad = lax.psum_scatter(grad_bias, AXES, scatter_dimension=0, tiled=True)
@@ -805,13 +1025,14 @@
     mats_grad = jnp.concatenate(
         [proj_grad[0], grad_mod, grad_time2, grad_fin, thin_grad, grad_time1, grad_table], 1
     )
-    return (mats_grad, scattered(up_slabs, True), scattered(down_slabs, False), bias_grad)
+    return (mats_grad, scattered(up_slabs), scattered(down_slabs), bias_grad)
 
 
 def update_kernel(
     sums_ref,
     rows_ref,
     lat_ref,
+    bias_sum,
     loss_ref,
     mats_ref,
     up_ref,
@@ -939,12 +1160,11 @@
     start_last = 13 * D
     width_last = mats_grad.shape[1] - start_last
     room = 11 * 128
-    thin = sums_ref[EXPERTS + SHARED][:16, :128]
+    thin = jnp.concatenate(
+        [rows_ref[EXPERTS + SHARED + 1, 0][:, :128], jnp.zeros((4, 128), full)], 0
+    )
     thin = jnp.where(
-        (lax.broadcasted_iota(jnp.int32, (16, 128), 1) < EXPERTS + 2 * PD)
-        & (lax.broadcasted_iota(jnp.int32, (16, 128), 0) < ROWS),
-        thin,
-        0.0,
+        lax.broadcasted_iota(jnp.int32, (16, 128), 1) < EXPERTS + 2 * PD, thin, 0.0
     )
 
     def padded(member):
@@ -958,11 +1178,10 @@
         + pltpu.roll(padded(table), EXPERTS + 2 * PD + FREQ, 1)
     )
     mats_grad[:, start_last:] = last[:ROWS, :width_last]
-    bias_grad[...] = sums_ref[EXPERTS + SHARED][ROWS : ROWS + 1, : bias_grad.shape[1]]
 
     part[...] = jnp.zeros_like(part)
     widths = column_widths()
-    mats_at, line_at = 360, 416
+    mats_at, line_at, bias_at = 360, 416, 432
     total_cols = mats_grad.shape[1]
     cuts = [(at, min(at + 128, total_cols)) for at in range(0, total_cols, 128)]
     for number, (begin, end) in enumerate(cuts):
@@ -1012,6 +1231,8 @@
     line = lax.fori_loop(0, EXPERTS + SHARED, begin_up, line)
     line = lax.fori_loop(0, EXPERTS + SHARED, begin_down, line)
     part[line_at : line_at + 1, :] = line
+    for k in range(D // 128):
+        part[bias_at + 16 * k : bias_at + 16 * (k + 1), :] = bias_sum[:, 128 * k : 128 * (k + 1)]
 
     exchange(
         [
@@ -1047,6 +1268,14 @@
 
     line = sums_row(line_at)
     loss_out[...] = pick(line, 46)
+    room = bias_grad.shape[1]
+    begin = (wide * NARROW_PIECES + narrow) * room
+    parts = []
+    for k in range(3):
+        block = jnp.minimum(begin // 128 + k, 47)
+        parts.append(sums_row(bias_at + (block % 3) * 16 + block // 3))
+    parts = jnp.broadcast_to(jnp.concatenate(parts, 1), (8, D))
+    bias_grad[...] = pltpu.roll(parts, (D - begin % 128) % D, 1)[0:1, :room]
     for number, (begin, end) in enumerate(cuts):
         mats_col_new[:, begin:end] = decay * mats_col[:, begin:end] + (1.0 - decay) * (
             sums_row(mats_at + number, end - begin) / D
@@ -1145,7 +1374,7 @@
     settle(bias_new, bias_copy, index, bias_ref[...], bias_step, clipped(46, 15 * D))
 
 
-def update_kernel_call(sums, rows, lat, masters, factors, loss_part):
+def update_kernel_call(sums, rows, lat, bias_sum, masters, factors, loss_part):
     mats, up_weights, down_weights, biases = masters
     mats_row, mats_col, up_row, up_col, down_row, down_col, bias_state = factors
     full, low = jnp.float32, jnp.bfloat16
@@ -1153,6 +1382,7 @@
         sums,
         rows,
         lat,
+        bias_sum,
         loss_part.reshape(1, 1),
         mats,
         up_weights,
@@ -1171,10 +1401,10 @@
         return jax.ShapeDtypeStruct(member.shape, kind)
 
     stacks = []
-    for at in (4, 5, 6):
+    for at in (5, 6, 7):
         stacks.append([like(args[at], full), like(args[at], full), like(args[at], low)])
-        stacks[-1] += [like(args[2 * at], full), like(args[2 * at + 1], full)]
-    lines = [like(args[7], full), like(args[7], full), like(args[7], low), like(args[7], full)]
+        stacks[-1] += [like(args[2 * at - 1], full), like(args[2 * at], full)]
+    lines = [like(args[8], kind) for kind in (full, full, low, full)]
     vmem = pl.BlockSpec(memory_space=pltpu.VMEM)
     dma = pltpu.SemaphoreType.DMA
     outs = pl.pallas_call(
@@ -1862,7 +2092,7 @@
     )
 
 
-def forward_fused(mats, up_weights, down_weights, biases, latents, noise, timesteps, labels, routes):
+def forward_fused(mats, up_weights, down_weights, biases, latents, noise, timesteps, labels):
     num_latents = latents.shape[0]
     rows_here = num_latents * PATCHES
     steps_f = timesteps.astype(jnp.float32)
@@ -1882,99 +2112,97 @@
         jnp.pad(freq_low, less),
         jnp.pad(label_low, less),
     )
-    mats_full, bias_full, down_full, up_full = outs[:4]
-    modulation, final_mod, pre_time, cond = [member[:num_latents] for member in outs[4:8]]
-    qkv_out, attended, middle, moe_in, logits, shared_out = outs[8:]
-    logits = logits[:, :EXPERTS]
-    n_up = up_full.shape[0]
-    full = mats_full.reshape(NARROW_PIECES, D, -1)
-    matrices = [
-        full[0][:, : 3 * D],
-        full[0][:, 3 * D : 4 * D],
-        jnp.concatenate([full[1][:, : 4 * D], full[2][:, : 2 * D]], 1),
-        full[3][:, 1024 : 1024 + D],
-        full[2][:, 2 * D : 4 * D],
-        full[0][:, 4 * D : 4 * D + 16],
-        full[1][:, 4 * D : 4 * D + 16],
-        full[2][:, 4 * D : 4 * D + 16],
-        full[3][:, 1024 + D :],
-        full[3][:, :CLASSES],
-    ]
-    line = jnp.sum(bias_full.reshape(-1, 16, D).astype(jnp.float32), 0).reshape(-1)[: 15 * D]
-    vectors = cut_pieces(line, bias_widths(), 0)
-    up_full = up_full.reshape(n_up, NARROW_PIECES, D, D)
-    down_full = down_full.reshape(n_up, FF, D)
-    weights = (matrices, vectors, up_full, down_full)
-    w_qkv, w_proj, w_mod, w_time2, w_final, w_router, w_head, w_patch, w_time1, w_table = matrices
-    b_qkv, b_proj, b_mod, b_patch, b_time1, b_time2, b_final = vectors
-    shift_attn, scale_attn, gate_attn, shift_moe, scale_moe, gate_moe = [
-        member[:, None, :] for member in jnp.split(modulation, 6, 1)
-    ]
-    shift_fin, scale_fin = [member[:, None, :] for member in jnp.split(final_mod, 2, 1)]
-    embedded = (
-        contract(patches, w_patch, 1, 1).reshape(num_latents, PATCHES, D)
-        + b_patch
-        + positions()[None]
-    )
-    normed_one, inv_one = layer_norm(embedded)
-    attn_in = (
-        (normed_one * (1.0 + scale_attn) + shift_attn).astype(jnp.bfloat16).reshape(rows_here, D)
-    )
-    qkv_out = qkv_out.reshape(num_latents, PATCHES, 3, HEADS, HD)
-    scores = jnp.einsum(
-        LQK, qkv_out[:, :, 0], qkv_out[:, :, 1], preferred_element_type=jnp.float32
-    ) * HD ** (-0.5)
-    attn_out = (product(attended, w_proj) + b_proj).reshape(num_latents, PATCHES, D)
-    middle = middle.reshape(num_latents, PATCHES, D)
-    normed_two, inv_two = layer_norm(middle)
+    n_up = outs[3].shape[0]
+    return SimpleNamespace(
+        patches=jnp.pad(patches, ((0, 0), (0, 128 - PD))),
+        freq_low=jnp.pad(freq_low, less),
+        mats_full=outs[0],
+        bias_full=outs[1],
+        down_full=outs[2].reshape(n_up, FF, D),
+        up_full=outs[3].reshape(n_up, NARROW_PIECES, D, D),
+        mods=outs[4],
+        fin=outs[5],
+        pre_time=outs[6],
+        cond=outs[7],
+        qkv=outs[8],
+        attended=outs[9],
+        middle=outs[10],
+        moe_in=outs[11],
+        logits=outs[12],
+        shared_out=outs[13],
+    )
+
+
+def backward_fused(fused, latents, noise, labels, routes, total_tokens):
+    num_latents = latents.shape[0]
+    rows_here = num_latents * PATCHES
+    less = ((0, 8 - num_latents), (0, 0))
+    mods, fin = fused.mods[:num_latents], fused.fin[:num_latents]
+    gate_moe = mods[:, None, 5 * D :]
+    shift_fin, scale_fin = fin[:, None, :D], fin[:, None, D:]
+    mats_full = fused.mats_full.reshape(NARROW_PIECES, D, -1)
+    w_head = mats_full[1][:, 4 * D : 4 * D + PD]
+    line = jnp.sum(fused.bias_full.reshape(-1, 16, D).astype(jnp.float32), 0)
     route_hot = (routes[:, :, None] == jnp.arange(EXPERTS, dtype=jnp.int32)[None, None, :]).astype(
         jnp.float32
     )
+    logits = fused.logits[:, :EXPERTS]
     gate_vals = jax.nn.softmax(jnp.sum(route_hot * logits[:, None, :], 2), -1)
     slot_of, slot_meta = pack_slots(routes)
-    routed = experts_forward(slot_of, slot_meta, moe_in, up_full, down_full)
-    moe_out = gate_vals[:, 0:1] * routed[0] + gate_vals[:, 1:2] * routed[1] + shared_out
+    routed = experts_forward(slot_of, slot_meta, fused.moe_in, fused.up_full, fused.down_full)
+    moe_out = gate_vals[:, 0:1] * routed[0] + gate_vals[:, 1:2] * routed[1] + fused.shared_out
     moe_out = moe_out.reshape(num_latents, PATCHES, D)
-    final_state = middle + gate_moe * moe_out
+    final_state = fused.middle.reshape(num_latents, PATCHES, D) + gate_moe * moe_out
     normed_fin, inv_fin = layer_norm(final_state)
     head_in = (
         (normed_fin * (1.0 + scale_fin) + shift_fin).astype(jnp.bfloat16).reshape(rows_here, D)
     )
     errors = product(head_in, w_head) - noise.reshape(rows_here, PD)
-    kept = SimpleNamespace(
-        patches=patches,
-        freq_low=freq_low,
-        pre_time=pre_time,
-        hid_time=jax.nn.silu(pre_time).astype(jnp.bfloat16),
-        cond=cond,
-        cond_act=jax.nn.silu(cond).astype(jnp.bfloat16),
-        scale_attn=scale_attn,
-        gate_attn=gate_attn,
-        scale_moe=scale_moe,
-        gate_moe=gate_moe,
-        scale_fin=scale_fin,
-        normed_one=normed_one,
-        inv_one=inv_one,
-        attn_in=attn_in,
-        qkv_out=qkv_out,
-        log_totals=jax.nn.logsumexp(scores, -1),
-        attended=attended,
-        attn_out=attn_out,
-        normed_two=normed_two,
-        inv_two=inv_two,
-        moe_in=moe_in,
-        route_hot=route_hot,
-        gate_vals=gate_vals,
-        slot_of=slot_of,
-        slot_meta=slot_meta,
-        routed=routed,
-        moe_out=moe_out,
-        normed_fin=normed_fin,
-        inv_fin=inv_fin,
-        head_in=head_in,
-        errors=errors,
-    )
-    return weights, kept
+    grad_head, grad_head_in, unused = linear_back(errors * (2.0 / total_tokens), head_in, w_head)
+    grad_head_in = grad_head_in.reshape(num_latents, PATCHES, D)
+    grad_fin = jnp.concatenate(
+        [jnp.sum(grad_head_in, 1), jnp.sum(grad_head_in * normed_fin, 1)], 1
+    )
+    grad_state = norm_back(grad_head_in * (1.0 + scale_fin), normed_fin, inv_fin)
+    grad_gate = jnp.sum(moe_out * grad_state, 1)
+    grad_moe = (gate_moe * grad_state).reshape(rows_here, D)
+    grad_gates = jnp.stack([jnp.sum(routed[k] * grad_moe, 1) for k in range(2)], 1)
+    grad_pair = jnp.stack(
+        [(gate_vals[:, k : k + 1] * grad_moe).astype(jnp.bfloat16) for k in range(2)], 0
+    )
+    up_slabs, down_slabs, dx_routed = experts_backward(
+        slot_of, slot_meta, fused.moe_in, grad_pair, fused.up_full, fused.down_full
+    )
+    grad_picked = gate_vals * (grad_gates - jnp.sum(gate_vals * grad_gates, 1, keepdims=True))
+    grad_logits = jnp.sum(route_hot * grad_picked[:, :, None], 1)
+    grad_router = contract(fused.moe_in, grad_logits.astype(jnp.bfloat16), 0, 0)
+    thin = jnp.pad(jnp.concatenate([grad_router, grad_head], 1), ((0, 0), (0, 128 - 32)))
+    label_parts = jnp.stack([labels // 32, labels % 32], 1).astype(jnp.bfloat16)
+    members = (
+        fused.moe_in,
+        grad_moe.astype(jnp.bfloat16),
+        dx_routed,
+        jnp.pad(grad_logits, ((0, 0), (0, 128 - EXPERTS))),
+        fused.middle,
+        fused.qkv,
+        fused.attended,
+        grad_state.reshape(rows_here, D),
+        fused.patches,
+        positions(),
+        fused.mods,
+        fused.mats_full,
+        line,
+        fused.pre_time,
+        fused.cond,
+        fused.freq_low,
+        jnp.pad(grad_gate, less),
+        jnp.pad(grad_fin, less),
+        thin,
+        jnp.pad(label_parts, ((0, 8 - num_latents), (0, 126))),
+    )
+    return jnp.sum(errors * errors), reduce_slabs(
+        down_slabs, up_slabs, fused.up_full, fused.down_full, members
+    )
 
 
 def backward(weights, kept, total_tokens):
@@ -2003,8 +2231,20 @@
         [(gate_vals[:, k : k + 1] * grad_moe).astype(jnp.bfloat16) for k in range(2)], 0
     )
     up_slabs, down_slabs, grad_moe_in = experts_backward(
-        kept.slot_of, kept.slot_meta, moe_in, grad_pair, grad_moe_low, up_full, down_full
-    )
+        kept.slot_of, kept.slot_meta, moe_in, grad_pair, up_full, down_full
+    )
+    up_all = [up_slabs.transpose(0, 1, 3, 2, 4).reshape(-1, D, FF)]
+    down_all = [down_slabs.reshape(-1, FF, D)]
+    for shared_id in range(EXPERTS, EXPERTS + SHARED):
+        up_part = jnp.concatenate([up_full[shared_id, k] for k in range(NARROW_PIECES)], 1)
+        activated, slope = gelu_slope(product(moe_in, up_part))
+        grad_act = contract(grad_moe_low, down_full[shared_id], 1, 1)
+        grad_pre = (grad_act * slope).astype(jnp.bfloat16)
+        down_all.append(contract(activated.astype(jnp.bfloat16), grad_moe_low, 0, 0)[None])
+        up_all.append(contract(moe_in, grad_pre, 0, 0)[None])
+        grad_moe_in = grad_moe_in + contract(grad_pre, up_part, 1, 1)
+    up_slabs = jnp.concatenate([member.astype(jnp.float32) for member in up_all], 0)
+    down_slabs = jnp.concatenate([member.astype(jnp.float32) for member in down_all], 0)
     grad_picked = gate_vals * (grad_gates - jnp.sum(gate_vals * grad_gates, 1, keepdims=True))
     grad_logits = jnp.sum(kept.route_hot * grad_picked[:, :, None], 1)
     grad_router, grad_from_router, unused = linear_back(grad_logits, moe_in, w_router)
@@ -2069,12 +2309,7 @@
     grad_hid_time = contract(grad_cond_low, w_time2, 1, 1)
     grad_pre_time = slope_back(jax.nn.silu, kept.pre_time, grad_hid_time)
     grad_time_low = grad_pre_time.astype(jnp.bfloat16)
-    mats_slabs = (
-        jnp.concatenate([grad_w_qkv, grad_proj], 1)
-        .astype(jnp.bfloat16)
-        .reshape(1, WIDE_PIECES, PIECE, NARROW_PIECES, D)
-        .transpose(0, 1, 3, 2, 4)
-    )
+    mats_slabs = jnp.concatenate([grad_w_qkv, grad_proj], 1)[None]
     thin = jnp.concatenate([grad_router, grad_head, grad_patch], 1)
     grad_bias = jnp.concatenate(
         [
@@ -2254,11 +2489,16 @@
     *factors,
 ):
     rows_here = mats.shape[0]
-    kernel_fits = lax.axis_size(WIDE) == WIDE_PIECES and lax.axis_size(NARROW) == NARROW_PIECES
-    if kernel_fits:
-        gathered, kept = forward_fused(
-            mats, up_weights, down_weights, biases, latents, noise, timesteps, labels, routes
-        )
+    total_tokens = latents.shape[0] * PATCHES * lax.axis_size(AXES)
+    masters = (mats, up_weights, down_weights, biases)
+    if lax.axis_size(WIDE) == WIDE_PIECES and lax.axis_size(NARROW) == NARROW_PIECES:
+        fused = forward_fused(
+            mats, up_weights, down_weights, biases, latents, noise, timesteps, labels
+        )
+        loss_part, (sums, turned, lat, bias_sum) = backward_fused(
+            fused, latents, noise, labels, routes, total_tokens
+        )
+        outs = update_kernel_call(sums, turned, lat, bias_sum, masters, factors, loss_part)
     else:
         flat = jnp.concatenate([mats.reshape(-1), biases], 0).astype(jnp.bfloat16)
         flat = lax.all_gather(flat, AXES, axis=0, tiled=False)
@@ -2271,22 +2511,9 @@
             )
         )
         kept = forward(gathered, latents, noise, timesteps, labels, routes)
-    total_tokens = latents.shape[0] * PATCHES * lax.axis_size(AXES)
-    up_slabs, down_slabs, mats_slabs, thin, grad_bias, lows, grad_cond = backward(
-        gathered, kept, total_tokens
-    )
-    loss_part = jnp.sum(kept.errors * kept.errors)
-    masters = (mats, up_weights, down_weights, biases)
-    if kernel_fits:
-        sums, rows, lat = reduce_slabs(
-            down_slabs,
-            up_slabs,
-            mats_slabs,
-            thin_slab(thin, grad_bias),
-            lat_block(lows, grad_cond, labels),
-        )
-        outs = update_kernel_call(sums, rows, lat, masters, factors, loss_part)
-    else:
+        members = backward(gathered, kept, total_tokens)
+        up_slabs, down_slabs, mats_slabs, thin, grad_bias, lows, grad_cond = members
+        loss_part = jnp.sum(kept.errors * kept.errors)
         grads = plain_grads(
             down_slabs, up_slabs, mats_slabs, thin, grad_bias, lows, grad_cond, labels, rows_here
         )

time: 880 us -> 763 us (0.87)
  matrix products: 55.8 us -> 4.6 us
  local copies, waits for them, and re-layouts: 78.3 us -> 34 us
  other arithmetic: 38.4 us -> 25.8 us
  Pallas kernels: 693 us -> 681 us
    dot_general x5 -> x0, matrix products: 34.4 us -> none  [the longest x1 12.7 us: backward(): jnp.einsum('lhqk,lqhd->lkhd', grad_scores, queries, preferred_element_typ...]
    pallas_call x1, Pallas kernels: 110 us -> 86.3 us  [experts_backward(): pl.pallas_call(backward_kernel, grid_spec=pltpu.PrefetchScalarGridSpec(nu...]
    reshape x7 -> x2, local copies, waits for them, and re-layouts: 20.8 us -> 0.37 us  [backward_fused(): errors = product(head_in, w_head) - noise.reshape(rows_here, PD)]
    dot_general x13 -> x3, matrix products: 17.3 us -> 2.41 us  [contract(): lax.dot_general(left, right, (((left_dim,), (right_dim,)), ((), ())), pre...]
    pallas_call x1, Pallas kernels: 234 us -> 246 us  [reduce_slabs(): pl.pallas_call(reduce_kernel, out_shape=[jax.ShapeDtypeStruct((direct, PI...]
    unnamed x223 -> x84, local copies, waits for them, and re-layouts: 29.6 us -> 18.6 us
where the time goes in v2:
time: 763 us; the launch traced here: 749 us
  Pallas kernels  681 us (89%)
  local copies, waits for them, and re-layouts  34 us (4%)
  other arithmetic  25.8 us (3%)
    pallas_call x1, Pallas kernels, gather_weights(): pl.pallas_call(gather_kernel, out_shape=[jax.ShapeDtypeStruct((2, 2, 4, 2...  254 us
    pallas_call x1, Pallas kernels, reduce_slabs(): pl.pallas_call(reduce_kernel, out_shape=[jax.ShapeDtypeStruct((direct, PI...  246 us
    pallas_call x1, Pallas kernels, experts_backward(): pl.pallas_call(backward_kernel, grid_spec=pltpu.PrefetchScalarGridSpec(nu...  86.3 us
    pallas_call x1, Pallas kernels, update_kernel_call(): pl.pallas_call(update_kernel, out_shape=[jax.ShapeDtypeStruct((1, 1), ful...  53.4 us
    pallas_call x1, Pallas kernels, experts_forward(): pl.pallas_call(forward_kernel, grid_spec=pltpu.PrefetchScalarGridSpec(num...  41.5 us
    unnamed x84, local copies, waits for them, and re-layouts  18.6 us

profile of v2, /device:TPU:0, one launch (start us, length us, event | category | flops | bytes accessed | tf_op | source)
XLA Modules:
  0.0 748.6 jit_solution(3373844807959184667)
XLA Ops:
  0.7 1.1 convert_element_type.125
  2.2 0.7 fusion.15.mats_in
  2.9 1.0 multiply_sine_fusion.1
  3.9 1.0 pad_maximum_fusion.1.places
  6.2 0.8 pad.59.patches
  8.3 0.9 pad.58.up_in
  9.7 0.9 convert_element_type.127.down_in
  11.3 253.6 %gather_weights.1 = (bf16[2,2,4,2,3,16,1664]{6,5,4,3,2,1,0:T(8,128)(2,1)}, bf16[4,2,2,2,16,384]{5,4,3,2,1,0:T(8,128)(2,1)}, bf16[18,4,2,2,2,48,384]{6,5,4,3,2,1,...) custom-call(bf16[4,16,1664]{2,1,0:T(8,128)(2,1)} %fusion.15.mats_in,, ...), custom_call_target="tpu_custom_call" | custom-call | tf_op jit(solution)/shard_map/gather_weights/pallas_call | solution.py:1909
  264.9 1.2 copy.72
  268.1 41.5 %experts_forward.1 = f32[2,1024,384]{2,1,0:T(8,128)} custom-call(s32[2,16]{1,0:T(2,128)} %pad_add_fusion.1.meta, s32[2,1024]{1,0:T(2,128)} %pad_add_fusion.slot_at.slots_ref, s32[2,1024]{1,0:T(2,128)} %pad_add_fusion.slot_at.slots_ref, bf16[1024,384]{1,0:T(8,128)(2,1)} %get-tuple-element.61.x_ref.moe_in, bf16[18,4,384,384]{3,2,1,0:T(8,128)(2,1)} %bitcast.112, ...), custom_call_target="tpu_custom_call" | custom-call | flops 20000000000 | bytes 50000000 | tf_op jit(solution)/shard_map/experts_forward/pallas_call | solution.py:222
  309.6 0.7 slice.89
  310.3 3.5 fusion.59
  314.9 2.7 slice_bitcast_fusion.2
  318.0 1.8 multiply_reduce_fusion.5
  319.8 2.0 fusion.5
  321.9 2.5 multiply_reduce_fusion.2
  325.1 0.7 pad.66.thin_in
  325.8 2.1 fusion.4
  327.9 0.6 select_maximum_fusion.grad_fin
  329.3 0.8 pad.63.grad_logits
  330.2 1.2 fusion.6
  331.4 1.3 pad_maximum_fusion.pair_ref
  332.7 86.3 %experts_backward.1 = (bf16[16,8,4,48,384]{4,3,2,1,0:T(8,128)(2,1)}, bf16[16,8,4,48,384]{4,3,2,1,0:T(8,128)(2,1)}, f32[1024,384]{1,0:T(8,128)}) custom-call(s32[2,16]{1,0:T(2,128)} %pad_add_fusion.1.meta, s32[2,1024]{1,0:T(2,128)} %pad_add_fusion.slot_at.slots_ref, s32[2,1024]{1,0:T(2,128)} %pad_add_fusion.slot_at.slots_ref, ...), custom_call_target="tpu_custom_call" | custom-call | flops 44999999488 | bytes 90000000 | tf_op jit(solution)/shard_map/experts_backward/pallas_call | solution.py:320
  419.0 0.7 convert_reduce_fusion.bias_rows
  420.0 0.7 fusion.48.label_parts
  420.6 246.3 %reduce_slabs.1 = (f32[18,48,384]{2,1,0:T(8,128)}, f32[20,4,12,384]{3,2,1,0:T(8,128)}, bf16[4,2,2,2,16,1536]{5,4,3,2,1,0:T(8,128)(2,1)}, f32[16,384]{1,0:T(8,128)}) custom-call(bf16[16,16,2,48,384]{4,3,2,1,0:T(8,128)(2,1)} %bitcast.116, bf16[16,16,2,48,384]{4,3,2,1,0:T(8,128)(2,1)} %bitcast.115, bf16[18,4,384,384]{3,2,1,0:T(8,128)(2,1)} %bitcast.114, ...), custom_call_target="tpu_custom_call" | custom-call | tf_op jit(solution)/shard_map/reduce_slabs/pallas_call | solution.py:948
  666.9 1.0 copy.80.down_row
  667.9 0.9 copy.79.up_row
  668.8 0.6 reshape.360.mats_col
  669.4 0.7 copy.78
  670.1 53.4 %update.1 = (f32[1,1]{1,0:T(1,128)}, f32[12,6296]{1,0:T(8,128)}, f32[12,6296]{1,0:T(8,128)}, bf16[12,6296]{1,0:T(8,128)(2,1)}, f32[12,10]{1,0:T(8,128)}, /*index...) custom-call(f32[18,48,384]{2,1,0:T(8,128)} %get-tuple-element.78.sum, ...), custom_call_target="tpu_custom_call" | custom-call | tf_op jit(solution)/shard_map/update/pallas_call | solution.py:1410
  723.5 1.6 reduce.5
  725.1 1.8 reduce.6
  726.9 1.7 copy.81
  728.6 1.4 copy.82
  730.5 1.2 reduce.7
  731.7 1.8 copy.98
  733.5 1.8 copy.99
  735.2 0.7 copy.100
  735.9 1.2 copy.101
  737.1 0.9 copy-done.9
  738.0 1.2 copy.102
  739.8 0.9 copy.103
  740.8 0.7 copy.104
  741.5 1.1 copy.105
  742.6 1.1 copy.106
  744.1 0.8 copy.107
  744.9 0.6 copy.108
  (136 shorter events, 12.1 us)
Async XLA Ops:
  0.7 4.3 copy-start.28
  0.7 5.1 copy-start.33
  0.7 5.2 copy-start.21
  0.7 5.2 copy-start.17
  2.0 5.7 copy-start.6
  8.1 1.6 copy-start.7
  8.2 2.4 copy-start.32
  10.6 255.5 %copy-start.20 = (s32[1024,2]{0,1:T(2,128)S(1)}, s32[1024,2]{0,1:T(2,128)}, u32[]{:S(2)}) copy-start(s32[1024,2]{0,1:T(2,128)} %param.20) | copy-start | bytes 24580
  268.1 42.3 %copy-start.1 = (f32[1024,384]{1,0:T(8,128)S(1)}, f32[1024,384]{1,0:T(8,128)}, u32[]{:S(2)}) copy-start(f32[1024,384]{1,0:T(8,128)} %get-tuple-element.64.middle) | copy-start | bytes 4718596
  268.1 42.3 %copy-start.11 = (f32[1024,384]{1,0:T(8,128)S(1)}, f32[1024,384]{1,0:T(8,128)}, u32[]{:S(2)}) copy-start(f32[1024,384]{1,0:T(8,128)} %get-tuple-element.67) | copy-start | bytes 4718596
  313.8 0.7 copy-start.27
  314.9 3.1 copy-start.4
  319.8 2.0 copy-start.3
  321.9 2.6 copy-start.8
  321.9 2.8 copy-start.5
  324.4 1.4 copy-start.2
  327.9 2.3 copy-start
  332.7 86.3 %copy-start.16 = (bf16[4,2,2,2,16,384]{5,4,3,2,1,0:T(8,128)(2,1)S(1)}, bf16[4,2,2,2,16,384]{5,4,3,2,1,0:T(8,128)(2,1)}, u32[]{:S(2)}) copy-start(bf16[4,2,2,2,16,384]{5,4,3,2,1,0:T(8,128)(2,1)} %get-tuple-element.75) | copy-start | bytes 1179652
  420.6 246.3 %copy-start.24 = (f32[18,48]{1,0:T(8,128)S(1)}, f32[18,48]{1,0:T(8,128)}, u32[]{:S(2)}) copy-start(f32[18,48]{1,0:T(8,128)} %param.29) | copy-start | bytes 10372
  420.6 247.3 %copy-start.25 = (f32[18,12]{0,1:T(8,128)S(1)}, f32[18,12]{0,1:T(8,128)}, u32[]{:S(2)}) copy-start(f32[18,12]{0,1:T(8,128)} %param.27) | copy-start | bytes 2596
  420.6 248.2 %copy-start.23 = (f32[6296]{0:T(1024)S(1)}, f32[6296]{0:T(1024)}, u32[]{:S(2)}) copy-start(f32[6296]{0:T(1024)} %param.26) | copy-start | bytes 75556
  420.6 248.8 %copy-start.26 = (f32[10,12]{1,0:T(8,128)S(1)}, f32[10,12]{1,0:T(8,128)}, u32[]{:S(2)}) copy-start(f32[10,12]{1,0:T(8,128)} %param.25) | copy-start | bytes 1444
  723.5 11.7 %copy-start.18 = (bf16[12,6296]{1,0:T(8,128)(2,1)S(1)}, bf16[12,6296]{1,0:T(8,128)(2,1)}, u32[]{:S(2)}) copy-start(bf16[12,6296]{1,0:T(8,128)(2,1)} %get-tuple-element.253) | copy-start | bytes 453316
  723.5 12.4 %copy-start.10 = (f32[18,12,1536]{2,1,0:T(8,128)S(1)}, f32[18,12,1536]{2,1,0:T(8,128)}, u32[]{:S(2)}) copy-start(f32[18,12,1536]{2,1,0:T(8,128)} %get-tuple-element.256) | copy-start | bytes 3981316
  735.9 2.1 copy-start.9
  738.0 1.8 copy-start.14
  739.8 1.0 copy-start.19
  739.8 1.7 copy-start.13
  740.8 1.8 copy-start.12
  742.6 1.5 copy-start.15
  742.6 2.3 copy-start.22
  742.6 2.9 copy-start.31
  742.6 3.5 copy-start.30
  742.6 4.0 copy-start.29

commit v3 on v2

--- a/solution.py
+++ b/solution.py
@@ -1,3 +1,4 @@
+import functools
 import math
 from types import SimpleNamespace
 
@@ -175,29 +176,28 @@
     return ((slots_ref[0:1, :] == place) | (slots_ref[1:2, :] == place)).astype(jnp.bfloat16)
 
 
-def forward_kernel(meta, slot_at, slots_ref, x_ref, up_ref, down_ref, routed_ref, y_ref):
+def routed_blocks(meta, slots_ref, x_ref, up_ref, down_ref, y_ref):
     stack_id = pl.program_id(0)
-    tokens = x_ref.shape[0]
-
-    def expert(rows):
+    start = meta[0, stack_id]
+
+    def block(number, unused):
+        base = pl.multiple_of(start + number * BLK, 8)
+        rows = product(slot_pick(slots_ref, base, BLK), x_ref[...]).astype(jnp.bfloat16)
         total = None
         for cut in range(0, FF, CUT):
             pre_act = product(rows, up_columns(up_ref[0], cut))
             part = product(gelu_only(pre_act).astype(jnp.bfloat16), down_ref[0, cut : cut + CUT])
             total = part if total is None else total + part
-        return total
-
-    start = meta[0, stack_id]
-
-    def block(number, unused):
-        base = pl.multiple_of(start + number * BLK, 8)
-        rows = product(slot_pick(slots_ref, base, BLK), x_ref[...]).astype(jnp.bfloat16)
-        y_ref[pl.ds(base, BLK), :] = expert(rows)
+        y_ref[pl.ds(base, BLK), :] = total
         return unused
 
     lax.fori_loop(0, (meta[1, stack_id] + BLK - 1) // BLK, block, 0)
 
-    @pl.when(stack_id == EXPERTS - 1)
+
+def forward_kernel(meta, slot_at, slots_ref, x_ref, up_ref, down_ref, routed_ref, y_ref):
+    routed_blocks(meta, slots_ref, x_ref, up_ref, down_ref, y_ref)
+
+    @pl.when(pl.program_id(0) == EXPERTS - 1)
     def _():
         def group(number, unused):
             for step in range(8):
@@ -206,7 +206,136 @@
                     routed_ref[k, pl.ds(token, 1), :] = y_ref[pl.ds(slot_at[k, token], 1), :]
             return unused
 
-        lax.fori_loop(0, tokens // 8, group, 0)
+        lax.fori_loop(0, x_ref.shape[0] // 8, group, 0)
+
+
+def head_kernel(
+    token_scale,
+    meta,
+    slot_at,
+    slots_ref,
+    x_ref,
+    up_ref,
+    down_ref,
+    logits_ref,
+    routes_ref,
+    shared_ref,
+    middle_ref,
+    noise_ref,
+    mods_ref,
+    fin_ref,
+    head_ref,
+    pair_out,
+    both_out,
+    state_out,
+    logits_out,
+    thin_out,
+    gate_out,
+    fin_out,
+    loss_out,
+    routed_ref,
+    y_ref,
+):
+    routed_blocks(meta, slots_ref, x_ref, up_ref, down_ref, y_ref)
+    low = jnp.bfloat16
+
+    @pl.when(pl.program_id(0) == EXPERTS - 1)
+    def _():
+        gate_out[...] = jnp.zeros_like(gate_out)
+        fin_out[...] = jnp.zeros_like(fin_out)
+        thin_out[...] = jnp.zeros_like(thin_out)
+        loss_out[...] = jnp.zeros_like(loss_out)
+        lane = lax.broadcasted_iota(jnp.int32, (PATCHES, 128), 1)
+
+        def latent(lat, unused):
+            base = pl.multiple_of(lat * PATCHES, PATCHES)
+            span = pl.ds(base, PATCHES)
+
+            def group(number, unused):
+                for step in range(8):
+                    token = number * 8 + step
+                    for k in range(2):
+                        routed_ref[k, pl.ds(token, 1), :] = y_ref[
+                            pl.ds(slot_at[k, base + token], 1), :
+                        ]
+                return unused
+
+            lax.fori_loop(0, PATCHES // 8, group, 0)
+            hot = [
+                (lane == routes_ref[span, k : k + 1]).astype(jnp.float32) for k in range(2)
+            ]
+            picked = [jnp.sum(hot[k] * logits_ref[span, :], 1, keepdims=True) for k in range(2)]
+            most = jnp.maximum(picked[0], picked[1])
+            powers = [jnp.exp(picked[k] - most) for k in range(2)]
+            gates = [powers[k] / (powers[0] + powers[1]) for k in range(2)]
+            moe_out = gates[0] * routed_ref[0] + gates[1] * routed_ref[1] + shared_ref[span, :]
+            gate_moe = mods_ref[pl.ds(lat, 1), 5 * D :]
+            normed, inv_std = layer_norm(middle_ref[span, :] + gate_moe * moe_out)
+            scale = 1.0 + fin_ref[pl.ds(lat, 1), D:]
+            head_in = (normed * scale + fin_ref[pl.ds(lat, 1), :D]).astype(low)
+            errors = product(head_in, head_ref[...]) - noise_ref[span, :]
+            loss_out[...] += jnp.sum(jnp.sum(errors * errors, 1, keepdims=True), 0, keepdims=True)
+            errors = (errors * token_scale).astype(low)
+            grads = contract(errors, head_ref[...], 1, 1)
+            fin_out[pl.ds(lat, 1), :D] = jnp.sum(grads, 0, keepdims=True)
+            fin_out[pl.ds(lat, 1), D:] = jnp.sum(grads * normed, 0, keepdims=True)
+            state = norm_back(grads * scale, normed, inv_std)
+            state_out[span, :] = state
+            gate_out[pl.ds(lat, 1), :] = jnp.sum(moe_out * state, 0, keepdims=True)
+            grads = gate_moe * state
+            both_out[span, :] = grads.astype(low)
+            slopes = []
+            for k in range(2):
+                slopes.append(jnp.sum(routed_ref[k] * grads, 1, keepdims=True))
+                pair_out[k, span, :] = (gates[k] * grads).astype(low)
+            usual = gates[0] * slopes[0] + gates[1] * slopes[1]
+            grad_logits = (
+                hot[0] * (gates[0] * (slopes[0] - usual)) + hot[1] * (gates[1] * (slopes[1] - usual))
+            )
+            logits_out[span, :] = grad_logits
+            thin_out[...] += contract(x_ref[span, :], grad_logits.astype(low), 0, 0) + pltpu.roll(
+                contract(head_in, errors, 0, 0), EXPERTS, 1
+            )
+            return unused
+
+        lax.fori_loop(0, x_ref.shape[0] // PATCHES, latent, 0)
+
+
+def experts_and_head(slot_of, meta, moe_in, up_full, down_full, token_scale, members):
+    tokens = moe_in.shape[0]
+    full, low = jnp.float32, jnp.bfloat16
+    shapes = (
+        ((2, tokens, D), low),
+        ((tokens, D), low),
+        ((tokens, D), full),
+        ((tokens, 128), full),
+        ((D, 128), full),
+        ((8, D), full),
+        ((8, 2 * D), full),
+        ((1, 1), full),
+    )
+    return pl.pallas_call(
+        functools.partial(head_kernel, token_scale),
+        grid_spec=pltpu.PrefetchScalarGridSpec(
+            num_scalar_prefetch=2,
+            grid=(EXPERTS,),
+            in_specs=[
+                whole_block((2, tokens)),
+                whole_block((tokens, D)),
+                pl.BlockSpec((1, NARROW_PIECES, D, D), lambda e, *unused: (e, 0, 0, 0)),
+                pl.BlockSpec((1, FF, D), lambda e, *unused: (e, 0, 0)),
+            ]
+            + [whole_block(member.shape) for member in members],
+            out_specs=[whole_block(shape) for shape, kind in shapes],
+            scratch_shapes=[
+                pltpu.VMEM((2, PATCHES, D), full),
+                pltpu.VMEM((slot_room(tokens), D), full),
+            ],
+        ),
+        out_shape=[jax.ShapeDtypeStruct(shape, kind) for shape, kind in shapes],
+        compiler_params=pltpu.CompilerParams(vmem_limit_bytes=VMEM_ROOM),
+        name="experts_and_head",
+    )(meta, slot_of, slot_of, moe_in, up_full, down_full, *members)
 
 
 def slot_room(tokens):
@@ -386,6 +515,7 @@
     out_two,
     keep_two,
     got_two,
+    got_last,
     keep_z,
     out_z,
     got_z,
@@ -474,17 +604,29 @@
             out_one.at[s % 2], got_one.at[s % ring], one_send.at[s % 2], one_recv.at[s % ring], to_one
         )
 
-    def two_copy(s):
-        return remote(out_two.at[s % 2], got_two.at[s], two_send.at[s % 2], two_recv.at[s], to_two)
-
-    def z_copy(s, k):
-        return remote(
-            out_z.at[s % 2, (z + k) % 4],
-            got_z.at[s, k - 1],
-            z_send.at[s % 2, k - 1],
-            z_recv.at[s, k - 1],
-            levels[k - 1],
-        )
+    def two_copy(s, turned=False):
+        if turned:
+            start, end = out_two.at[s % 2, 0], got_last.at[s // 2]
+        else:
+            start, end = out_two.at[s % 2], got_two.at[s // 2]
+        return remote(start, end, two_send.at[s % 2], two_recv.at[s], to_two)
+
+    def z_copy(s, k, turned=False):
+        start, end = out_z.at[s % 2, (z + k) % 4], got_z.at[s, k - 1]
+        if not turned:
+            start, end = start.at[0], end.at[0]
+        return remote(start, end, z_send.at[s % 2, k - 1], z_recv.at[s, k - 1], levels[k - 1])
+
+    def by_order(s, run):
+        turned = s % 2 == 1
+
+        @pl.when(turned)
+        def _():
+            run(True)
+
+        @pl.when(jnp.logical_not(turned))
+        def _():
+            run(False)
 
     def row_copy(r, k):
         mate = mates[k - 1]
@@ -554,7 +696,7 @@
                 place = level * 2 + other
                 base = level * 4 + other * second_step
                 keep_at = base + first_mine * first_step
-                keep_one[s % 2, place] = own[s % 3, keep_at].astype(full) + got_core[
+                keep_one[s % 3, place] = own[s % 3, keep_at].astype(full) + got_core[
                     s % ring, keep_at
                 ].astype(full)
 
@@ -565,41 +707,90 @@
     def stage_one(s):
         one_copy(s).wait_recv()
 
-        @pl.when(s >= 2)
-        def _():
-            two_copy(s).wait_send()
-
-        for level in range(4):
-            send_at = level * 2 + 1 - second_mine
-            out_two[s % 2, level] = (
-                keep_one[s % 2, send_at] + got_one[s % ring, send_at].astype(full)
-            ).astype(low)
-        two_copy(s).start()
-        for level in range(4):
-            keep_at = level * 2 + second_mine
-            keep_two[s % 2, level] = keep_one[s % 2, keep_at] + got_one[s % ring, keep_at].astype(
-                full
-            )
+        def run(turned):
+            @pl.when(s >= 2)
+            def _():
+                sent(s, turned)
+
+            if turned:
+                for level in range(4):
+                    for other in range(2):
+                        out_z[s % 2, level, other] = (
+                            keep_one[s % 3, level * 2 + other]
+                            + got_one[s % ring, level * 2 + other].astype(full)
+                        ).astype(low)
+                for k in range(1, 4):
+                    z_copy(s, k, True).start()
+                for other in range(2):
+                    keep_two[s % 3, other] = keep_one[s % 3, z * 2 + other] + got_one[
+                        s % ring, z * 2 + other
+                    ].astype(full)
+            else:
+                for level in range(4):
+                    send_at = level * 2 + 1 - second_mine
+                    out_two[s % 2, level] = (
+                        keep_one[s % 3, send_at] + got_one[s % ring, send_at].astype(full)
+                    ).astype(low)
+                two_copy(s).start()
+                for level in range(4):
+                    keep_at = level * 2 + second_mine
+                    keep_two[s % 3, level] = keep_one[s % 3, keep_at] + got_one[
+                        s % ring, keep_at
+                    ].astype(full)
+
+        by_order(s, run)
 
         @pl.when(s < slabs - ring)
         def _():
             pl.semaphore_signal(one_free, inc=1, device_id=to_one, device_id_type=MESH_ID)
 
-    def stage_two(s):
-        two_copy(s).wait_recv()
-
-        @pl.when(s >= 2)
-        def _():
+    def sent(s, turned):
+        if turned:
+            for k in range(1, 4):
+                z_copy(s, k, True).wait_send()
+        else:
+            two_copy(s).wait_send()
+
+    def sent_last(s, turned):
+        if turned:
+            two_copy(s, True).wait_send()
+        else:
             for k in range(1, 4):
                 z_copy(s, k).wait_send()
 
-        for level in range(4):
-            out_z[s % 2, level] = (
-                keep_two[s % 2, level] + got_two[s, level].astype(full)
-            ).astype(low)
-        for k in range(1, 4):
-            z_copy(s, k).start()
-        keep_z[s % 2] = keep_two[s % 2, z] + got_two[s, z].astype(full)
+    def stage_two(s):
+        def run(turned):
+            if turned:
+                for k in range(1, 4):
+                    z_copy(s, k, True).wait_recv()
+            else:
+                two_copy(s).wait_recv()
+
+            @pl.when(s >= 2)
+            def _():
+                sent_last(s, turned)
+
+            if turned:
+
+                def gathered(other):
+                    total = keep_two[s % 3, other]
+                    for k in range(3):
+                        total = total + got_z[s, k, other].astype(full)
+                    return total
+
+                out_two[s % 2, 0] = gathered(1 - second_mine).astype(low)
+                two_copy(s, True).start()
+                keep_z[s % 3] = gathered(second_mine)
+            else:
+                for level in range(4):
+                    out_z[s % 2, level, 0] = (
+                        keep_two[s % 3, level] + got_two[s // 2, level].astype(full)
+                    ).astype(low)
+                for k in range(1, 4):
+                    z_copy(s, k).start()
+                keep_z[s % 3] = keep_two[s % 3, z] + got_two[s // 2, z].astype(full)
+
+        by_order(s, run)
 
     def direct_place(s):
         late_at = s - n_down - n_up
@@ -609,11 +800,20 @@
         return jnp.where(s < n_down + n_up, s - n_down, s - n_down - SHARED)
 
     def finish(s):
-        total = keep_z[s % 2]
-        for k in range(1, 4):
-            z_copy(s, k).wait_recv()
-        for k in range(3):
-            total = total + got_z[s, k].astype(full)
+        def run(turned):
+            if turned:
+                two_copy(s, True).wait_recv()
+                keep_z[s % 3] += got_last[s // 2].astype(full)
+            else:
+                for k in range(1, 4):
+                    z_copy(s, k).wait_recv()
+                total = keep_z[s % 3]
+                for k in range(3):
+                    total = total + got_z[s, k, 0].astype(full)
+                keep_z[s % 3] = total
+
+        by_order(s, run)
+        total = keep_z[s % 3]
 
         @pl.when(direct_place(s))
         def _():
@@ -849,7 +1049,7 @@
             first += count
 
         for lag, stage in enumerate((stage_core, stage_one, stage_two, finish, rows_in)):
-            s = t - ahead - lag
+            s = t - ahead - 2 * lag
 
             @pl.when((s >= 0) & (s < slabs))
             def _():
@@ -914,15 +1114,16 @@
 
         return unused
 
-    lax.fori_loop(0, slabs + ahead + 4, tick, 0)
+    lax.fori_loop(0, slabs + ahead + 8, tick, 0)
     for back in range(4):
         core_copy(down_ref.at[0], slabs - 1 - back).wait_send()
     turned = rows_ref.shape[0]
     for back in range(2):
-        one_copy(slabs - 1 - back).wait_send()
-        two_copy(slabs - 1 - back).wait_send()
+        s = slabs - 1 - back
+        one_copy(s).wait_send()
+        sent(s, s % 2 == 1)
+        sent_last(s, s % 2 == 1)
         for k in range(1, 4):
-            z_copy(slabs - 1 - back, k).wait_send()
             row_copy(turned - 1 - back, k).wait_send()
     for k in range(1, 4):
         lat_level(k).wait_send()
@@ -936,7 +1137,7 @@
     routed = down_slabs.shape[0]
     slabs = 2 * routed + n_late
     direct, turned = routed + SHARED, routed + SHARED + 2
-    ring = 6
+    ring = 4
     low, full = jnp.bfloat16, jnp.float32
     sources = [
         member.reshape(routed, WIDE_PIECES * NARROW_PIECES // 2, 2, PIECE, D)
@@ -959,14 +1160,15 @@
             pltpu.VMEM((3, 16, PIECE, D), low),
             pltpu.VMEM((ring, 16, PIECE, D), low),
             pltpu.VMEM((2, 8, PIECE, D), low),
-            pltpu.VMEM((2, 8, PIECE, D), full),
+            pltpu.VMEM((3, 8, PIECE, D), full),
             pltpu.VMEM((ring, 8, PIECE, D), low),
             pltpu.VMEM((2, 4, PIECE, D), low),
-            pltpu.VMEM((2, 4, PIECE, D), full),
-            pltpu.VMEM((slabs, 4, PIECE, D), low),
-            pltpu.VMEM((2, PIECE, D), full),
-            pltpu.VMEM((2, 4, PIECE, D), low),
-            pltpu.VMEM((slabs, 3, PIECE, D), low),
+            pltpu.VMEM((3, 4, PIECE, D), full),
+            pltpu.VMEM(((slabs + 1) // 2, 4, PIECE, D), low),
+            pltpu.VMEM(((slabs + 1) // 2, PIECE, D), low),
+            pltpu.VMEM((3, PIECE, D), full),
+            pltpu.VMEM((2, 4, 2, PIECE, D), low),
+            pltpu.VMEM((slabs, 3, 2, PIECE, D), low),
             pltpu.VMEM((2, NARROW_PIECES, ROWS, D), full),
             pltpu.VMEM((n_late, 16, 2, PIECE, D), low),
             pltpu.VMEM((NARROW_PIECES, D, D), low),
@@ -1028,16 +1230,52 @@
     return (mats_grad, scattered(up_slabs), scattered(down_slabs), bias_grad)
 
 
+def spread(value, place):
+    lane = lax.broadcasted_iota(jnp.int32, (1, 128), 1)
+    return jnp.where(lane == place, value, 0.0)
+
+
+def pick(row, place):
+    lane = lax.broadcasted_iota(jnp.int32, (1, 128), 1)
+    return jnp.sum(jnp.where(lane == place, row, 0.0), 1, keepdims=True)
+
+
+def total(values):
+    return jnp.sum(jnp.sum(values, 1, keepdims=True), 0, keepdims=True)
+
+
+def turn_line(values):
+    count = max(values.shape)
+    same = lax.broadcasted_iota(jnp.int32, (count, count), 0) == lax.broadcasted_iota(
+        jnp.int32, (count, count), 1
+    )
+    across = 1 if values.shape[0] == 1 else 0
+    return jnp.sum(jnp.where(same, values, 0.0), across, keepdims=True)
+
+
+def joined(chunks):
+    return jnp.concatenate([chunks[j] for j in range(NARROW_PIECES)], 1)
+
+
+def by_piece(values, start_last, width_last):
+    bounds = [sum(column_widths()[:k]) for k in range(len(column_widths()) + 1)]
+    last_lane = lax.broadcasted_iota(jnp.int32, (ROWS, width_last), 1) + start_last
+    chosen_value = values[0]
+    for k in range(6, len(column_widths())):
+        chosen_value = jnp.where(last_lane >= bounds[k], values[k - 5], chosen_value)
+    return chosen_value
+
+
+def factored(grad, row, col, mean):
+    return grad * lax.rsqrt(row * col / mean)
+
+
 def update_kernel(
     sums_ref,
     rows_ref,
     lat_ref,
     bias_sum,
     loss_ref,
-    mats_ref,
-    up_ref,
-    down_ref,
-    bias_ref,
     mats_row,
     mats_col,
     up_row,
@@ -1045,26 +1283,17 @@
     down_row,
     down_col,
     bias_state,
-    loss_out,
     mats_grad,
-    mats_new,
-    mats_copy,
     mats_row_new,
     mats_col_new,
-    up_grad,
-    up_new,
-    up_copy,
     up_row_new,
     up_col_new,
-    down_grad,
-    down_new,
-    down_copy,
     down_row_new,
     down_col_new,
     bias_grad,
-    bias_new,
-    bias_copy,
     bias_state_new,
+    line_out,
+    squares_out,
     part,
     got_plane,
     mine,
@@ -1108,17 +1337,6 @@
             copy.start()
         for copy in copies:
             copy.wait()
-
-    lane = lax.broadcasted_iota(jnp.int32, (1, 128), 1)
-
-    def spread(value, place):
-        return jnp.where(lane == place, value, 0.0)
-
-    def pick(row, place):
-        return jnp.sum(jnp.where(lane == place, row, 0.0), 1, keepdims=True)
-
-    def total(values):
-        return jnp.sum(jnp.sum(values, 1, keepdims=True), 0, keepdims=True)
 
     count = lat_ref.shape[0] // 4
     order = lax.broadcasted_iota(jnp.int32, (count, count * 4), 0) * 4
@@ -1199,19 +1417,17 @@
             sq = values * values + eps_fact
         else:
             sq = jnp.where((last_lane >= bounds[k]) & (last_lane < bounds[k + 1]), last_sq, 0.0)
-        new = decay * mats_row[:, k : k + 1] + (1.0 - decay) * (
+        new = decay * turn_line(mats_row[k : k + 1, :]) + (1.0 - decay) * (
             jnp.sum(sq, 1, keepdims=True) / widths[k]
         )
-        mats_row_new[:, k : k + 1] = new
+        mats_row_new[k : k + 1, :] = turn_line(new)
         line = line + spread(jnp.sum(new, 0, keepdims=True), k)
 
     def begin_up(e, line):
-        for j in range(NARROW_PIECES):
-            up_grad[e, :, j * D : (j + 1) * D] = rows_ref[e, j]
-        values = up_grad[e]
+        values = joined(rows_ref[e])
         sq = values * values + eps_fact
-        new = decay * up_row[e] + (1.0 - decay) * (jnp.sum(sq, 1, keepdims=True) / FF)
-        up_row_new[e] = new
+        new = decay * turn_line(up_row[pl.ds(e, 1), :]) + (1.0 - decay) * (jnp.sum(sq, 1, keepdims=True) / FF)
+        up_row_new[pl.ds(e, 1), :] = turn_line(new)
         cols = jnp.sum(sq, 0, keepdims=True)
         for k in range(FF // 128):
             part[pl.ds(24 * k + e, 1), :] = cols[:, 128 * k : 128 * (k + 1)]
@@ -1219,10 +1435,9 @@
 
     def begin_down(e, line):
         values = sums_ref[e]
-        down_grad[e] = values
         sq = values * values + eps_fact
-        new = decay * down_row[e] + (1.0 - decay) * (jnp.sum(sq, 1, keepdims=True) / D)
-        down_row_new[e] = new
+        new = decay * turn_line(down_row[pl.ds(e, 1), :]) + (1.0 - decay) * (jnp.sum(sq, 1, keepdims=True) / D)
+        down_row_new[pl.ds(e, 1), :] = turn_line(new)
         cols = jnp.sum(sq, 0, keepdims=True)
         for k in range(D // 128):
             part[pl.ds(24 * (12 + k) + e, 1), :] = cols[:, 128 * k : 128 * (k + 1)]
@@ -1267,7 +1482,7 @@
         return result[row // 64, (row // 16) % 4, pl.ds(row % 16, 1), :width]
 
     line = sums_row(line_at)
-    loss_out[...] = pick(line, 46)
+    line_out[...] = line
     room = bias_grad.shape[1]
     begin = (wide * NARROW_PIECES + narrow) * room
     parts = []
@@ -1284,25 +1499,21 @@
     squares = jnp.zeros((1, 128), full)
     for k in range(5):
         begin, end = bounds[k], bounds[k + 1]
-        step = mats_grad[:, begin:end] * lax.rsqrt(
-            mats_row_new[:, k : k + 1] * mats_col_new[:, begin:end] / (pick(line, k) / D)
-        )
-        mats_new[:, begin:end] = step
+        step = factored(
+            mats_grad[:, begin:end],
+            turn_line(mats_row_new[k : k + 1, :]),
+            mats_col_new[:, begin:end],
+            pick(line, k) / D,
+        )
         squares = squares + spread(total(step * step), k)
-
-    def by_piece(values):
-        chosen_value = values[0]
-        for k in range(6, len(widths)):
-            chosen_value = jnp.where(last_lane >= bounds[k], values[k - 5], chosen_value)
-        return chosen_value
-
-    row_last = by_piece([mats_row_new[:, k : k + 1] for k in range(5, len(widths))])
-    mean_last = by_piece([pick(line, k) / D for k in range(5, len(widths))])
-    step_last = mats_grad[:, start_last:] * lax.rsqrt(
-        row_last * mats_col_new[:, start_last:] / mean_last
-    )
-    mats_new[:, start_last:] = step_last
-    for k in range(5, len(widths)):
+    last = range(5, len(widths))
+    step_last = factored(
+        mats_grad[:, start_last:],
+        by_piece([turn_line(mats_row_new[k : k + 1, :]) for k in last], start_last, width_last),
+        mats_col_new[:, start_last:],
+        by_piece([pick(line, k) / D for k in last], start_last, width_last),
+    )
+    for k in last:
         inside = (last_lane >= bounds[k]) & (last_lane < bounds[k + 1])
         squares = squares + spread(total(jnp.where(inside, step_last * step_last, 0.0)), k)
 
@@ -1310,16 +1521,16 @@
         cols = jnp.concatenate([sums_row(24 * k + e) for k in range(FF // 128)], 1)
         new = decay * up_col[pl.ds(e, 1), :] + (1.0 - decay) * (cols / D)
         up_col_new[pl.ds(e, 1), :] = new
-        step = up_grad[e] * lax.rsqrt(up_row_new[e] * new / (pick(line, 10 + e) / D))
-        up_new[e] = step
+        row = turn_line(up_row_new[pl.ds(e, 1), :])
+        step = factored(joined(rows_ref[e]), row, new, pick(line, 10 + e) / D)
         return squares + spread(total(step * step), 10 + e)
 
     def step_down(e, squares):
         cols = jnp.concatenate([sums_row(24 * (12 + k) + e) for k in range(D // 128)], 1)
         new = decay * down_col[pl.ds(e, 1), :] + (1.0 - decay) * (cols / FF)
         down_col_new[pl.ds(e, 1), :] = new
-        step = down_grad[e] * lax.rsqrt(down_row_new[e] * new / (pick(line, 28 + e) / FF))
-        down_new[e] = step
+        row = turn_line(down_row_new[pl.ds(e, 1), :])
+        step = factored(sums_ref[e], row, new, pick(line, 28 + e) / FF)
         return squares + spread(total(step * step), 28 + e)
 
     squares = lax.fori_loop(0, EXPERTS + SHARED, step_up, squares)
@@ -1344,7 +1555,52 @@
             for k in range(1, 4)
         ]
     )
-    squares = jnp.sum(squares_level[...], 0)[0:1]
+    squares_out[...] = jnp.sum(squares_level[...], 0)[0:1]
+
+
+def settle_kernel(
+    total_tokens,
+    sums_ref,
+    rows_ref,
+    up_ref,
+    down_ref,
+    mats_ref,
+    bias_ref,
+    mats_grad,
+    mats_row,
+    mats_col,
+    up_row,
+    up_col,
+    down_row,
+    down_col,
+    bias_grad,
+    bias_state,
+    line_ref,
+    squares_ref,
+    loss_out,
+    mats_grad_out,
+    mats_new,
+    mats_copy,
+    mats_row_out,
+    mats_col_out,
+    up_grad,
+    up_new,
+    up_copy,
+    up_row_out,
+    up_col_out,
+    down_grad,
+    down_new,
+    down_copy,
+    down_row_out,
+    down_col_out,
+    bias_grad_out,
+    bias_new,
+    bias_copy,
+    bias_state_out,
+):
+    line, squares = line_ref[...], squares_ref[...]
+    low = jnp.bfloat16
+    group = up_ref.shape[0]
 
     def clipped(place, entries):
         rms = jnp.sqrt(pick(squares, place) / entries)
@@ -1355,63 +1611,89 @@
         new_ref[index] = value
         copy_ref[index] = value.astype(low)
 
-    for k in range(5):
-        index = (slice(None), slice(bounds[k], bounds[k + 1]))
-        settle(
-            mats_new, mats_copy, index, mats_ref[index], mats_new[index], clipped(k, D * widths[k])
-        )
-    limit = by_piece([clipped(k, D * widths[k]) for k in range(5, len(widths))])
-    index = (slice(None), slice(start_last, None))
-    settle(mats_new, mats_copy, index, mats_ref[index], mats_new[index], limit)
-
-    def settle_pair(e, unused):
-        settle(up_new, up_copy, e, up_ref[e], up_new[e], clipped(10 + e, D * FF))
-        settle(down_new, down_copy, e, down_ref[e], down_new[e], clipped(28 + e, D * FF))
-        return unused
-
-    lax.fori_loop(0, EXPERTS + SHARED, settle_pair, 0)
-    index = (slice(None), slice(None))
-    settle(bias_new, bias_copy, index, bias_ref[...], bias_step, clipped(46, 15 * D))
-
-
-def update_kernel_call(sums, rows, lat, bias_sum, masters, factors, loss_part):
+    for i in range(group):
+        e = pl.program_id(0) * group + i
+        grad = joined(rows_ref[i])
+        up_grad[i] = grad
+        step = factored(
+            grad,
+            turn_line(up_row[pl.ds(e, 1), :]),
+            up_col[pl.ds(e, 1), :],
+            pick(line, 10 + e) / D,
+        )
+        settle(up_new, up_copy, i, up_ref[i], step, clipped(10 + e, D * FF))
+        grad = sums_ref[i]
+        down_grad[i] = grad
+        step = factored(
+            grad,
+            turn_line(down_row[pl.ds(e, 1), :]),
+            down_col[pl.ds(e, 1), :],
+            pick(line, 28 + e) / FF,
+        )
+        settle(down_new, down_copy, i, down_ref[i], step, clipped(28 + e, D * FF))
+
+    @pl.when(pl.program_id(0) == 0)
+    def _():
+        widths = column_widths()
+        bounds = [sum(widths[:k]) for k in range(len(widths) + 1)]
+        start_last = bounds[5]
+        width_last = bounds[-1] - start_last
+        loss_out[...] = pick(line, 46) / total_tokens
+        for given, out in (
+            (mats_grad, mats_grad_out),
+            (mats_row, mats_row_out),
+            (mats_col, mats_col_out),
+            (up_row, up_row_out),
+            (up_col, up_col_out),
+            (down_row, down_row_out),
+            (down_col, down_col_out),
+            (bias_grad, bias_grad_out),
+            (bias_state, bias_state_out),
+        ):
+            out[...] = given[...]
+        for k in range(6):
+            if k < 5:
+                index = (slice(None), slice(bounds[k], bounds[k + 1]))
+                row, mean = turn_line(mats_row[k : k + 1, :]), pick(line, k) / D
+                limit = clipped(k, D * widths[k])
+            else:
+                last = range(5, len(widths))
+                index = (slice(None), slice(start_last, None))
+                row, mean, limit = [
+                    by_piece(values, start_last, width_last)
+                    for values in (
+                        [turn_line(mats_row[j : j + 1, :]) for j in last],
+                        [pick(line, j) / D for j in last],
+                        [clipped(j, D * widths[j]) for j in last],
+                    )
+                ]
+            step = factored(mats_grad[index], row, mats_col[index], mean)
+            settle(mats_new, mats_copy, index, mats_ref[index], step, limit)
+        index = (slice(None), slice(None))
+        step = bias_grad[...] * lax.rsqrt(bias_state[...])
+        settle(bias_new, bias_copy, index, bias_ref[...], step, clipped(46, 15 * D))
+
+
+def update_kernel_call(sums, rows, lat, bias_sum, masters, factors, loss_part, total_tokens):
     mats, up_weights, down_weights, biases = masters
     mats_row, mats_col, up_row, up_col, down_row, down_col, bias_state = factors
     full, low = jnp.float32, jnp.bfloat16
-    args = (
-        sums,
-        rows,
-        lat,
-        bias_sum,
-        loss_part.reshape(1, 1),
-        mats,
-        up_weights,
-        down_weights,
-        biases.reshape(1, -1),
-        mats_row.T,
-        mats_col.reshape(1, -1),
-        up_row[:, :, None],
-        up_col,
-        down_row[:, :, None],
-        down_col,
-        bias_state.reshape(1, -1),
-    )
-
-    def like(member, kind):
+    mats_col, bias_state, biases = [
+        member.reshape(1, -1) for member in (mats_col, bias_state, biases)
+    ]
+
+    def like(member, kind=full):
         return jax.ShapeDtypeStruct(member.shape, kind)
 
-    stacks = []
-    for at in (5, 6, 7):
-        stacks.append([like(args[at], full), like(args[at], full), like(args[at], low)])
-        stacks[-1] += [like(args[2 * at - 1], full), like(args[2 * at], full)]
-    lines = [like(args[8], kind) for kind in (full, full, low, full)]
+    row = jax.ShapeDtypeStruct((1, 128), full)
+    rows_like = [mats_row, mats_col, up_row, up_col, down_row, down_col, bias_state, bias_state]
     vmem = pl.BlockSpec(memory_space=pltpu.VMEM)
     dma = pltpu.SemaphoreType.DMA
-    outs = pl.pallas_call(
+    found = pl.pallas_call(
         update_kernel,
-        out_shape=[jax.ShapeDtypeStruct((1, 1), full)] + stacks[0] + stacks[1] + stacks[2] + lines,
-        in_specs=[vmem] * len(args),
-        out_specs=[vmem] * 20,
+        out_shape=[like(member) for member in [mats] + rows_like] + [row, row],
+        in_specs=[vmem] * 12,
+        out_specs=[vmem] * 11,
         scratch_shapes=[
             pltpu.VMEM((512, 128), full),
             pltpu.VMEM((8, 64, 128), full),
@@ -1427,29 +1709,57 @@
             collective_id=1, has_side_effects=True, vmem_limit_bytes=VMEM_ROOM
         ),
         name="update",
-    )(*args)
-    return (
-        outs[0][0, 0],
-        outs[1],
-        outs[2],
-        outs[3],
-        outs[4].T,
-        outs[5].reshape(-1),
-        outs[6],
-        outs[7],
-        outs[8],
-        outs[9][:, :, 0],
-        outs[10],
-        outs[11],
-        outs[12],
-        outs[13],
-        outs[14][:, :, 0],
-        outs[15],
-        outs[16].reshape(-1),
-        outs[17].reshape(-1),
-        outs[18].reshape(-1),
-        outs[19].reshape(-1),
-    )
+    )(
+        sums,
+        rows,
+        lat,
+        bias_sum,
+        loss_part.reshape(1, 1),
+        mats_row,
+        mats_col,
+        up_row,
+        up_col,
+        down_row,
+        down_col,
+        bias_state,
+    )
+    group = 3
+    wholes = [biases] + list(found)
+
+    def whole(member):
+        return pl.BlockSpec(member.shape, lambda g: (0,) * len(member.shape))
+
+    def parts(member):
+        rest = member.shape[1:]
+        return pl.BlockSpec((group,) + rest, lambda g: (g,) + (0,) * len(rest))
+
+    one = jax.ShapeDtypeStruct((1, 1), full)
+    outs = (
+        [(one, whole(one))]
+        + [(like(mats, kind), whole(mats)) for kind in (full, full, low)]
+        + [(like(member), whole(member)) for member in (mats_row, mats_col)]
+        + [(like(up_weights, kind), parts(up_weights)) for kind in (full, full, low)]
+        + [(like(member), whole(member)) for member in (up_row, up_col)]
+        + [(like(down_weights, kind), parts(down_weights)) for kind in (full, full, low)]
+        + [(like(member), whole(member)) for member in (down_row, down_col)]
+        + [(like(biases, kind), whole(biases)) for kind in (full, full, low, full)]
+    )
+    outs = list(
+        pl.pallas_call(
+            functools.partial(settle_kernel, total_tokens),
+            grid=(up_weights.shape[0] // group,),
+            in_specs=[parts(member) for member in (sums, rows, up_weights, down_weights)]
+            + [whole(member) for member in [mats] + wholes],
+            out_shape=[shape for shape, spec in outs],
+            out_specs=[spec for shape, spec in outs],
+            compiler_params=pltpu.CompilerParams(vmem_limit_bytes=VMEM_ROOM),
+            name="finish",
+        )(sums, rows, up_weights, down_weights, mats, *wholes)
+    )
+    outs[0] = outs[0][0, 0]
+    for at in (5, 16, 17, 18, 19):
+        outs[at] = outs[at].reshape(-1)
+    return tuple(outs)
 
 
 def gather_kernel(
@@ -1499,7 +1809,10 @@
     here_sem,
 ):
     n_down, n_up = down_in.shape[0], up_own.shape[0]
-    slabs = 1 + n_down + n_up
+    lead, n_mats = 3, mats_out.shape[4]
+    after_mats = lead + n_mats
+    first_up = n_down + n_mats
+    slabs = first_up + n_up
     wide, narrow = lax.axis_index(WIDE), lax.axis_index(NARROW)
     z, x = wide // 2, wide % 2
     y, c = narrow // 2, narrow % 2
@@ -1572,113 +1885,176 @@
 
     for k in range(1, 4):
         bias_level(k).start()
-    own_mats.wait()
     for k in range(1, 4):
-        near_mats(k).wait_recv()
         near_up(k).start()
-    for n in range(NARROW_PIECES):
-        mats_own[n * ROWS : (n + 1) * ROWS] = mats_got[n].astype(jnp.float32)[:ROWS]
-    mats_got[0, :, :] = mats_own[:16].astype(jnp.bfloat16)
-    mats_got[1, :, :] = mats_own[16:32].astype(jnp.bfloat16)
-    mats_got[2, :, :] = mats_own[32:].astype(jnp.bfloat16)
+
+    def mats_ready():
+        own_mats.wait()
+        for k in range(1, 4):
+            near_mats(k).wait_recv()
+        for n in range(NARROW_PIECES):
+            mats_own[n * ROWS : (n + 1) * ROWS] = mats_got[n].astype(jnp.float32)[:ROWS]
+        for n in range(n_mats):
+            mats_got[n, :, :] = mats_own[16 * n : 16 * (n + 1)].astype(jnp.bfloat16)
+
     own_bias.wait()
 
     def turn(number):
         return (number + EXPERTS) % n_up
 
-    def whole(kind, s):
-        if kind == 0:
-            return mats_out
-        if kind == 1:
-            return down_out.at[turn(s - 1)]
-        return up_out.at[turn(s - 1 - n_down)]
+    def down_at(s):
+        return turn(jnp.where(s < lead, s, s - n_mats))
 
     def source(kind, s):
         if kind == 0:
-            return mats_got.at[pl.ds(0, 3)]
+            return mats_got.at[s - lead]
         if kind == 1:
-            return down_in.at[turn(s - 1)]
-        return up_own.at[turn(s - 1 - n_down)]
-
-    def piece(ref, kind, at):
+            return down_in.at[down_at(s)]
+        return up_own.at[turn(s - first_up)]
+
+    def piece(kind, s, at):
         z_at, x_at, y_at, c_at = at
+        if kind == 0:
+            return mats_out.at[y_at, c_at, z_at, x_at, s - lead]
         if kind == 1:
-            return ref.at[z_at, x_at, y_at, c_at]
-        return ref.at[y_at, c_at, z_at, x_at]
+            return down_out.at[down_at(s), z_at, x_at, y_at, c_at]
+        return up_out.at[turn(s - first_up), y_at, c_at, z_at, x_at]
 
     every = slice(None)
 
     def own_copy(kind, s):
         return pltpu.make_async_copy(
-            source(kind, s), piece(whole(kind, s), kind, (z, x, y, c)), own_sem.at[3 + s % 2]
-        )
-
-    def level_copy(kind, s, k):
+            source(kind, s), piece(kind, s, (z, x, y, c)), own_sem.at[3 + s % 4]
+        )
+
+    def level_copy(kind, s, k, turned=False, first=0):
+        if turned:
+            part = piece(kind, s, (z, x, every, c) if first == 0 else (z, every, y, c))
+            start = part
+        else:
+            part = piece(kind, s, (z, x, y, c))
+            start = source(kind, s)
         return remote(
-            source(kind, s),
-            piece(whole(kind, s), kind, (z, x, y, c)),
-            level_send.at[s % 4, k - 1],
-            level_recv.at[s, k - 1],
-            levels[k - 1],
-        )
-
-    def one_copy(kind, s):
-        part = piece(whole(kind, s), kind, (every, x, y, c))
-        return remote(part, part, one_send.at[s % 4], one_recv.at[s], to_one)
-
-    def two_copy(kind, s, first):
-        at = (every, every, y, c) if first == 0 else (every, x, every, c)
-        part = piece(whole(kind, s), kind, at)
-        return remote(part, part, two_send.at[s % 4], two_recv.at[s], to_two)
+            start, part, level_send.at[s % 8, k - 1], level_recv.at[s, k - 1], levels[k - 1]
+        )
+
+    def both_parts(kind, s, first):
+        return piece(kind, s, (every, x, every, c) if first else (every, every, y, c))
+
+    def one_copy(kind, s, turned=False, first=0):
+        part = both_parts(kind, s, 1 - first) if turned else piece(kind, s, (every, x, y, c))
+        return remote(part, part, one_send.at[s % 8], one_recv.at[s], to_one)
+
+    def two_copy(kind, s, turned=False, first=0):
+        if turned:
+            part, start = piece(kind, s, (z, x, y, c)), source(kind, s)
+        else:
+            part = both_parts(kind, s, first)
+            start = part
+        return remote(start, part, two_send.at[s % 8], two_recv.at[s], to_two)
 
     def core_copy(kind, s):
-        part = piece(whole(kind, s), kind, (every, every, every, c))
-        return remote(part, part, core_send.at[s % 4], core_recv.at[s], to_core)
+        part = piece(kind, s, (every, every, every, c))
+        return remote(part, part, core_send.at[s % 8], core_recv.at[s], to_core)
+
+    def by_order(kind, s, run):
+        if kind == 0:
+            run(False)
+            return
+        turned = (s % 5 == 1) | (s % 5 == 3)
+
+        @pl.when(turned)
+        def _():
+            run(True)
+
+        @pl.when(jnp.logical_not(turned))
+        def _():
+            run(False)
+
+    def by_core(run):
+        for first in range(2):
+
+            @pl.when(c == first)
+            def _():
+                run(first)
 
     def stage_level(kind, s):
         own_copy(kind, s).start()
-        for k in range(1, 4):
-            level_copy(kind, s, k).start()
+
+        def run(turned):
+            if turned:
+                two_copy(kind, s, True).start()
+            else:
+                for k in range(1, 4):
+                    level_copy(kind, s, k).start()
+
+        by_order(kind, s, run)
 
     def stage_one(kind, s):
         own_copy(kind, s).wait()
-        for k in range(1, 4):
-            level_copy(kind, s, k).wait_recv()
-        one_copy(kind, s).start()
+
+        def run(turned):
+            if turned:
+                two_copy(kind, s, True).wait_recv()
+
+                def send(first):
+                    for k in range(1, 4):
+                        level_copy(kind, s, k, True, first).start()
+
+                by_core(send)
+            else:
+                for k in range(1, 4):
+                    level_copy(kind, s, k).wait_recv()
+                one_copy(kind, s).start()
+
+        by_order(kind, s, run)
 
     def stage_two(kind, s):
-        one_copy(kind, s).wait_recv()
-        for first in range(2):
-
-            @pl.when(c == first)
-            def _():
-                two_copy(kind, s, first).start()
+        def run(turned):
+            if turned:
+                for k in range(1, 4):
+                    level_copy(kind, s, k, True).wait_recv()
+                by_core(lambda first: one_copy(kind, s, True, first).start())
+            else:
+                one_copy(kind, s).wait_recv()
+                by_core(lambda first: two_copy(kind, s, False, first).start())
+
+        by_order(kind, s, run)
 
     def stage_core(kind, s):
-        two_copy(kind, s, 0).wait_recv()
+        def run(turned):
+            if turned:
+                one_copy(kind, s, True).wait_recv()
+            else:
+                two_copy(kind, s).wait_recv()
+
+        by_order(kind, s, run)
         core_copy(kind, s).start()
 
     def stage_last(kind, s):
         core_copy(kind, s).wait_recv()
 
     def stage_sent(kind, s):
-        for k in range(1, 4):
-            level_copy(kind, s, k).wait_send()
-        one_copy(kind, s).wait_send()
-        two_copy(kind, s, 0).wait_send()
+        def run(turned):
+            for k in range(1, 4):
+                level_copy(kind, s, k, turned).wait_send()
+            one_copy(kind, s, turned).wait_send()
+            two_copy(kind, s, turned).wait_send()
+
+        by_order(kind, s, run)
         core_copy(kind, s).wait_send()
 
     stages = (
-        (stage_sent, 4),
+        (stage_sent, 8),
         (stage_level, 0),
-        (stage_one, 1),
-        (stage_two, 2),
-        (stage_core, 3),
-        (stage_last, 4),
+        (stage_one, 2),
+        (stage_two, 4),
+        (stage_core, 6),
+        (stage_last, 8),
     )
 
     lats = patches.shape[0] // PATCHES
-    shared_at = 1 + n_down + SHARED + 4
+    ready, shared_at = after_mats + 8, first_up + SHARED + 8
     low, full = jnp.bfloat16, jnp.float32
 
     def matrix(number, begin, end):
@@ -1804,31 +2180,35 @@
                     [up_wide[n, e * ROWS : (e + 1) * ROWS] for n in range(NARROW_PIECES)], 0
                 ).astype(jnp.bfloat16)
 
+        @pl.when(t == 2)
+        def _():
+            mats_ready()
+
         for stage, lag in stages:
             s = t - lag
 
-            @pl.when(s == 0)
+            @pl.when((s >= lead) & (s < after_mats))
             def _():
-                stage(0, 0)
-
-            @pl.when((s >= 1) & (s < 1 + n_down))
+                stage(0, jnp.clip(s, lead, after_mats - 1))
+
+            @pl.when(((s >= 0) & (s < lead)) | ((s >= after_mats) & (s < first_up)))
             def _():
-                stage(1, jnp.clip(s, 1, n_down))
-
-            @pl.when((s >= 1 + n_down) & (s < slabs))
+                stage(1, jnp.clip(s, 0, first_up - 1))
+
+            @pl.when((s >= first_up) & (s < slabs))
             def _():
-                stage(2, jnp.clip(s, 1 + n_down, slabs - 1))
-
-        @pl.when(t == 5)
+                stage(2, jnp.clip(s, first_up, slabs - 1))
+
+        @pl.when(t == ready)
         def _():
             bias_core().wait_recv()
             conditions()
 
         for number, unit in enumerate((attention_in, attention_heads, attention_out)):
 
-            @pl.when((t >= 6) & (t < 6 + 3 * lats) & ((t - 6) % 3 == number))
+            @pl.when((t > ready) & (t <= ready + 3 * lats) & ((t - ready - 1) % 3 == number))
             def _():
-                unit(pl.multiple_of(jnp.clip((t - 6) // 3, 0, lats - 1) * PATCHES, PATCHES))
+                unit(pl.multiple_of(jnp.clip((t - ready - 1) // 3, 0, lats - 1) * PATCHES, PATCHES))
 
         for shared_id in range(SHARED):
             begin = shared_at + shared_id * lats
@@ -1845,7 +2225,7 @@
 
         return unused
 
-    lax.fori_loop(0, slabs + 4, tick, 0)
+    lax.fori_loop(0, slabs + 8, tick, 0)
     for k in range(1, 4):
         near_mats(k).wait_send()
         near_up(k).wait_send()
@@ -1900,7 +2280,7 @@
     )
     room = (n_up * rows + 15) // 16 * 16
     up_in = jnp.pad(up_in, ((0, 0), (0, room - n_up * rows), (0, 0)))
-    slabs = 1 + 2 * n_up
+    slabs = 3 + 2 * n_up
     spread = mats_in.shape[2]
     dma = pltpu.SemaphoreType.DMA
     anywhere = pl.BlockSpec(memory_space=pl.ANY)
@@ -1937,14 +2317,14 @@
             pltpu.VMEM((2, 2, 4, 2, PIECE, D), low),
             dma((2, 4)),
             dma((2, 4)),
-            dma((5,)),
-            dma((4, 3)),
+            dma((7,)),
+            dma((8, 3)),
             dma((slabs, 3)),
-            dma((4,)),
+            dma((8,)),
             dma((slabs,)),
-            dma((4,)),
+            dma((8,)),
             dma((slabs,)),
-            dma((4,)),
+            dma((8,)),
             dma((slabs,)),
             dma((6,)),
             dma((6,)),
@@ -2136,57 +2516,42 @@
 def backward_fused(fused, latents, noise, labels, routes, total_tokens):
     num_latents = latents.shape[0]
     rows_here = num_latents * PATCHES
-    less = ((0, 8 - num_latents), (0, 0))
-    mods, fin = fused.mods[:num_latents], fused.fin[:num_latents]
-    gate_moe = mods[:, None, 5 * D :]
-    shift_fin, scale_fin = fin[:, None, :D], fin[:, None, D:]
-    mats_full = fused.mats_full.reshape(NARROW_PIECES, D, -1)
-    w_head = mats_full[1][:, 4 * D : 4 * D + PD]
     line = jnp.sum(fused.bias_full.reshape(-1, 16, D).astype(jnp.float32), 0)
-    route_hot = (routes[:, :, None] == jnp.arange(EXPERTS, dtype=jnp.int32)[None, None, :]).astype(
-        jnp.float32
-    )
-    logits = fused.logits[:, :EXPERTS]
-    gate_vals = jax.nn.softmax(jnp.sum(route_hot * logits[:, None, :], 2), -1)
     slot_of, slot_meta = pack_slots(routes)
-    routed = experts_forward(slot_of, slot_meta, fused.moe_in, fused.up_full, fused.down_full)
-    moe_out = gate_vals[:, 0:1] * routed[0] + gate_vals[:, 1:2] * routed[1] + fused.shared_out
-    moe_out = moe_out.reshape(num_latents, PATCHES, D)
-    final_state = fused.middle.reshape(num_latents, PATCHES, D) + gate_moe * moe_out
-    normed_fin, inv_fin = layer_norm(final_state)
-    head_in = (
-        (normed_fin * (1.0 + scale_fin) + shift_fin).astype(jnp.bfloat16).reshape(rows_here, D)
-    )
-    errors = product(head_in, w_head) - noise.reshape(rows_here, PD)
-    grad_head, grad_head_in, unused = linear_back(errors * (2.0 / total_tokens), head_in, w_head)
-    grad_head_in = grad_head_in.reshape(num_latents, PATCHES, D)
-    grad_fin = jnp.concatenate(
-        [jnp.sum(grad_head_in, 1), jnp.sum(grad_head_in * normed_fin, 1)], 1
-    )
-    grad_state = norm_back(grad_head_in * (1.0 + scale_fin), normed_fin, inv_fin)
-    grad_gate = jnp.sum(moe_out * grad_state, 1)
-    grad_moe = (gate_moe * grad_state).reshape(rows_here, D)
-    grad_gates = jnp.stack([jnp.sum(routed[k] * grad_moe, 1) for k in range(2)], 1)
-    grad_pair = jnp.stack(
-        [(gate_vals[:, k : k + 1] * grad_moe).astype(jnp.bfloat16) for k in range(2)], 0
+    members = (
+        fused.logits,
+        routes,
+        fused.shared_out,
+        fused.middle,
+        jnp.pad(noise.reshape(rows_here, PD), ((0, 0), (0, 128 - PD))),
+        fused.mods,
+        fused.fin,
+        fused.mats_full[0, 1].reshape(D, -1)[:, 4 * D :],
+    )
+    grad_pair, grad_both, grad_state, grad_logits, thin, grad_gate, grad_fin, loss_part = (
+        experts_and_head(
+            slot_of,
+            slot_meta,
+            fused.moe_in,
+            fused.up_full,
+            fused.down_full,
+            2.0 / total_tokens,
+            members,
+        )
     )
     up_slabs, down_slabs, dx_routed = experts_backward(
         slot_of, slot_meta, fused.moe_in, grad_pair, fused.up_full, fused.down_full
     )
-    grad_picked = gate_vals * (grad_gates - jnp.sum(gate_vals * grad_gates, 1, keepdims=True))
-    grad_logits = jnp.sum(route_hot * grad_picked[:, :, None], 1)
-    grad_router = contract(fused.moe_in, grad_logits.astype(jnp.bfloat16), 0, 0)
-    thin = jnp.pad(jnp.concatenate([grad_router, grad_head], 1), ((0, 0), (0, 128 - 32)))
     label_parts = jnp.stack([labels // 32, labels % 32], 1).astype(jnp.bfloat16)
     members = (
         fused.moe_in,
-        grad_moe.astype(jnp.bfloat16),
+        grad_both,
         dx_routed,
-        jnp.pad(grad_logits, ((0, 0), (0, 128 - EXPERTS))),
+        grad_logits,
         fused.middle,
         fused.qkv,
         fused.attended,
-        grad_state.reshape(rows_here, D),
+        grad_state,
         fused.patches,
         positions(),
         fused.mods,
@@ -2195,12 +2560,12 @@
         fused.pre_time,
         fused.cond,
         fused.freq_low,
-        jnp.pad(grad_gate, less),
-        jnp.pad(grad_fin, less),
+        grad_gate,
+        grad_fin,
         thin,
         jnp.pad(label_parts, ((0, 8 - num_latents), (0, 126))),
     )
-    return jnp.sum(errors * errors), reduce_slabs(
+    return loss_part, reduce_slabs(
         down_slabs, up_slabs, fused.up_full, fused.down_full, members
     )
 
@@ -2498,7 +2863,9 @@
         loss_part, (sums, turned, lat, bias_sum) = backward_fused(
             fused, latents, noise, labels, routes, total_tokens
         )
-        outs = update_kernel_call(sums, turned, lat, bias_sum, masters, factors, loss_part)
+        return update_kernel_call(
+            sums, turned, lat, bias_sum, masters, factors, loss_part, total_tokens
+        )
     else:
         flat = jnp.concatenate([mats.reshape(-1), biases], 0).astype(jnp.bfloat16)
         flat = lax.all_gather(flat, AXES, axis=0, tiled=False)

time: 763 us -> 662 us (0.87); the launches traced: 749 us -> 662 us
  Pallas kernels: 681 us -> 638 us
  local copies, waits for them, and re-layouts: 34 us -> 10.6 us
  other arithmetic: 25.8 us -> 11.8 us
    pallas_call x1, Pallas kernels: 254 us -> 215 us  [gather_weights(): pl.pallas_call(gather_kernel, out_shape=[jax.ShapeDtypeStruct((2, 2, 4, 2...]
    unnamed x84 -> x25, local copies, waits for them, and re-layouts: 18.6 us -> 3.15 us
    pallas_call x1, Pallas kernels: 246 us -> 232 us  [reduce_slabs(): pl.pallas_call(reduce_kernel, out_shape=[jax.ShapeDtypeStruct((direct, PI...]
    pallas_call x2 -> x3, Pallas kernels: 94.9 us -> 104 us  [the longest x1 49.8 us: experts_and_head(): pl.pallas_call(functools.partial(head_kernel, token_scale), grid_spec=plt...]
    reduce_sum x8 -> x0, other arithmetic: 8.51 us -> none  [the longest x1 3.46 us: layer_norm(): centred = source - jnp.mean(source, -1, keepdims=True)]
where the time goes in v3:
time: 662 us
  Pallas kernels  638 us (96%)
  other arithmetic  11.8 us (2%)
  local copies, waits for them, and re-layouts  10.6 us (2%)
    pallas_call x1, Pallas kernels, reduce_slabs(): pl.pallas_call(reduce_kernel, out_shape=[jax.ShapeDtypeStruct((direct, PI...  232 us
    pallas_call x1, Pallas kernels, gather_weights(): pl.pallas_call(gather_kernel, out_shape=[jax.ShapeDtypeStruct((2, 2, 4, 2...  215 us
    pallas_call x1, Pallas kernels, experts_backward(): pl.pallas_call(backward_kernel, grid_spec=pltpu.PrefetchScalarGridSpec(nu...  86.6 us
    pallas_call x1, Pallas kernels, experts_and_head(): pl.pallas_call(functools.partial(head_kernel, token_scale), grid_spec=plt...  49.8 us
    pallas_call x1, Pallas kernels, update_kernel_call(): pl.pallas_call(update_kernel, out_shape=[like(member) for member in [mats...  45.5 us

profile of v3, /device:TPU:0, one launch (start us, length us, event | category | flops | bytes accessed | tf_op | source)
XLA Modules:
  0.0 661.5 jit_solution(14286813616593033245)
XLA Ops:
  0.7 1.1 convert_element_type.99
  1.8 0.1 fusion.44
  1.9 0.1 slice.63
  2.0 0.1 slice.65
  2.1 0.1 concatenate.23
  2.2 0.7 fusion.9.mats_in
  2.9 1.0 multiply_sine_fusion.1
  3.9 1.0 pad_maximum_fusion.places
  4.9 0.3 dynamic_update_slice.3
  5.2 0.6 reshape.163.bias_in
  5.8 0.1 fusion.42
  5.9 0.1 add_convert_fusion
  6.0 0.2 convert_element_type.105
  6.2 0.8 pad.47.patches
  7.0 0.1 fusion.32
  7.1 0.6 fusion.26.freq_low
  7.7 0.1 convert_element_type.102
  7.8 0.3 reshape.164
  8.1 0.1 copy.48
  8.3 0.9 pad.46.up_in
  9.2 0.9 convert_element_type.101.down_in
  10.1 0.1 iota_compare_fusion.10
  10.2 0.6 pad_convert_fusion.label_hot
  10.8 215.4 %gather_weights.1 = (bf16[2,2,4,2,3,16,1664]{6,5,4,3,2,1,0:T(8,128)(2,1)}, bf16[4,2,2,2,16,384]{5,4,3,2,1,0:T(8,128)(2,1)}, bf16[18,4,2,2,2,48,384]{6,5,4,3,2,1,...) custom-call(bf16[4,16,1664]{2,1,0:T(8,128)(2,1)} %fusion.9.mats_in, ...), custom_call_target="tpu_custom_call" | custom-call | tf_op jit(solution)/shard_map/gather_weights/pallas_call | solution.py:2289
  226.2 1.4 slice.54
  227.6 0.6 slice.66.head_ref
  228.3 0.1 convert_reduce_fusion.1
  228.4 0.1 select_reduce_fusion.2
  228.5 0.4 select_reduce_fusion.1
  228.9 0.6 pad_add_fusion.slot_at.slots_ref
  229.5 0.6 pad_add_fusion.1.meta
  230.1 0.2 reshape.168
  230.3 0.8 pad.51.noise_ref
  231.1 1.0 copy.49.routes_ref
  232.2 49.8 %experts_and_head.1 = (bf16[2,1024,384]{2,1,0:T(8,128)(2,1)}, bf16[1024,384]{1,0:T(8,128)(2,1)}, f32[1024,384]{1,0:T(8,128)}, f32[1024,128]{1,0:T(8,128)}, f32[3...) custom-call(s32[2,16]{1,0:T(2,128)} %pad_add_fusion.1.meta, ...), custom_call_target="tpu_custom_call" | custom-call | tf_op jit(solution)/shard_map/experts_and_head/pallas_call | solution.py:317
  282.0 86.6 %experts_backward.1 = (bf16[16,8,4,48,384]{4,3,2,1,0:T(8,128)(2,1)}, bf16[16,8,4,48,384]{4,3,2,1,0:T(8,128)(2,1)}, f32[1024,384]{1,0:T(8,128)}) custom-call(s32[2,16]{1,0:T(2,128)} %pad_add_fusion.1.meta, s32[2,1024]{1,0:T(2,128)} %pad_add_fusion.slot_at.slots_ref, s32[2,1024]{1,0:T(2,128)} %pad_add_fusion.slot_at.slots_ref, ...), custom_call_target="tpu_custom_call" | custom-call | flops 44999999488 | bytes 90000000 | tf_op jit(solution)/shard_map/experts_backward/pallas_call | solution.py:449
  368.6 0.7 convert_reduce_fusion.bias_rows
  369.2 0.1 copy.50
  369.4 0.1 copy.51
  369.5 0.7 fusion.34.label_parts
  370.1 231.6 %reduce_slabs.1 = (f32[18,48,384]{2,1,0:T(8,128)}, f32[20,4,12,384]{3,2,1,0:T(8,128)}, bf16[4,2,2,2,16,1536]{5,4,3,2,1,0:T(8,128)(2,1)}, f32[16,384]{1,0:T(8,128)}) custom-call(bf16[16,16,2,48,384]{4,3,2,1,0:T(8,128)(2,1)} %bitcast.40, bf16[16,16,2,48,384]{4,3,2,1,0:T(8,128)(2,1)} %bitcast.39, bf16[18,4,384,384]{3,2,1,0:T(8,128)(2,1)} %bitcast.38, ...), custom_call_target="tpu_custom_call" | custom-call | tf_op jit(solution)/shard_map/reduce_slabs/pallas_call | solution.py:1149
  601.7 0.6 reshape.173.mats_col
  602.4 0.7 copy.52.up_row
  603.1 45.5 %update.1 = (f32[12,6296]{1,0:T(8,128)}, f32[10,12]{1,0:T(8,128)}, f32[1,6296]{1,0:T(1,128)}, f32[18,12]{1,0:T(8,128)}, f32[18,1536]{1,0:T(8,128)}, /*index=5*/f...) custom-call(f32[18,48,384]{2,1,0:T(8,128)} %get-tuple-element.104.su, ...), custom_call_target="tpu_custom_call" | custom-call | tf_op jit(solution)/shard_map/update/pallas_call | solution.py:1692
  648.5 9.0 %finish.1 = (f32[1,1]{1,0:T(1,128)}, f32[12,6296]{1,0:T(8,128)}, f32[12,6296]{1,0:T(8,128)}, bf16[12,6296]{1,0:T(8,128)(2,1)}, f32[10,12]{1,0:T(8,128)}, /*index...) custom-call(f32[18,48,384]{2,1,0:T(8,128)} %get-tuple-element.104.su, ...), custom_call_target="tpu_custom_call" | custom-call | tf_op jit(solution)/shard_map/finish/pallas_call | solution.py:1748
  657.5 1.4 reduce.1
  658.9 1.4 copy.53
  660.3 1.2 reduce.2
  (38 shorter events, 0.2 us)
Async XLA Ops:
  0.7 4.3 copy-start.8
  0.7 5.1 copy-start.10
  0.7 5.2 copy-start.4
  0.7 5.2 copy-start.3
  1.9 5.8 copy-start
  7.8 1.4 copy-start.1
  8.2 1.8 copy-start.9
  226.2 2.1 copy-start.5
  282.0 86.6 %copy-start.2 = (bf16[4,2,2,2,16,384]{5,4,3,2,1,0:T(8,128)(2,1)S(1)}, bf16[4,2,2,2,16,384]{5,4,3,2,1,0:T(8,128)(2,1)}, u32[]{:S(2)}) copy-start(bf16[4,2,2,2,16,384]{5,4,3,2,1,0:T(8,128)(2,1)} %get-tuple-element.98) | copy-start | bytes 1179652
  370.1 231.6 %copy-start.6 = (f32[6296]{0:T(1024)S(1)}, f32[6296]{0:T(1024)}, u32[]{:S(2)}) copy-start(f32[6296]{0:T(1024)} %param.26) | copy-start | bytes 75556
  370.1 232.3 %copy-start.7 = (f32[18,12]{0,1:T(8,128)S(1)}, f32[18,12]{0,1:T(8,128)}, u32[]{:S(2)}) copy-start(f32[18,12]{0,1:T(8,128)} %param.27) | copy-start | bytes 2596

commit v4 on v3

--- a/solution.py
+++ b/solution.py
@@ -141,7 +141,7 @@
     before = (place[:, None] < place[None, :]).astype(jnp.bfloat16)
     rank_in = product(either, before)
     counts = jnp.sum(either.astype(jnp.float32), 1).astype(jnp.int32)
-    padded = (counts + 7) // 8 * 8
+    padded = (counts + 15) // 16 * 16
     starts = jnp.sum(jnp.where(ids > ids.T, padded[None, :], 0), 1)
     slots = rank_in.astype(jnp.int32) + starts[:, None]
     slot_of = jnp.stack([jnp.sum(jnp.where(member, slots, 0), 0) for member in named], 0)
@@ -176,26 +176,44 @@
     return ((slots_ref[0:1, :] == place) | (slots_ref[1:2, :] == place)).astype(jnp.bfloat16)
 
 
-def routed_blocks(meta, slots_ref, x_ref, up_ref, down_ref, y_ref):
-    stack_id = pl.program_id(0)
-    start = meta[0, stack_id]
+def over_blocks(meta, run):
+    start, count = meta[0, pl.program_id(0)], meta[1, pl.program_id(0)]
+    blocks = (count + BLK // 2 - 1) // BLK
+    rest = count - blocks * BLK
 
     def block(number, unused):
-        base = pl.multiple_of(start + number * BLK, 8)
-        rows = product(slot_pick(slots_ref, base, BLK), x_ref[...]).astype(jnp.bfloat16)
+        run(pl.multiple_of(start + number * BLK, 16), BLK)
+        return unused
+
+    lax.fori_loop(0, blocks, block, 0)
+
+    @pl.when(rest > BLK // 4)
+    def _():
+        run(pl.multiple_of(start + blocks * BLK, 16), BLK // 2)
+
+    @pl.when((rest > 0) & (rest <= BLK // 4))
+    def _():
+        run(pl.multiple_of(start + blocks * BLK, 16), BLK // 4)
+
+
+def routed_blocks(meta, slots_ref, x_ref, up_ref, down_ref, x_out, y_ref):
+    def run(base, size):
+        rows = product(slot_pick(slots_ref, base, size), x_ref[...]).astype(jnp.bfloat16)
+        x_out[pl.ds(base, size), :] = rows
         total = None
         for cut in range(0, FF, CUT):
             pre_act = product(rows, up_columns(up_ref[0], cut))
             part = product(gelu_only(pre_act).astype(jnp.bfloat16), down_ref[0, cut : cut + CUT])
             total = part if total is None else total + part
-        y_ref[pl.ds(base, BLK), :] = total
-        return unused
-
-    lax.fori_loop(0, (meta[1, stack_id] + BLK - 1) // BLK, block, 0)
-
-
-def forward_kernel(meta, slot_at, slots_ref, x_ref, up_ref, down_ref, routed_ref, y_ref):
-    routed_blocks(meta, slots_ref, x_ref, up_ref, down_ref, y_ref)
+        y_ref[pl.ds(base, size), :] = total
+
+    over_blocks(meta, run)
+
+
+def forward_kernel(
+    meta, slot_at, slots_ref, x_ref, up_ref, down_ref, routed_ref, x_out, y_ref
+):
+    routed_blocks(meta, slots_ref, x_ref, up_ref, down_ref, x_out, y_ref)
 
     @pl.when(pl.program_id(0) == EXPERTS - 1)
     def _():
@@ -233,10 +251,11 @@
     gate_out,
     fin_out,
     loss_out,
+    x_out,
     routed_ref,
     y_ref,
 ):
-    routed_blocks(meta, slots_ref, x_ref, up_ref, down_ref, y_ref)
+    routed_blocks(meta, slots_ref, x_ref, up_ref, down_ref, x_out, y_ref)
     low = jnp.bfloat16
 
     @pl.when(pl.program_id(0) == EXPERTS - 1)
@@ -313,6 +332,7 @@
         ((8, D), full),
         ((8, 2 * D), full),
         ((1, 1), full),
+        ((slot_room(tokens), D), low),
     )
     return pl.pallas_call(
         functools.partial(head_kernel, token_scale),
@@ -339,7 +359,7 @@
 
 
 def slot_room(tokens):
-    return tokens * 2 + EXPERTS * 8 + BLK
+    return tokens * 2 + EXPERTS * 16 + BLK
 
 
 def whole_block(shape):
@@ -359,10 +379,13 @@
                 pl.BlockSpec((1, NARROW_PIECES, D, D), lambda e, *unused: (e, 0, 0, 0)),
                 pl.BlockSpec((1, FF, D), lambda e, *unused: (e, 0, 0)),
             ],
-            out_specs=whole_block((2, tokens, D)),
+            out_specs=[whole_block((2, tokens, D)), whole_block((slot_room(tokens), D))],
             scratch_shapes=[pltpu.VMEM((slot_room(tokens), D), jnp.float32)],
         ),
-        out_shape=jax.ShapeDtypeStruct((2, tokens, D), jnp.float32),
+        out_shape=[
+            jax.ShapeDtypeStruct((2, tokens, D), jnp.float32),
+            jax.ShapeDtypeStruct((slot_room(tokens), D), jnp.bfloat16),
+        ],
         compiler_params=pltpu.CompilerParams(vmem_limit_bytes=VMEM_ROOM),
         cost_estimate=pl.CostEstimate(
             flops=20_000_000_000, bytes_accessed=50_000_000, transcendentals=0
@@ -387,7 +410,7 @@
     dx_slots,
 ):
     stack_id = pl.program_id(0)
-    tokens = x_ref.shape[0]
+    tokens = pair_ref.shape[1]
     up_sum[...] = jnp.zeros_like(up_sum)
     down_sum[...] = jnp.zeros_like(down_sum)
 
@@ -404,22 +427,20 @@
             total = part if total is None else total + part
         return total
 
-    start = meta[0, stack_id]
-    stop = start + meta[1, stack_id]
-
-    def block(number, unused):
-        base = pl.multiple_of(start + number * BLK, 8)
-        rows = product(slot_pick(slots_ref, base, BLK), x_ref[...]).astype(jnp.bfloat16)
-        place = base + lax.broadcasted_iota(jnp.int32, (BLK, tokens), 0)
+    stop = meta[0, stack_id] + meta[1, stack_id]
+
+    def run(base, size):
+        place = base + lax.broadcasted_iota(jnp.int32, (size, tokens), 0)
         place = jnp.where(place < stop, place, -1)
         grads = None
         for k in range(2):
             part = product((slots_ref[k : k + 1, :] == place).astype(jnp.bfloat16), pair_ref[k])
             grads = part if grads is None else grads + part
-        dx_slots[pl.ds(base, BLK), :] = expert(rows, grads.astype(jnp.bfloat16))
-        return unused
-
-    lax.fori_loop(0, (meta[1, stack_id] + BLK - 1) // BLK, block, 0)
+        dx_slots[pl.ds(base, size), :] = expert(
+            x_ref[pl.ds(base, size), :], grads.astype(jnp.bfloat16)
+        )
+
+    over_blocks(meta, run)
     for n in range(NARROW_PIECES):
         up_out[0, :, n] = (
             up_sum[:, n * D : (n + 1) * D]
@@ -442,8 +463,8 @@
         lax.fori_loop(0, tokens // 8, group, 0)
 
 
-def experts_backward(slot_of, meta, moe_in, grad_pair, up_full, down_full):
-    tokens = moe_in.shape[0]
+def experts_backward(slot_of, meta, slot_rows, grad_pair, up_full, down_full):
+    tokens = slot_of.shape[1]
     slabs = (EXPERTS, WIDE_PIECES, NARROW_PIECES, PIECE, D)
     slab_spec = pl.BlockSpec((1,) + slabs[1:], lambda e, *unused: (e, 0, 0, 0, 0))
     return pl.pallas_call(
@@ -453,7 +474,7 @@
             grid=(EXPERTS,),
             in_specs=[
                 whole_block((2, tokens)),
-                whole_block((tokens, D)),
+                whole_block(slot_rows.shape),
                 whole_block((2, tokens, D)),
                 pl.BlockSpec((1, NARROW_PIECES, D, D), lambda e, *unused: (e, 0, 0, 0)),
                 pl.BlockSpec((1, FF, D), lambda e, *unused: (e, 0, 0)),
@@ -475,7 +496,7 @@
             flops=45_000_000_000, bytes_accessed=90_000_000, transcendentals=0
         ),
         name="experts_backward",
-    )(meta, slot_of, slot_of, moe_in, grad_pair, up_full, down_full)
+    )(meta, slot_of, slot_of, slot_rows, grad_pair, up_full, down_full)
 
 
 def reduce_kernel(
@@ -483,26 +504,26 @@
     up_ref,
     up_all,
     down_all,
-    moe_in,
-    grad_both,
-    dx_routed,
-    grad_logits,
-    middle,
-    qkv,
-    attended,
-    grad_state,
-    patches,
-    places,
-    mods,
-    mats_all,
-    bias_rows,
-    pre_time,
-    cond,
-    freq_low,
-    grad_gate,
-    grad_fin,
-    thin_in,
-    label_parts,
+    moe_in_far,
+    grad_both_far,
+    dx_routed_far,
+    grad_logits_far,
+    middle_far,
+    qkv_far,
+    attended_far,
+    grad_state_far,
+    patches_far,
+    places_far,
+    mods_far,
+    mats_all_far,
+    bias_rows_far,
+    pre_time_far,
+    cond_far,
+    freq_low_far,
+    grad_gate_far,
+    grad_fin_far,
+    thin_in_far,
+    label_parts_far,
     out_ref,
     rows_ref,
     lat_ref,
@@ -552,8 +573,58 @@
     here_sem,
     core_free,
     one_free,
+    load_sem,
+    moe_in,
+    grad_both,
+    dx_routed,
+    grad_logits,
+    middle,
+    qkv,
+    attended,
+    grad_state,
+    patches,
+    places,
+    mods,
+    mats_all,
+    bias_rows,
+    pre_time,
+    cond,
+    freq_low,
+    grad_gate,
+    grad_fin,
+    thin_in,
+    label_parts,
 ):
     full, low = jnp.float32, jnp.bfloat16
+    loads = [
+        pltpu.make_async_copy(far, near, load_sem.at[number])
+        for number, (far, near) in enumerate(
+            (
+                (moe_in_far, moe_in),
+                (grad_both_far, grad_both),
+                (dx_routed_far, dx_routed),
+                (grad_logits_far, grad_logits),
+                (middle_far, middle),
+                (qkv_far, qkv),
+                (attended_far, attended),
+                (grad_state_far, grad_state),
+                (patches_far, patches),
+                (places_far, places),
+                (mods_far, mods),
+                (mats_all_far, mats_all),
+                (bias_rows_far, bias_rows),
+                (pre_time_far, pre_time),
+                (cond_far, cond),
+                (freq_low_far, freq_low),
+                (grad_gate_far, grad_gate),
+                (grad_fin_far, grad_fin),
+                (thin_in_far, thin_in),
+                (label_parts_far, label_parts),
+            )
+        )
+    ]
+    for load in loads:
+        load.start()
     n_down, n_up, n_late = down_ref.shape[0], up_ref.shape[0], late.shape[0]
     slabs = n_down + n_up + n_late
     ahead, ring = 2, got_core.shape[0]
@@ -1058,6 +1129,13 @@
         @pl.when(t == 0)
         def _():
             prepare()
+            for load in loads[:3]:
+                load.wait()
+
+        @pl.when(t == first_lat)
+        def _():
+            for load in loads[3:]:
+                load.wait()
 
         for shared_id in range(SHARED):
             start_at = shared_id * lats
@@ -1154,7 +1232,7 @@
             jax.ShapeDtypeStruct((4, 2, 2, 2, LAT_ROWS, LAT_COLS), low),
             jax.ShapeDtypeStruct((16, D), full),
         ],
-        in_specs=[anywhere] * 4 + [vmem] * len(members),
+        in_specs=[anywhere] * (4 + len(members)),
         out_specs=[vmem, vmem, anywhere, vmem],
         scratch_shapes=[
             pltpu.VMEM((3, 16, PIECE, D), low),
@@ -1202,7 +1280,9 @@
             dma((2,)),
             regular,
             regular,
-        ],
+            dma((len(members),)),
+        ]
+        + [pltpu.VMEM(member.shape, member.dtype) for member in members],
         compiler_params=pltpu.CompilerParams(
             collective_id=0, has_side_effects=True, vmem_limit_bytes=REDUCE_ROOM
         ),
@@ -1296,9 +1376,7 @@
     squares_out,
     part,
     got_plane,
-    mine,
     got_level,
-    column,
     result,
     squares_plane,
     squares_level,
@@ -1460,18 +1538,11 @@
     here = part[pl.ds(pl.multiple_of(spot * 64, 64), 64), :]
     for k in range(1, 8):
         here = here + got_plane[k]
-    mine[...] = here.reshape(4, 16, 128)
+    got_level[z] = here.reshape(4, 16, 128)
     exchange(
-        [
-            remote(mine.at[(z + k) % 4], got_level.at[k], 1, k, level_device(k))
-            for k in range(1, 4)
-        ]
-    )
-    column[z] = mine[z] + got_level[1] + got_level[2] + got_level[3]
-    exchange(
-        [remote(column.at[z], column.at[z], 2, k, level_device(k)) for k in range(1, 4)]
-    )
-    result[spot] = column[...]
+        [remote(got_level.at[z], got_level.at[z], 1, k, level_device(k)) for k in range(1, 4)]
+    )
+    result[spot] = got_level[0] + got_level[1] + got_level[2] + got_level[3]
     exchange(
         [remote(result.at[spot], result.at[spot], 3, k, plane_device(k)) for k in range(1, 8)]
     )
@@ -1697,9 +1768,7 @@
         scratch_shapes=[
             pltpu.VMEM((512, 128), full),
             pltpu.VMEM((8, 64, 128), full),
-            pltpu.VMEM((4, 16, 128), full),
-            pltpu.VMEM((4, 16, 128), full),
-            pltpu.VMEM((4, 16, 128), full),
+            pltpu.VMEM((4, 4, 16, 128), full),
             pltpu.VMEM((8, 4, 16, 128), full),
             pltpu.VMEM((8, 8, 128), full),
             pltpu.VMEM((4, 8, 128), full),
@@ -1771,7 +1840,7 @@
     places,
     freq_low,
     label_hot,
-    mats_out,
+    mats_far,
     bias_out,
     down_out,
     up_out,
@@ -1779,12 +1848,12 @@
     fin_out,
     time_out,
     cond_out,
-    qkv_out,
-    att_out,
-    middle_out,
-    moe_out,
-    logits_out,
-    shared_out,
+    qkv_out_far,
+    att_out_far,
+    middle_out_far,
+    moe_out_far,
+    logits_out_far,
+    shared_out_far,
     mats_got,
     mats_own,
     up_got,
@@ -1807,7 +1876,29 @@
     bias_send,
     bias_recv,
     here_sem,
+    mats_sem,
+    mats_out,
+    qkv_out,
+    att_out,
+    middle_out,
+    moe_out,
+    logits_out,
+    shared_out,
 ):
+    leaves = [
+        pltpu.make_async_copy(near, far, mats_sem.at[number])
+        for number, (near, far) in enumerate(
+            (
+                (mats_out, mats_far),
+                (qkv_out, qkv_out_far),
+                (att_out, att_out_far),
+                (middle_out, middle_out_far),
+                (moe_out, moe_out_far),
+                (logits_out, logits_out_far),
+                (shared_out, shared_out_far),
+            )
+        )
+    ]
     n_down, n_up = down_in.shape[0], up_own.shape[0]
     lead, n_mats = 3, mats_out.shape[4]
     after_mats = lead + n_mats
@@ -1935,7 +2026,7 @@
             part = piece(kind, s, (z, x, y, c))
             start = source(kind, s)
         return remote(
-            start, part, level_send.at[s % 8, k - 1], level_recv.at[s, k - 1], levels[k - 1]
+            start, part, level_send.at[s % 12, k - 1], level_recv.at[s, k - 1], levels[k - 1]
         )
 
     def both_parts(kind, s, first):
@@ -1943,7 +2034,7 @@
 
     def one_copy(kind, s, turned=False, first=0):
         part = both_parts(kind, s, 1 - first) if turned else piece(kind, s, (every, x, y, c))
-        return remote(part, part, one_send.at[s % 8], one_recv.at[s], to_one)
+        return remote(part, part, one_send.at[s % 12], one_recv.at[s], to_one)
 
     def two_copy(kind, s, turned=False, first=0):
         if turned:
@@ -1951,11 +2042,11 @@
         else:
             part = both_parts(kind, s, first)
             start = part
-        return remote(start, part, two_send.at[s % 8], two_recv.at[s], to_two)
+        return remote(start, part, two_send.at[s % 12], two_recv.at[s], to_two)
 
     def core_copy(kind, s):
         part = piece(kind, s, (every, every, every, c))
-        return remote(part, part, core_send.at[s % 8], core_recv.at[s], to_core)
+        return remote(part, part, core_send.at[s % 12], core_recv.at[s], to_core)
 
     def by_order(kind, s, run):
         if kind == 0:
@@ -2045,16 +2136,16 @@
         core_copy(kind, s).wait_send()
 
     stages = (
-        (stage_sent, 8),
+        (stage_sent, 12),
         (stage_level, 0),
-        (stage_one, 2),
-        (stage_two, 4),
-        (stage_core, 6),
-        (stage_last, 8),
+        (stage_one, 3),
+        (stage_two, 6),
+        (stage_core, 9),
+        (stage_last, 12),
     )
 
     lats = patches.shape[0] // PATCHES
-    ready, shared_at = after_mats + 8, first_up + SHARED + 8
+    ready, shared_at = after_mats + 12, first_up + SHARED + 12
     low, full = jnp.bfloat16, jnp.float32
 
     def matrix(number, begin, end):
@@ -2210,6 +2301,11 @@
             def _():
                 unit(pl.multiple_of(jnp.clip((t - ready - 1) // 3, 0, lats - 1) * PATCHES, PATCHES))
 
+        @pl.when(t == ready + 3 * lats + 1)
+        def _():
+            for leave in leaves[:-1]:
+                leave.start()
+
         for shared_id in range(SHARED):
             begin = shared_at + shared_id * lats
 
@@ -2223,9 +2319,15 @@
                     shared_id, pl.multiple_of(jnp.clip(t - begin, 0, lats - 1) * PATCHES, PATCHES)
                 )
 
+        @pl.when(t == shared_at + SHARED * lats)
+        def _():
+            leaves[-1].start()
+
         return unused
 
-    lax.fori_loop(0, slabs + 8, tick, 0)
+    lax.fori_loop(0, slabs + 12, tick, 0)
+    for leave in leaves:
+        leave.wait()
     for k in range(1, 4):
         near_mats(k).wait_send()
         near_up(k).wait_send()
@@ -2305,7 +2407,7 @@
             jax.ShapeDtypeStruct((tokens, D), full),
         ],
         in_specs=[anywhere] * 4 + [vmem] * 4,
-        out_specs=[vmem] * 2 + [anywhere] * 2 + [vmem] * 10,
+        out_specs=[anywhere, vmem] + [anywhere] * 2 + [vmem] * 4 + [anywhere] * 6,
         scratch_shapes=[
             pltpu.VMEM((NARROW_PIECES, 16, spread), low),
             pltpu.VMEM((PIECE, spread), jnp.float32),
@@ -2318,17 +2420,25 @@
             dma((2, 4)),
             dma((2, 4)),
             dma((7,)),
-            dma((8, 3)),
+            dma((12, 3)),
             dma((slabs, 3)),
-            dma((8,)),
+            dma((12,)),
             dma((slabs,)),
-            dma((8,)),
+            dma((12,)),
             dma((slabs,)),
-            dma((8,)),
+            dma((12,)),
             dma((slabs,)),
             dma((6,)),
             dma((6,)),
             dma((2,)),
+            dma((7,)),
+            pltpu.VMEM((2, 2, 4, 2, 3, 16, spread), low),
+            pltpu.VMEM((tokens, 3 * D), low),
+            pltpu.VMEM((tokens, D), low),
+            pltpu.VMEM((tokens, D), full),
+            pltpu.VMEM((tokens, D), low),
+            pltpu.VMEM((tokens, 128), full),
+            pltpu.VMEM((tokens, D), full),
         ],
         compiler_params=pltpu.CompilerParams(
             collective_id=2, has_side_effects=True, vmem_limit_bytes=VMEM_ROOM
@@ -2422,7 +2532,7 @@
     )
     gate_vals = jax.nn.softmax(jnp.sum(route_hot * logits[:, None, :], 2), -1)
     slot_of, slot_meta = pack_slots(routes)
-    routed = experts_forward(slot_of, slot_meta, moe_in, up_full, down_full)
+    routed, slot_rows = experts_forward(slot_of, slot_meta, moe_in, up_full, down_full)
     moe_out = gate_vals[:, 0:1] * routed[0] + gate_vals[:, 1:2] * routed[1]
     for shared_id in range(EXPERTS, EXPERTS + SHARED):
         for cut in range(0, FF, CUT):
@@ -2463,6 +2573,7 @@
         gate_vals=gate_vals,
         slot_of=slot_of,
         slot_meta=slot_meta,
+        slot_rows=slot_rows,
         routed=routed,
         moe_out=moe_out,
         normed_fin=normed_fin,
@@ -2528,7 +2639,17 @@
         fused.fin,
         fused.mats_full[0, 1].reshape(D, -1)[:, 4 * D :],
     )
-    grad_pair, grad_both, grad_state, grad_logits, thin, grad_gate, grad_fin, loss_part = (
+    (
+        grad_pair,
+        grad_both,
+        grad_state,
+        grad_logits,
+        thin,
+        grad_gate,
+        grad_fin,
+        loss_part,
+        slot_rows,
+    ) = (
         experts_and_head(
             slot_of,
             slot_meta,
@@ -2540,7 +2661,7 @@
         )
     )
     up_slabs, down_slabs, dx_routed = experts_backward(
-        slot_of, slot_meta, fused.moe_in, grad_pair, fused.up_full, fused.down_full
+        slot_of, slot_meta, slot_rows, grad_pair, fused.up_full, fused.down_full
     )
     label_parts = jnp.stack([labels // 32, labels % 32], 1).astype(jnp.bfloat16)
     members = (
@@ -2596,7 +2717,7 @@
         [(gate_vals[:, k : k + 1] * grad_moe).astype(jnp.bfloat16) for k in range(2)], 0
     )
     up_slabs, down_slabs, grad_moe_in = experts_backward(
-        kept.slot_of, kept.slot_meta, moe_in, grad_pair, up_full, down_full
+        kept.slot_of, kept.slot_meta, kept.slot_rows, grad_pair, up_full, down_full
     )
     up_all = [up_slabs.transpose(0, 1, 3, 2, 4).reshape(-1, D, FF)]
     down_all = [down_slabs.reshape(-1, FF, D)]

time: 662 us -> 635 us (0.959); the launches traced: 662 us -> 626 us
  Pallas kernels: 638 us -> 602 us
    pallas_call x1, Pallas kernels: 86.6 us -> 64.7 us  [experts_backward(): pl.pallas_call(backward_kernel, grid_spec=pltpu.PrefetchScalarGridSpec(nu...]
where the time goes in v4:
time: 635 us; the launch traced here: 626 us
  Pallas kernels  602 us (95%)
  other arithmetic  11.8 us (2%)
  local copies, waits for them, and re-layouts  10.6 us (2%)
    pallas_call x1, Pallas kernels, reduce_slabs(): pl.pallas_call(reduce_kernel, out_shape=[jax.ShapeDtypeStruct((direct, PI...  230 us
    pallas_call x1, Pallas kernels, gather_weights(): pl.pallas_call(gather_kernel, out_shape=[jax.ShapeDtypeStruct((2, 2, 4, 2...  209 us
    pallas_call x1, Pallas kernels, experts_backward(): pl.pallas_call(backward_kernel, grid_spec=pltpu.PrefetchScalarGridSpec(nu...  64.7 us
    pallas_call x1, Pallas kernels, experts_and_head(): pl.pallas_call(functools.partial(head_kernel, token_scale), grid_spec=plt...  46.6 us
    pallas_call x1, Pallas kernels, update_kernel_call(): pl.pallas_call(update_kernel, out_shape=[like(member) for member in [mats...  42.9 us

profile of v4, /device:TPU:0, one launch (start us, length us, event | category | flops | bytes accessed | tf_op | source)
XLA Modules:
  0.0 626.2 jit_solution(14631990575093340728)
XLA Ops:
  0.7 1.1 convert_element_type.99
  1.8 0.1 fusion.44
  1.9 0.1 slice.63
  2.0 0.1 slice.65
  2.1 0.1 concatenate.23
  2.2 0.7 fusion.9.mats_in
  2.9 1.0 multiply_sine_fusion.1
  3.9 1.0 pad_maximum_fusion.places.places_far
  4.9 0.3 dynamic_update_slice.3
  5.2 0.6 reshape.163.bias_in
  5.8 0.1 fusion.42
  5.9 0.1 add_convert_fusion
  6.0 0.2 convert_element_type.105
  6.2 0.8 pad.47.patches.patches_far
  7.0 0.1 fusion.32
  7.1 0.6 fusion.26.freq_low.freq_low_far
  7.7 0.1 convert_element_type.102
  7.8 0.3 reshape.164
  8.1 0.1 copy.48
  8.3 0.9 pad.46.up_in
  9.2 0.9 convert_element_type.101.down_in
  10.1 0.1 iota_compare_fusion.10
  10.2 0.6 pad_convert_fusion.label_hot
  10.8 209.2 %gather_weights.1 = (bf16[2,2,4,2,3,16,1664]{6,5,4,3,2,1,0:T(8,128)(2,1)}, bf16[4,2,2,2,16,384]{5,4,3,2,1,0:T(8,128)(2,1)}, bf16[18,4,2,2,2,48,384]{6,5,4,3,2,1,...) custom-call(bf16[4,16,1664]{2,1,0:T(8,128)(2,1)} %fusion.9.mats_in, ...), custom_call_target="tpu_custom_call" | custom-call | tf_op jit(solution)/shard_map/gather_weights/pallas_call | solution.py:2391
  220.0 1.4 slice.54
  221.4 0.6 slice.66.head_ref
  222.1 0.1 convert_reduce_fusion.1
  222.2 0.1 select_reduce_fusion.2
  222.3 0.4 select_reduce_fusion.1
  222.7 0.6 pad_add_fusion.slot_at.slots_ref
  223.3 0.6 pad_add_fusion.1.meta
  223.9 0.2 reshape.168
  224.1 0.8 pad.51.noise_ref
  224.9 1.0 copy.49.routes_ref
  225.9 46.6 %experts_and_head.1 = (bf16[2,1024,384]{2,1,0:T(8,128)(2,1)}, bf16[1024,384]{1,0:T(8,128)(2,1)}, f32[1024,384]{1,0:T(8,128)}, f32[1024,128]{1,0:T(8,128)}, f32[3...) custom-call(s32[2,16]{1,0:T(2,128)} %pad_add_fusion.1.meta, ...), custom_call_target="tpu_custom_call" | custom-call | tf_op jit(solution)/shard_map/experts_and_head/pallas_call | solution.py:337
  272.5 64.7 %experts_backward.1 = (bf16[16,8,4,48,384]{4,3,2,1,0:T(8,128)(2,1)}, bf16[16,8,4,48,384]{4,3,2,1,0:T(8,128)(2,1)}, f32[1024,384]{1,0:T(8,128)}) custom-call(s32[2,16]{1,0:T(2,128)} %pad_add_fusion.1.meta, s32[2,1024]{1,0:T(2,128)} %pad_add_fusion.slot_at.slots_ref, s32[2,1024]{1,0:T(2,128)} %pad_add_fusion.slot_at.slots_ref, ...), custom_call_target="tpu_custom_call" | custom-call | flops 44999999488 | bytes 90000000 | tf_op jit(solution)/shard_map/experts_backward/pallas_call | solution.py:470
  337.3 0.7 convert_reduce_fusion.bias_rows_far
  338.0 0.1 copy.50
  338.1 0.1 copy.51
  338.2 0.7 fusion.34.label_parts_far
  338.8 229.6 %reduce_slabs.1 = (f32[18,48,384]{2,1,0:T(8,128)}, f32[20,4,12,384]{3,2,1,0:T(8,128)}, bf16[4,2,2,2,16,1536]{5,4,3,2,1,0:T(8,128)(2,1)}, f32[16,384]{1,0:T(8,128)}) custom-call(bf16[16,16,2,48,384]{4,3,2,1,0:T(8,128)(2,1)} %bitcast.40, bf16[16,16,2,48,384]{4,3,2,1,0:T(8,128)(2,1)} %bitcast.39, bf16[18,4,384,384]{3,2,1,0:T(8,128)(2,1)} %bitcast.38, ...), custom_call_target="tpu_custom_call" | custom-call | tf_op jit(solution)/shard_map/reduce_slabs/pallas_call | solution.py:1227
  568.5 0.6 reshape.173.mats_col
  569.1 0.7 copy.52.up_row
  569.8 42.9 %update.1 = (f32[12,6296]{1,0:T(8,128)}, f32[10,12]{1,0:T(8,128)}, f32[1,6296]{1,0:T(1,128)}, f32[18,12]{1,0:T(8,128)}, f32[18,1536]{1,0:T(8,128)}, /*index=5*/f...) custom-call(f32[18,48,384]{2,1,0:T(8,128)} %get-tuple-element.106.su, ...), custom_call_target="tpu_custom_call" | custom-call | tf_op jit(solution)/shard_map/update/pallas_call | solution.py:1763
  612.7 9.0 %finish.1 = (f32[1,1]{1,0:T(1,128)}, f32[12,6296]{1,0:T(8,128)}, f32[12,6296]{1,0:T(8,128)}, bf16[12,6296]{1,0:T(8,128)(2,1)}, f32[10,12]{1,0:T(8,128)}, /*index...) custom-call(f32[18,48,384]{2,1,0:T(8,128)} %get-tuple-element.106.su, ...), custom_call_target="tpu_custom_call" | custom-call | tf_op jit(solution)/shard_map/finish/pallas_call | solution.py:1817
  621.7 1.4 reduce.1
  623.1 1.4 copy.53
  624.5 1.2 reduce.2
  (38 shorter events, 0.2 us)
Async XLA Ops:
  0.7 4.3 copy-start.8
  0.7 5.1 copy-start.10
  0.7 5.2 copy-start.4
  0.7 5.2 copy-start.3
  1.9 5.8 copy-start
  7.8 1.4 copy-start.1
  8.2 1.8 copy-start.9
  220.0 2.1 copy-start.5
  272.5 64.7 %copy-start.2 = (bf16[4,2,2,2,16,384]{5,4,3,2,1,0:T(8,128)(2,1)S(1)}, bf16[4,2,2,2,16,384]{5,4,3,2,1,0:T(8,128)(2,1)}, u32[]{:S(2)}) copy-start(bf16[4,2,2,2,16,384]{5,4,3,2,1,0:T(8,128)(2,1)} %get-tuple-element.100) | copy-start | bytes 1179652
  338.8 229.6 %copy-start.6 = (f32[6296]{0:T(1024)S(1)}, f32[6296]{0:T(1024)}, u32[]{:S(2)}) copy-start(f32[6296]{0:T(1024)} %param.26) | copy-start | bytes 75556
  338.8 230.3 %copy-start.7 = (f32[18,12]{0,1:T(8,128)S(1)}, f32[18,12]{0,1:T(8,128)}, u32[]{:S(2)}) copy-start(f32[18,12]{0,1:T(8,128)} %param.27) | copy-start | bytes 2596

commit v5 on v4

--- a/solution.py
+++ b/solution.py
@@ -44,7 +44,7 @@
 
 SQRT_2_PI = math.sqrt(2.0 / math.pi)
 VMEM_ROOM = 56 * 1024 * 1024
-REDUCE_ROOM = 60 * 1024 * 1024
+REDUCE_ROOM = 61 * 1024 * 1024
 
 
 def column_widths():
@@ -182,22 +182,22 @@
     rest = count - blocks * BLK
 
     def block(number, unused):
-        run(pl.multiple_of(start + number * BLK, 16), BLK)
+        run(pl.multiple_of(start + number * BLK, 16), BLK, number > 0)
         return unused
 
     lax.fori_loop(0, blocks, block, 0)
 
     @pl.when(rest > BLK // 4)
     def _():
-        run(pl.multiple_of(start + blocks * BLK, 16), BLK // 2)
+        run(pl.multiple_of(start + blocks * BLK, 16), BLK // 2, blocks > 0)
 
     @pl.when((rest > 0) & (rest <= BLK // 4))
     def _():
-        run(pl.multiple_of(start + blocks * BLK, 16), BLK // 4)
+        run(pl.multiple_of(start + blocks * BLK, 16), BLK // 4, blocks > 0)
 
 
 def routed_blocks(meta, slots_ref, x_ref, up_ref, down_ref, x_out, y_ref):
-    def run(base, size):
+    def run(base, size, unused):
         rows = product(slot_pick(slots_ref, base, size), x_ref[...]).astype(jnp.bfloat16)
         x_out[pl.ds(base, size), :] = rows
         total = None
@@ -404,32 +404,40 @@
     down_ref,
     up_out,
     down_out,
-    dx_ref,
+    dx_slots,
     up_sum,
     down_sum,
-    dx_slots,
 ):
     stack_id = pl.program_id(0)
     tokens = pair_ref.shape[1]
-    up_sum[...] = jnp.zeros_like(up_sum)
-    down_sum[...] = jnp.zeros_like(down_sum)
-
-    def expert(rows, grads):
+
+    @pl.when(meta[1, stack_id] == 0)
+    def _():
+        up_sum[...] = jnp.zeros_like(up_sum)
+        down_sum[...] = jnp.zeros_like(down_sum)
+
+    def expert(rows, grads, later):
         total = None
         for cut in range(0, FF, CUT):
             up_part = up_columns(up_ref[0], cut)
             activated, slope = gelu_slope(product(rows, up_part))
             grad_act = contract(grads, down_ref[0, cut : cut + CUT], 1, 1)
             grad_pre = (grad_act * slope).astype(jnp.bfloat16)
-            down_sum[cut : cut + CUT, :] += contract(activated.astype(jnp.bfloat16), grads, 0, 0)
-            up_sum[:, cut : cut + CUT] += contract(rows, grad_pre, 0, 0)
+            down_part = contract(activated.astype(jnp.bfloat16), grads, 0, 0)
+            up_grad = contract(rows, grad_pre, 0, 0)
+            down_sum[cut : cut + CUT, :] = down_part + jnp.where(
+                later, down_sum[cut : cut + CUT, :], 0.0
+            )
+            up_sum[:, cut : cut + CUT] = up_grad + jnp.where(
+                later, up_sum[:, cut : cut + CUT], 0.0
+            )
             part = contract(grad_pre, up_part, 1, 1)
             total = part if total is None else total + part
         return total
 
     stop = meta[0, stack_id] + meta[1, stack_id]
 
-    def run(base, size):
+    def run(base, size, later):
         place = base + lax.broadcasted_iota(jnp.int32, (size, tokens), 0)
         place = jnp.where(place < stop, place, -1)
         grads = None
@@ -437,7 +445,7 @@
             part = product((slots_ref[k : k + 1, :] == place).astype(jnp.bfloat16), pair_ref[k])
             grads = part if grads is None else grads + part
         dx_slots[pl.ds(base, size), :] = expert(
-            x_ref[pl.ds(base, size), :], grads.astype(jnp.bfloat16)
+            x_ref[pl.ds(base, size), :], grads.astype(jnp.bfloat16), later
         )
 
     over_blocks(meta, run)
@@ -448,19 +456,6 @@
             .reshape(WIDE_PIECES, PIECE, D)
         )
     down_out[0] = down_sum[...].astype(jnp.bfloat16).reshape(WIDE_PIECES, NARROW_PIECES, PIECE, D)
-
-    @pl.when(stack_id == EXPERTS - 1)
-    def _():
-        def group(number, unused):
-            for step in range(8):
-                token = number * 8 + step
-                dx_ref[pl.ds(token, 1), :] = (
-                    dx_slots[pl.ds(slot_at[0, token], 1), :]
-                    + dx_slots[pl.ds(slot_at[1, token], 1), :]
-                )
-            return unused
-
-        lax.fori_loop(0, tokens // 8, group, 0)
 
 
 def experts_backward(slot_of, meta, slot_rows, grad_pair, up_full, down_full):
@@ -479,17 +474,16 @@
                 pl.BlockSpec((1, NARROW_PIECES, D, D), lambda e, *unused: (e, 0, 0, 0)),
                 pl.BlockSpec((1, FF, D), lambda e, *unused: (e, 0, 0)),
             ],
-            out_specs=[slab_spec, slab_spec, whole_block((tokens, D))],
+            out_specs=[slab_spec, slab_spec, whole_block(slot_rows.shape)],
             scratch_shapes=[
                 pltpu.VMEM((D, FF), jnp.float32),
                 pltpu.VMEM((FF, D), jnp.float32),
-                pltpu.VMEM((slot_room(tokens), D), jnp.float32),
             ],
         ),
         out_shape=[
             jax.ShapeDtypeStruct(slabs, jnp.bfloat16),
             jax.ShapeDtypeStruct(slabs, jnp.bfloat16),
-            jax.ShapeDtypeStruct((tokens, D), jnp.float32),
+            jax.ShapeDtypeStruct(slot_rows.shape, jnp.float32),
         ],
         compiler_params=pltpu.CompilerParams(vmem_limit_bytes=VMEM_ROOM),
         cost_estimate=pl.CostEstimate(
@@ -500,6 +494,7 @@
 
 
 def reduce_kernel(
+    slot_at,
     down_ref,
     up_ref,
     up_all,
@@ -540,6 +535,7 @@
     keep_z,
     out_z,
     got_z,
+    got_pair,
     row_parts,
     late,
     up_here,
@@ -683,9 +679,9 @@
         return remote(start, end, two_send.at[s % 2], two_recv.at[s], to_two)
 
     def z_copy(s, k, turned=False):
-        start, end = out_z.at[s % 2, (z + k) % 4], got_z.at[s, k - 1]
+        start, end = out_z.at[s % 2, (z + k) % 4], got_pair.at[s // 2, k - 1]
         if not turned:
-            start, end = start.at[0], end.at[0]
+            start, end = start.at[0], got_z.at[s // 2, k - 1]
         return remote(start, end, z_send.at[s % 2, k - 1], z_recv.at[s, k - 1], levels[k - 1])
 
     def by_order(s, run):
@@ -846,7 +842,7 @@
                 def gathered(other):
                     total = keep_two[s % 3, other]
                     for k in range(3):
-                        total = total + got_z[s, k, other].astype(full)
+                        total = total + got_pair[s // 2, k, other].astype(full)
                     return total
 
                 out_two[s % 2, 0] = gathered(1 - second_mine).astype(low)
@@ -880,7 +876,7 @@
                     z_copy(s, k).wait_recv()
                 total = keep_z[s % 3]
                 for k in range(3):
-                    total = total + got_z[s, k, 0].astype(full)
+                    total = total + got_z[s // 2, k].astype(full)
                 keep_z[s % 3] = total
 
         by_order(s, run)
@@ -953,7 +949,7 @@
     def shared_block(shared_id, start):
         span = pl.ds(start, PATCHES)
         rows, grads = moe_in[span, :], grad_both[span, :]
-        total = dx_routed[span, :] if shared_id == 0 else dx_sum[span, :]
+        total = jnp.zeros((PATCHES, D), full) if shared_id == 0 else dx_sum[span, :]
         for cut in range(0, FF, CUT):
             up_part = up_columns(up_here, cut)
             activated, slope = gelu_slope(product(rows, up_part))
@@ -972,6 +968,18 @@
                 late[SHARED + shared_id, w * 2 + n // 2, n % 2] = up_sum[
                     w * PIECE : (w + 1) * PIECE, n * D : (n + 1) * D
                 ].astype(low)
+
+    def back_rows(start):
+        def group(number, unused):
+            for step in range(8):
+                token = start + number * 8 + step
+                dx_sum[pl.ds(token, 1), :] += (
+                    dx_routed[pl.ds(slot_at[0, token], 1), :]
+                    + dx_routed[pl.ds(slot_at[1, token], 1), :]
+                )
+            return unused
+
+        lax.fori_loop(0, PATCHES // 8, group, 0)
 
     def back_out(start):
         span = pl.ds(start, PATCHES)
@@ -1101,6 +1109,7 @@
 
     first_lat = SHARED * lats
     units = (
+        back_rows,
         back_out,
         lambda start: back_pair(0, start),
         lambda start: back_pair(1, start),
@@ -1210,7 +1219,7 @@
     lat_core().wait()
 
 
-def reduce_slabs(down_slabs, up_slabs, up_all, down_all, members):
+def reduce_slabs(slot_of, down_slabs, up_slabs, up_all, down_all, members):
     n_late = 2 * SHARED + 2
     routed = down_slabs.shape[0]
     slabs = 2 * routed + n_late
@@ -1232,7 +1241,7 @@
             jax.ShapeDtypeStruct((4, 2, 2, 2, LAT_ROWS, LAT_COLS), low),
             jax.ShapeDtypeStruct((16, D), full),
         ],
-        in_specs=[anywhere] * (4 + len(members)),
+        in_specs=[pl.BlockSpec(memory_space=pltpu.SMEM)] + [anywhere] * (4 + len(members)),
         out_specs=[vmem, vmem, anywhere, vmem],
         scratch_shapes=[
             pltpu.VMEM((3, 16, PIECE, D), low),
@@ -1246,7 +1255,8 @@
             pltpu.VMEM(((slabs + 1) // 2, PIECE, D), low),
             pltpu.VMEM((3, PIECE, D), full),
             pltpu.VMEM((2, 4, 2, PIECE, D), low),
-            pltpu.VMEM((slabs, 3, 2, PIECE, D), low),
+            pltpu.VMEM(((slabs + 1) // 2, 3, PIECE, D), low),
+            pltpu.VMEM((slabs // 2, 3, 2, PIECE, D), low),
             pltpu.VMEM((2, NARROW_PIECES, ROWS, D), full),
             pltpu.VMEM((n_late, 16, 2, PIECE, D), low),
             pltpu.VMEM((NARROW_PIECES, D, D), low),
@@ -1287,7 +1297,7 @@
             collective_id=0, has_side_effects=True, vmem_limit_bytes=REDUCE_ROOM
         ),
         name="reduce_slabs",
-    )(*sources, up_all, down_all, *members)
+    )(slot_of, *sources, up_all, down_all, *members)
     return sums, rows, lats.reshape(-1, LAT_COLS), bias_sum
 
 
@@ -1521,8 +1531,8 @@
             part[pl.ds(24 * (12 + k) + e, 1), :] = cols[:, 128 * k : 128 * (k + 1)]
         return line + spread(jnp.sum(new, 0, keepdims=True), 28 + e)
 
-    line = lax.fori_loop(0, EXPERTS + SHARED, begin_up, line)
-    line = lax.fori_loop(0, EXPERTS + SHARED, begin_down, line)
+    line = lax.fori_loop(0, EXPERTS + SHARED, begin_up, line, unroll=True)
+    line = lax.fori_loop(0, EXPERTS + SHARED, begin_down, line, unroll=True)
     part[line_at : line_at + 1, :] = line
     for k in range(D // 128):
         part[bias_at + 16 * k : bias_at + 16 * (k + 1), :] = bias_sum[:, 128 * k : 128 * (k + 1)]
@@ -1604,8 +1614,8 @@
         step = factored(sums_ref[e], row, new, pick(line, 28 + e) / FF)
         return squares + spread(total(step * step), 28 + e)
 
-    squares = lax.fori_loop(0, EXPERTS + SHARED, step_up, squares)
-    squares = lax.fori_loop(0, EXPERTS + SHARED, step_down, squares)
+    squares = lax.fori_loop(0, EXPERTS + SHARED, step_up, squares, unroll=True)
+    squares = lax.fori_loop(0, EXPERTS + SHARED, step_down, squares, unroll=True)
     state = decay * bias_state[...] + (1.0 - decay) * (
         bias_grad[...] * bias_grad[...] + eps_fact
     )
@@ -2687,7 +2697,7 @@
         jnp.pad(label_parts, ((0, 8 - num_latents), (0, 126))),
     )
     return loss_part, reduce_slabs(
-        down_slabs, up_slabs, fused.up_full, fused.down_full, members
+        slot_of, down_slabs, up_slabs, fused.up_full, fused.down_full, members
     )
 
 
@@ -2716,9 +2726,14 @@
     grad_pair = jnp.stack(
         [(gate_vals[:, k : k + 1] * grad_moe).astype(jnp.bfloat16) for k in range(2)], 0
     )
-    up_slabs, down_slabs, grad_moe_in = experts_backward(
+    up_slabs, down_slabs, dx_slots = experts_backward(
         kept.slot_of, kept.slot_meta, kept.slot_rows, grad_pair, up_full, down_full
     )
+    place = jnp.arange(dx_slots.shape[0], dtype=jnp.int32)[None, :]
+    used = place < jnp.max(kept.slot_meta[0] + kept.slot_meta[1])
+    dx_slots = jnp.where(used.T, dx_slots, 0.0)
+    slot_hot = [(kept.slot_of[k][:, None] == place).astype(jnp.float32) for k in range(2)]
+    grad_moe_in = jnp.dot(slot_hot[0] + slot_hot[1], dx_slots, precision=lax.Precision.HIGHEST)
     up_all = [up_slabs.transpose(0, 1, 3, 2, 4).reshape(-1, D, FF)]
     down_all = [down_slabs.reshape(-1, FF, D)]
     for shared_id in range(EXPERTS, EXPERTS + SHARED):

time: 635 us -> 615 us (0.969)
  Pallas kernels: 602 us -> 582 us
    pallas_call x1, Pallas kernels: 64.7 us -> 54.6 us  [experts_backward(): pl.pallas_call(backward_kernel, grid_spec=pltpu.PrefetchScalarGridSpec(nu...]
    pallas_call x1, Pallas kernels: 42.9 us -> 33.9 us  [update_kernel_call(): pl.pallas_call(update_kernel, out_shape=[like(member) for member in [mats...]
where the time goes in v5:
time: 615 us; the launch traced here: 606 us
  Pallas kernels  582 us (95%)
  other arithmetic  11.8 us (2%)
  local copies, waits for them, and re-layouts  10.6 us (2%)
    pallas_call x1, Pallas kernels, reduce_slabs(): pl.pallas_call(reduce_kernel, out_shape=[jax.ShapeDtypeStruct((direct, PI...  229 us
    pallas_call x1, Pallas kernels, gather_weights(): pl.pallas_call(gather_kernel, out_shape=[jax.ShapeDtypeStruct((2, 2, 4, 2...  209 us
    pallas_call x1, Pallas kernels, experts_backward(): pl.pallas_call(backward_kernel, grid_spec=pltpu.PrefetchScalarGridSpec(nu...  54.6 us
    pallas_call x1, Pallas kernels, experts_and_head(): pl.pallas_call(functools.partial(head_kernel, token_scale), grid_spec=plt...  46.4 us
    pallas_call x1, Pallas kernels, update_kernel_call(): pl.pallas_call(update_kernel, out_shape=[like(member) for member in [mats...  33.9 us

profile of v5, /device:TPU:0, one launch (start us, length us, event | category | flops | bytes accessed | tf_op | source)
XLA Modules:
  0.0 606.0 jit_solution(6008808199241687911)
XLA Ops:
  0.7 1.1 convert_element_type.99
  1.8 0.1 fusion.44
  1.9 0.1 slice.63
  2.0 0.1 slice.65
  2.1 0.1 concatenate.23
  2.2 0.7 fusion.9.mats_in
  2.9 1.0 multiply_sine_fusion.1
  3.9 1.0 pad_maximum_fusion.places.places_far
  4.9 0.3 dynamic_update_slice.3
  5.2 0.6 reshape.163.bias_in
  5.8 0.1 fusion.42
  5.9 0.1 add_convert_fusion
  6.0 0.2 convert_element_type.105
  6.2 0.8 pad.47.patches.patches_far
  7.0 0.1 fusion.32
  7.1 0.6 fusion.26.freq_low.freq_low_far
  7.7 0.1 convert_element_type.102
  7.8 0.3 reshape.164
  8.1 0.1 copy.48
  8.3 0.9 pad.46.up_in
  9.2 0.9 convert_element_type.101.down_in
  10.1 0.1 iota_compare_fusion.10
  10.2 0.6 pad_convert_fusion.label_hot
  10.8 209.2 %gather_weights.1 = (bf16[2,2,4,2,3,16,1664]{6,5,4,3,2,1,0:T(8,128)(2,1)}, bf16[4,2,2,2,16,384]{5,4,3,2,1,0:T(8,128)(2,1)}, bf16[18,4,2,2,2,48,384]{6,5,4,3,2,1,...) custom-call(bf16[4,16,1664]{2,1,0:T(8,128)(2,1)} %fusion.9.mats_in, ...), custom_call_target="tpu_custom_call" | custom-call | tf_op jit(solution)/shard_map/gather_weights/pallas_call | solution.py:2401
  220.0 1.4 slice.54
  221.4 0.6 slice.66.head_ref
  222.0 0.1 convert_reduce_fusion.1
  222.2 0.1 select_reduce_fusion.2
  222.3 0.4 select_reduce_fusion.1
  222.7 0.6 pad_add_fusion.slot_at.slots_ref
  223.3 0.6 pad_add_fusion.1.meta
  223.8 0.2 reshape.168
  224.1 0.8 pad.51.noise_ref
  224.9 1.0 copy.49.routes_ref
  225.9 46.4 %experts_and_head.1 = (bf16[2,1024,384]{2,1,0:T(8,128)(2,1)}, bf16[1024,384]{1,0:T(8,128)(2,1)}, f32[1024,384]{1,0:T(8,128)}, f32[1024,128]{1,0:T(8,128)}, f32[3...) custom-call(s32[2,16]{1,0:T(2,128)} %pad_add_fusion.1.meta, ...), custom_call_target="tpu_custom_call" | custom-call | tf_op jit(solution)/shard_map/experts_and_head/pallas_call | solution.py:337
  272.3 54.6 %experts_backward.1 = (bf16[16,8,4,48,384]{4,3,2,1,0:T(8,128)(2,1)}, bf16[16,8,4,48,384]{4,3,2,1,0:T(8,128)(2,1)}, f32[2560,384]{1,0:T(8,128)}) custom-call(s32[2,16]{1,0:T(2,128)} %pad_add_fusion.1.meta, s32[2,1024]{1,0:T(2,128)} %pad_add_fusion.slot_at.slots_ref, s32[2,1024]{1,0:T(2,128)} %pad_add_fusion.slot_at.slots_ref, ...), custom_call_target="tpu_custom_call" | custom-call | flops 44999999488 | bytes 90000000 | tf_op jit(solution)/shard_map/experts_backward/pallas_call | solution.py:465
  326.9 0.7 convert_reduce_fusion.bias_rows_far
  327.5 0.1 copy.50
  327.7 0.1 copy.51
  327.8 0.7 fusion.34.label_parts_far
  328.4 228.9 %reduce_slabs.1 = (f32[18,48,384]{2,1,0:T(8,128)}, f32[20,4,12,384]{3,2,1,0:T(8,128)}, bf16[4,2,2,2,16,1536]{5,4,3,2,1,0:T(8,128)(2,1)}, f32[16,384]{1,0:T(8,128)}) custom-call(s32[2,1024]{1,0:T(2,128)} %pad_add_fusion.slot_at.slots_ref, bf16[16,16,2,48,384]{4,3,2,1,0:T(8,128)(2,1)} %bitcast.40, bf16[16,16,2,48,384]{4,3,2,1,0:T(8,128)(2,1)} %bitcast.39, ...), custom_call_target="tpu_custom_call" | custom-call | tf_op jit(solution)/shard_map/reduce_slabs/pallas_call | solution.py:1236
  557.4 0.6 reshape.173.mats_col
  558.0 0.7 copy.52.up_row
  558.7 33.9 %update.1 = (f32[12,6296]{1,0:T(8,128)}, f32[10,12]{1,0:T(8,128)}, f32[1,6296]{1,0:T(1,128)}, f32[18,12]{1,0:T(8,128)}, f32[18,1536]{1,0:T(8,128)}, /*index=5*/f...) custom-call(f32[18,48,384]{2,1,0:T(8,128)} %get-tuple-element.106.su, ...), custom_call_target="tpu_custom_call" | custom-call | tf_op jit(solution)/shard_map/update/pallas_call | solution.py:1773
  592.6 9.0 %finish.1 = (f32[1,1]{1,0:T(1,128)}, f32[12,6296]{1,0:T(8,128)}, f32[12,6296]{1,0:T(8,128)}, bf16[12,6296]{1,0:T(8,128)(2,1)}, f32[10,12]{1,0:T(8,128)}, /*index...) custom-call(f32[18,48,384]{2,1,0:T(8,128)} %get-tuple-element.106.su, ...), custom_call_target="tpu_custom_call" | custom-call | tf_op jit(solution)/shard_map/finish/pallas_call | solution.py:1827
  601.5 1.4 reduce.1
  603.0 1.4 copy.53
  604.3 1.2 reduce.2
  (38 shorter events, 0.2 us)
Async XLA Ops:
  0.7 4.3 copy-start.8
  0.7 5.1 copy-start.10
  0.7 5.2 copy-start.4
  0.7 5.2 copy-start.3
  1.9 5.8 copy-start
  7.8 1.4 copy-start.1
  8.2 1.8 copy-start.9
  220.0 2.1 copy-start.5
  272.3 54.6 %copy-start.2 = (bf16[4,2,2,2,16,384]{5,4,3,2,1,0:T(8,128)(2,1)S(1)}, bf16[4,2,2,2,16,384]{5,4,3,2,1,0:T(8,128)(2,1)}, u32[]{:S(2)}) copy-start(bf16[4,2,2,2,16,384]{5,4,3,2,1,0:T(8,128)(2,1)} %get-tuple-element.100) | copy-start | bytes 1179652
  328.4 228.9 %copy-start.6 = (f32[6296]{0:T(1024)S(1)}, f32[6296]{0:T(1024)}, u32[]{:S(2)}) copy-start(f32[6296]{0:T(1024)} %param.26) | copy-start | bytes 75556
  328.4 229.6 %copy-start.7 = (f32[18,12]{0,1:T(8,128)S(1)}, f32[18,12]{0,1:T(8,128)}, u32[]{:S(2)}) copy-start(f32[18,12]{0,1:T(8,128)} %param.27) | copy-start | bytes 2596

commit v6 on v5

--- a/solution.py
+++ b/solution.py
@@ -271,15 +271,15 @@
             span = pl.ds(base, PATCHES)
 
             def group(number, unused):
-                for step in range(8):
-                    token = number * 8 + step
+                for step in range(32):
+                    token = number * 32 + step
                     for k in range(2):
                         routed_ref[k, pl.ds(token, 1), :] = y_ref[
                             pl.ds(slot_at[k, base + token], 1), :
                         ]
                 return unused
 
-            lax.fori_loop(0, PATCHES // 8, group, 0)
+            lax.fori_loop(0, PATCHES // 32, group, 0)
             hot = [
                 (lane == routes_ref[span, k : k + 1]).astype(jnp.float32) for k in range(2)
             ]
@@ -896,7 +896,9 @@
                     row_copy(r, k).wait_send()
 
             for n in range(NARROW_PIECES):
-                row_parts[r % 2, n] = total[n * ROWS : (n + 1) * ROWS]
+                row_parts[r % 2, n] = jnp.concatenate(
+                    [total[n * ROWS : (n + 1) * ROWS], jnp.zeros((16 - ROWS, D), full)], 0
+                ).astype(low)
             rows_ref[r, narrow] = row_parts[r % 2, narrow]
             for k in range(1, 4):
                 row_copy(r, k).start()
@@ -1237,7 +1239,7 @@
         reduce_kernel,
         out_shape=[
             jax.ShapeDtypeStruct((direct, PIECE, D), full),
-            jax.ShapeDtypeStruct((turned, NARROW_PIECES, ROWS, D), full),
+            jax.ShapeDtypeStruct((turned, NARROW_PIECES, 16, D), low),
             jax.ShapeDtypeStruct((4, 2, 2, 2, LAT_ROWS, LAT_COLS), low),
             jax.ShapeDtypeStruct((16, D), full),
         ],
@@ -1257,7 +1259,7 @@
             pltpu.VMEM((2, 4, 2, PIECE, D), low),
             pltpu.VMEM(((slabs + 1) // 2, 3, PIECE, D), low),
             pltpu.VMEM((slabs // 2, 3, 2, PIECE, D), low),
-            pltpu.VMEM((2, NARROW_PIECES, ROWS, D), full),
+            pltpu.VMEM((2, NARROW_PIECES, 16, D), low),
             pltpu.VMEM((n_late, 16, 2, PIECE, D), low),
             pltpu.VMEM((NARROW_PIECES, D, D), low),
             pltpu.VMEM((FF, D), low),
@@ -1344,7 +1346,8 @@
 
 
 def joined(chunks):
-    return jnp.concatenate([chunks[j] for j in range(NARROW_PIECES)], 1)
+    chunks = chunks.astype(jnp.float32)
+    return jnp.concatenate([chunks[j][:ROWS] for j in range(NARROW_PIECES)], 1)
 
 
 def by_piece(values, start_last, width_last):
@@ -1445,7 +1448,7 @@
     hid_rows = rows_of(quarters[0][:, D : 2 * D])
     high = quarters[2][:, 2 * D : 3 * D]
     for j in range(NARROW_PIECES):
-        mats_grad[:, j * D : (j + 1) * D] = rows_ref[EXPERTS + SHARED, j]
+        mats_grad[:, j * D : (j + 1) * D] = rows_ref[EXPERTS + SHARED, j].astype(full)[:ROWS]
     mats_grad[:, 4 * D : 6 * D] = product(act_rows, quarters[0][:, 2 * D :])[:ROWS]
     mats_grad[:, 6 * D : 10 * D] = product(act_rows, quarters[1])[:ROWS]
     mats_grad[:, 10 * D : 11 * D] = product(hid_rows, high)[:ROWS]
@@ -1466,9 +1469,7 @@
     start_last = 13 * D
     width_last = mats_grad.shape[1] - start_last
     room = 11 * 128
-    thin = jnp.concatenate(
-        [rows_ref[EXPERTS + SHARED + 1, 0][:, :128], jnp.zeros((4, 128), full)], 0
-    )
+    thin = rows_ref[EXPERTS + SHARED + 1, 0].astype(full)[:, :128]
     thin = jnp.where(
         lax.broadcasted_iota(jnp.int32, (16, 128), 1) < EXPERTS + 2 * PD, thin, 0.0
     )
@@ -1858,6 +1859,7 @@
     fin_out,
     time_out,
     cond_out,
+    head_out,
     qkv_out_far,
     att_out_far,
     middle_out_far,
@@ -2180,6 +2182,7 @@
         act = jax.nn.silu(cond).astype(low)
         time_out[...] = pre_time
         cond_out[...] = cond
+        head_out[...] = matrix(1, 4 * D, 4 * D + 128)
         mods_out[:, : 4 * D] = product(act, matrix(1, 0, 4 * D)) + wide_row(rows, 4, 8)
         mods_out[:, 4 * D :] = product(act, matrix(2, 0, 2 * D)) + wide_row(rows, 8, 10)
         fin_out[...] = product(act, matrix(2, 2 * D, 4 * D)) + wide_row(rows, 13, 15)
@@ -2409,6 +2412,7 @@
             jax.ShapeDtypeStruct((8, 2 * D), full),
             jax.ShapeDtypeStruct((8, D), full),
             jax.ShapeDtypeStruct((8, D), full),
+            jax.ShapeDtypeStruct((D, 128), low),
             jax.ShapeDtypeStruct((tokens, 3 * D), low),
             jax.ShapeDtypeStruct((tokens, D), low),
             jax.ShapeDtypeStruct((tokens, D), full),
@@ -2417,7 +2421,7 @@
             jax.ShapeDtypeStruct((tokens, D), full),
         ],
         in_specs=[anywhere] * 4 + [vmem] * 4,
-        out_specs=[anywhere, vmem] + [anywhere] * 2 + [vmem] * 4 + [anywhere] * 6,
+        out_specs=[anywhere, vmem] + [anywhere] * 2 + [vmem] * 5 + [anywhere] * 6,
         scratch_shapes=[
             pltpu.VMEM((NARROW_PIECES, 16, spread), low),
             pltpu.VMEM((PIECE, spread), jnp.float32),
@@ -2625,12 +2629,13 @@
         fin=outs[5],
         pre_time=outs[6],
         cond=outs[7],
-        qkv=outs[8],
-        attended=outs[9],
-        middle=outs[10],
-        moe_in=outs[11],
-        logits=outs[12],
-        shared_out=outs[13],
+        head=outs[8],
+        qkv=outs[9],
+        attended=outs[10],
+        middle=outs[11],
+        moe_in=outs[12],
+        logits=outs[13],
+        shared_out=outs[14],
     )
 
 
@@ -2647,7 +2652,7 @@
         jnp.pad(noise.reshape(rows_here, PD), ((0, 0), (0, 128 - PD))),
         fused.mods,
         fused.fin,
-        fused.mats_full[0, 1].reshape(D, -1)[:, 4 * D :],
+        fused.head,
     )
     (
         grad_pair,

time: 615 us -> 607 us (0.987)
  no operation moved by 1% of the time
where the time goes in v6:
time: 607 us; the launch traced here: 598 us
  Pallas kernels  576 us (95%)
  other arithmetic  11.8 us (2%)
  local copies, waits for them, and re-layouts  8.54 us (1%)
    pallas_call x1, Pallas kernels, reduce_slabs(): pl.pallas_call(reduce_kernel, out_shape=[jax.ShapeDtypeStruct((direct, PI...  227 us
    pallas_call x1, Pallas kernels, gather_weights(): pl.pallas_call(gather_kernel, out_shape=[jax.ShapeDtypeStruct((2, 2, 4, 2...  209 us
    pallas_call x1, Pallas kernels, experts_backward(): pl.pallas_call(backward_kernel, grid_spec=pltpu.PrefetchScalarGridSpec(nu...  53.6 us
    pallas_call x1, Pallas kernels, experts_and_head(): pl.pallas_call(functools.partial(head_kernel, token_scale), grid_spec=plt...  44.6 us
    pallas_call x1, Pallas kernels, update_kernel_call(): pl.pallas_call(update_kernel, out_shape=[like(member) for member in [mats...  33.4 us

profile of v6, /device:TPU:0, one launch (start us, length us, event | category | flops | bytes accessed | tf_op | source)
XLA Modules:
  0.0 598.3 jit_solution(18121449772010775641)
XLA Ops:
  0.7 1.1 convert_element_type.99
  1.8 0.1 fusion.44
  1.9 0.0 copy-start
  1.9 0.1 slice.55
  2.0 0.1 slice.57
  2.1 0.1 concatenate.23
  2.2 0.7 fusion.9.mats_in
  2.9 1.0 multiply_sine_fusion.1
  3.9 1.0 pad_maximum_fusion.places.places_far
  4.9 0.3 dynamic_update_slice.3
  5.2 0.6 reshape.163.bias_in
  5.8 0.1 fusion.42
  5.9 0.1 add_convert_fusion
  6.0 0.2 convert_element_type.105
  6.2 0.8 pad.47.patches.patches_far
  7.0 0.1 fusion.32
  7.1 0.6 fusion.26.freq_low.freq_low_far
  7.7 0.1 convert_element_type.102
  7.8 0.0 copy-start.1
  7.8 0.3 reshape.164
  8.1 0.1 copy.48
  8.3 0.9 pad.46.up_in
  9.2 0.9 convert_element_type.101.down_in
  10.1 0.1 iota_compare_fusion.10
  10.2 0.6 pad_convert_fusion.label_hot
  10.8 209.2 %gather_weights.1 = (bf16[2,2,4,2,3,16,1664]{6,5,4,3,2,1,0:T(8,128)(2,1)}, bf16[4,2,2,2,16,384]{5,4,3,2,1,0:T(8,128)(2,1)}, bf16[18,4,2,2,2,48,384]{6,5,4,3,2,1,...) custom-call(bf16[4,16,1664]{2,1,0:T(8,128)(2,1)} %fusion.9.mats_in, ...), custom_call_target="tpu_custom_call" | custom-call | tf_op jit(solution)/shard_map/gather_weights/pallas_call | solution.py:2404
  220.0 0.1 convert_reduce_fusion.1
  220.2 0.1 select_reduce_fusion.2
  220.3 0.4 select_reduce_fusion.1
  220.6 0.6 pad_add_fusion.slot_at.slots_ref
  221.3 0.6 pad_add_fusion.1.meta
  221.8 0.2 reshape.168
  222.0 0.8 pad.51.noise_ref
  222.9 1.0 copy.49.routes_ref
  223.9 44.6 %experts_and_head.1 = (bf16[2,1024,384]{2,1,0:T(8,128)(2,1)}, bf16[1024,384]{1,0:T(8,128)(2,1)}, f32[1024,384]{1,0:T(8,128)}, f32[1024,128]{1,0:T(8,128)}, f32[3...) custom-call(s32[2,16]{1,0:T(2,128)} %pad_add_fusion.1.meta, ...), custom_call_target="tpu_custom_call" | custom-call | tf_op jit(solution)/shard_map/experts_and_head/pallas_call | solution.py:337
  268.5 53.6 %experts_backward.1 = (bf16[16,8,4,48,384]{4,3,2,1,0:T(8,128)(2,1)}, bf16[16,8,4,48,384]{4,3,2,1,0:T(8,128)(2,1)}, f32[2560,384]{1,0:T(8,128)}) custom-call(s32[2,16]{1,0:T(2,128)} %pad_add_fusion.1.meta, s32[2,1024]{1,0:T(2,128)} %pad_add_fusion.slot_at.slots_ref, s32[2,1024]{1,0:T(2,128)} %pad_add_fusion.slot_at.slots_ref, ...), custom_call_target="tpu_custom_call" | custom-call | flops 44999999488 | bytes 90000000 | tf_op jit(solution)/shard_map/experts_backward/pallas_call | solution.py:465
  322.1 0.7 convert_reduce_fusion.bias_rows_far
  322.8 0.1 copy.50
  322.9 0.1 copy.51
  323.1 0.7 fusion.34.label_parts_far
  323.7 226.5 %reduce_slabs.1 = (f32[18,48,384]{2,1,0:T(8,128)}, bf16[20,4,16,384]{3,2,1,0:T(8,128)(2,1)}, bf16[4,2,2,2,16,1536]{5,4,3,2,1,0:T(8,128)(2,1)}, f32[16,384]{1,0:T(8,128)}) custom-call(s32[2,1024]{1,0:T(2,128)} %pad_add_fusion.slot_at.slots_ref, bf16[16,16,2,48,384]{4,3,2,1,0:T(8,128)(2,1)} %bitcast.39, bf16[16,16,2,48,384]{4,3,2,1,0:T(8,128)(2,1)} %bitcast.38, ...), custom_call_target="tpu_custom_call" | custom-call | tf_op jit(solution)/shard_map/reduce_slabs/pallas_call | solution.py:1238
  550.3 0.6 reshape.173.mats_col
  550.9 0.7 copy.52.up_row
  551.6 33.4 %update.1 = (f32[12,6296]{1,0:T(8,128)}, f32[10,12]{1,0:T(8,128)}, f32[1,6296]{1,0:T(1,128)}, f32[18,12]{1,0:T(8,128)}, f32[18,1536]{1,0:T(8,128)}, /*index=5*/f...) custom-call(f32[18,48,384]{2,1,0:T(8,128)} %get-tuple-element.108.su, ...), custom_call_target="tpu_custom_call" | custom-call | tf_op jit(solution)/shard_map/update/pallas_call | solution.py:1774
  585.0 8.9 %finish.1 = (f32[1,1]{1,0:T(1,128)}, f32[12,6296]{1,0:T(8,128)}, f32[12,6296]{1,0:T(8,128)}, bf16[12,6296]{1,0:T(8,128)(2,1)}, f32[10,12]{1,0:T(8,128)}, /*index...) custom-call(f32[18,48,384]{2,1,0:T(8,128)} %get-tuple-element.108.su, ...), custom_call_target="tpu_custom_call" | custom-call | tf_op jit(solution)/shard_map/finish/pallas_call | solution.py:1828
  593.9 1.4 reduce.1
  595.3 1.4 copy.53
  596.7 1.2 reduce.2
  (36 shorter events, 0.2 us)
Async XLA Ops:
  0.7 4.3 copy-start.8
  0.7 5.1 copy-start.10
  0.7 5.2 copy-start.4
  0.7 5.2 copy-start.3
  1.9 5.8 copy-start
  7.8 1.4 copy-start.1
  8.2 1.8 copy-start.9
  9.2 210.8 %copy-start.5 = (s32[1024,2]{0,1:T(2,128)S(1)}, s32[1024,2]{0,1:T(2,128)}, u32[]{:S(2)}) copy-start(s32[1024,2]{0,1:T(2,128)} %param.20) | copy-start | bytes 24580
  268.5 53.6 %copy-start.2 = (bf16[4,2,2,2,16,384]{5,4,3,2,1,0:T(8,128)(2,1)S(1)}, bf16[4,2,2,2,16,384]{5,4,3,2,1,0:T(8,128)(2,1)}, u32[]{:S(2)}) copy-start(bf16[4,2,2,2,16,384]{5,4,3,2,1,0:T(8,128)(2,1)} %get-tuple-element.102) | copy-start | bytes 1179652
  323.7 226.6 %copy-start.6 = (f32[6296]{0:T(1024)S(1)}, f32[6296]{0:T(1024)}, u32[]{:S(2)}) copy-start(f32[6296]{0:T(1024)} %param.26) | copy-start | bytes 75556
  323.7 227.2 %copy-start.7 = (f32[18,12]{0,1:T(8,128)S(1)}, f32[18,12]{0,1:T(8,128)}, u32[]{:S(2)}) copy-start(f32[18,12]{0,1:T(8,128)} %param.27) | copy-start | bytes 2596
